TPU v7x, 32 devices: a whole 2x2x4 slice. The times are simulated.
32 devices in a mesh: items: 4 (over y, x), seq: 8 (over z, core).
Axes of the slice: x: 2, y: 2, z: 4, core: 2. Of those that a mesh axis runs over, the one named last changes fastest.
Arguments:
- tokens: bfloat16 [24, 3072, 256], P('items', 'seq'), may hold values from -6 to 6
- lengths: int32 [24], P('items'), may hold values from 768 to 3072, as said below
- pad_mask: int32 [24, 3072], P('items'), may hold values 0 or 1
- w_qkv: bfloat16 [256, 768], replicated, may hold values from -0.375 to 0.375
- w_out: bfloat16 [256, 256], replicated, may hold values from -2 to 2
- w_up: bfloat16 [256, 1024], replicated, may hold values from -0.375 to 0.375
- w_down: bfloat16 [1024, 256], replicated, may hold values from -0.1875 to 0.1875
- gain_attn: float32 [256], replicated, may hold values from 0.25 to 1.75
- shift_attn: float32 [256], replicated, may hold values from -4 to 4
- gain_ffn: float32 [256], replicated, may hold values from 0.25 to 1.75
- shift_ffn: float32 [256], replicated, may hold values from -4 to 4
- cotangent: bfloat16 [24, 3072, 256], P('items', 'seq'), may hold values from -6 to 6
Outputs:
- output: bfloat16 [24, 3072, 256], P('items', 'seq')
- grad_tokens: float32 [24, 3072, 256], P('items', 'seq')
- grad_qkv: float32 [256, 768], replicated
- grad_out: float32 [256, 256], replicated
- grad_up: float32 [256, 1024], replicated
- grad_down: float32 [1024, 256], replicated
- grad_gain_attn: float32 [256], replicated
- grad_shift_attn: float32 [256], replicated
- grad_gain_ffn: float32 [256], replicated
- grad_shift_ffn: float32 [256], replicated
Inputs may be any that keep to these rules, and one draw needn't show every extreme that they name: `lengths`: in each group of images 6g to 6g+5 one image has the full length 3072.
All inputs are finite; a program needn't handle non-finite values. No bound on the sum of `pad_mask` on one device may be relied on, other than what follows from the above.
Results may differ from a plain program's by a relative error of at most 0.01.
Values may be sent and summed in bfloat16 or wider, within the bound.
A program may use at most 128 MiB of HBM per device.

v0:
```python
import jax
import jax.numpy as jnp
from jax import lax
from jax.sharding import PartitionSpec as P

HEADS = 2
HEAD_DIM = 128
ROW = 96


epsilon = 1e-05
branch_scale = 0.7071067811865476
masked_value = -1e30


def from_behind(block, axis, distance):
    devices = range(lax.axis_size(axis))
    route = [(i - distance, i) for i in devices if i - distance in devices]
    return lax.ppermute(block, axis, route)


def layer_norm(inputs, gain_vec, shift_vec):
    average = jnp.mean(inputs, -1, keepdims=True)
    centred = inputs - average
    spread = jnp.mean(centred * centred, -1, keepdims=True)
    return centred * lax.rsqrt(spread + epsilon) * gain_vec + shift_vec


def smooth_act(inputs):
    return jax.nn.gelu(inputs, approximate=True)


def masked_scores(queries, keys_all, allowed):
    scores = jnp.einsum(
        "rqhd,rkhd->rhqk", queries, keys_all, preferred_element_type=jnp.float32
    ) * HEAD_DIM ** (-0.5)
    return jnp.where(allowed[:, None], scores, masked_value)


def shards(
    tokens,
    lengths,
    pad_mask,
    w_qkv,
    w_out,
    w_up,
    w_down,
    gain_attn,
    shift_attn,
    gain_ffn,
    shift_ffn,
    cotangent,
):
    item_count, block_len, feature_width = tokens.shape
    row_count = block_len // ROW
    batch_rows = item_count * row_count
    token_count = item_count * block_len
    first_pos = lax.axis_index("seq") * block_len
    positions = first_pos + jnp.arange(block_len, dtype=jnp.int32)
    own_mask = lax.dynamic_slice_in_dim(pad_mask, first_pos, block_len, 1)
    token_alive = (positions[None, :] < lengths[:, None]) & (own_mask == 1)
    prev_positions = first_pos - ROW + jnp.arange(ROW, dtype=jnp.int32)
    prev_mask = lax.dynamic_slice_in_dim(pad_mask, jnp.maximum(first_pos - ROW, 0), ROW, 1)
    prev_alive = (
        (prev_positions[None, :] >= 0)
        & (prev_positions[None, :] < lengths[:, None])
        & (prev_mask == 1)
    )
    alive_rows = token_alive.reshape(item_count, row_count, ROW)
    before_rows = jnp.concatenate([prev_alive[:, None], alive_rows[:, :-1]], 1)
    key_alive = jnp.concatenate([before_rows, alive_rows], 2).reshape(batch_rows, 1, 2 * ROW)
    query_pos = jnp.arange(ROW, dtype=jnp.int32)[:, None]
    key_pos = jnp.arange(2 * ROW, dtype=jnp.int32)[None, :] - ROW
    allowed = (key_pos < 0) & key_alive | (key_pos >= 0) & (key_pos <= query_pos) & (
        key_alive | (key_pos == query_pos)
    )
    inputs = tokens.astype(jnp.float32).reshape(token_count, feature_width)
    normed_attn, norm_attn_back = jax.vjp(layer_norm, inputs, gain_attn, shift_attn)
    normed_low = normed_attn.astype(jnp.bfloat16)
    projected = jnp.dot(normed_low, w_qkv, preferred_element_type=jnp.float32).astype(jnp.bfloat16)
    key_value = projected[:, feature_width:].reshape(item_count, row_count, ROW, 2 * feature_width)
    kv_weight = w_qkv[:, feature_width:]
    halo_kv = from_behind(key_value[:, -1], "seq", 1)
    before_kv = jnp.concatenate([halo_kv[:, None], key_value[:, :-1]], 1)
    window_kv = jnp.concatenate([before_kv, key_value], 2).reshape(
        batch_rows, 2 * ROW, 2 * feature_width
    )
    head_shape = (batch_rows, 2 * ROW, HEADS, HEAD_DIM)
    keys_all = window_kv[:, :, :feature_width].reshape(head_shape)
    values_all = window_kv[:, :, feature_width:].reshape(head_shape)
    queries = projected[:, :feature_width].reshape(batch_rows, ROW, HEADS, HEAD_DIM)
    scores = masked_scores(queries, keys_all, allowed)
    row_max = jnp.max(scores, -1, keepdims=True)
    exp_scores = jnp.exp(scores - row_max)
    row_total = jnp.sum(exp_scores, -1, keepdims=True)
    log_total = row_max + jnp.log(row_total)
    probs_low = (exp_scores / row_total).astype(jnp.bfloat16)
    attended = jnp.einsum(
        "rhqk,rkhd->rqhd", probs_low, values_all, preferred_element_type=jnp.float32
    )
    attended_low = attended.reshape(token_count, feature_width).astype(jnp.bfloat16)
    branch_attn = jnp.dot(attended_low, w_out, preferred_element_type=jnp.float32)
    middle = inputs + branch_scale * branch_attn
    normed_ffn, norm_ffn_back = jax.vjp(layer_norm, middle, gain_ffn, shift_ffn)
    normed_ffn_low = normed_ffn.astype(jnp.bfloat16)
    hidden_pre = jnp.dot(normed_ffn_low, w_up, preferred_element_type=jnp.float32)
    hidden, act_back = jax.vjp(smooth_act, hidden_pre)
    hidden_low = hidden.astype(jnp.bfloat16)
    branch_ffn = jnp.dot(hidden_low, w_down, preferred_element_type=jnp.float32)
    alive_flat = token_alive.reshape(token_count, 1).astype(jnp.float32)
    output = (
        (alive_flat * (middle + branch_scale * branch_ffn))
        .astype(jnp.bfloat16)
        .reshape(tokens.shape)
    )
    out_grad = cotangent.astype(jnp.float32).reshape(token_count, feature_width) * alive_flat
    ffn_grad_low = (branch_scale * out_grad).astype(jnp.bfloat16)
    grad_down = jnp.einsum(
        "nf,nd->fd", hidden_low, ffn_grad_low, preferred_element_type=jnp.float32
    )
    hidden_grad = jnp.einsum("nd,fd->nf", ffn_grad_low, w_down, preferred_element_type=jnp.float32)
    pre_grad_low = act_back(hidden_grad)[0].astype(jnp.bfloat16)
    grad_up = jnp.einsum(
        "nd,nf->df", normed_ffn_low, pre_grad_low, preferred_element_type=jnp.float32
    )
    normed_ffn_grad = jnp.einsum(
        "nf,df->nd", pre_grad_low, w_up, preferred_element_type=jnp.float32
    )
    middle_part, grad_gain_ffn, grad_shift_ffn = norm_ffn_back(normed_ffn_grad)
    middle_grad = out_grad + middle_part
    attn_grad_low = (branch_scale * middle_grad).astype(jnp.bfloat16)
    grad_out = jnp.einsum(
        "nd,ne->de", attended_low, attn_grad_low, preferred_element_type=jnp.float32
    )
    attended_grad = jnp.einsum(
        "ne,de->nd", attn_grad_low, w_out, preferred_element_type=jnp.float32
    )
    attended_grad = attended_grad.astype(jnp.bfloat16).reshape(batch_rows, ROW, HEADS, HEAD_DIM)
    scores_again = masked_scores(queries, keys_all, allowed)
    probs = jnp.exp(scores_again - log_total)
    probs_again = probs.astype(jnp.bfloat16)
    value_grad = jnp.einsum(
        "rhqk,rqhd->rkhd", probs_again, attended_grad, preferred_element_type=jnp.float32
    )
    prob_grad = jnp.einsum(
        "rqhd,rkhd->rhqk", attended_grad, values_all, preferred_element_type=jnp.float32
    )
    row_dot = jnp.sum(prob_grad * probs, -1, keepdims=True)
    score_grad = jnp.where(allowed[:, None], probs * (prob_grad - row_dot), 0.0).astype(
        jnp.bfloat16
    )
    query_grad = jnp.einsum(
        "rhqk,rkhd->rqhd", score_grad, keys_all, preferred_element_type=jnp.float32
    ) * HEAD_DIM ** (-0.5)
    key_grad = jnp.einsum(
        "rhqk,rqhd->rkhd", score_grad, queries, preferred_element_type=jnp.float32
    ) * HEAD_DIM ** (-0.5)
    window_grad = jnp.concatenate(
        [
            key_grad.reshape(batch_rows, 2 * ROW, feature_width),
            value_grad.reshape(batch_rows, 2 * ROW, feature_width),
        ],
        -1,
    )
    window_grad = window_grad.reshape(item_count, row_count, 2 * ROW, 2 * feature_width)
    next_low = window_grad[:, :, :ROW].astype(jnp.bfloat16)
    own_low = window_grad[:, :, ROW:].reshape(token_count, 2 * feature_width).astype(jnp.bfloat16)
    returned = from_behind(next_low[:, 0], "seq", -1)
    carried = jnp.concatenate([next_low[:, 1:], returned[:, None]], 1)
    carried = carried.reshape(token_count, 2 * feature_width)
    query_low = query_grad.reshape(token_count, feature_width).astype(jnp.bfloat16)
    direct_grad = jnp.concatenate([query_low, own_low], -1)
    kv_part = jnp.einsum("nd,ne->de", normed_low, carried, preferred_element_type=jnp.float32)
    grad_qkv = jnp.einsum("nd,ne->de", normed_low, direct_grad, preferred_element_type=jnp.float32)
    normed_attn_grad = jnp.einsum(
        "ne,de->nd", direct_grad, w_qkv, preferred_element_type=jnp.float32
    )
    normed_attn_grad = normed_attn_grad + jnp.einsum(
        "ne,de->nd", carried, kv_weight, preferred_element_type=jnp.float32
    )
    input_part, grad_gain_attn, grad_shift_attn = norm_attn_back(normed_attn_grad)
    grad_tokens = (middle_grad + input_part).reshape(tokens.shape)
    grad_qkv = grad_qkv + jnp.concatenate(
        [jnp.zeros((feature_width, feature_width), jnp.float32), kv_part], -1
    )
    (
        grad_qkv,
        grad_out,
        grad_up,
        grad_down,
        grad_gain_attn,
        grad_shift_attn,
        grad_gain_ffn,
        grad_shift_ffn,
    ) = lax.psum(
        (
            grad_qkv,
            grad_out,
            grad_up,
            grad_down,
            grad_gain_attn,
            grad_shift_attn,
            grad_gain_ffn,
            grad_shift_ffn,
        ),
        ("items", "seq"),
    )
    return (
        output,
        grad_tokens,
        grad_qkv,
        grad_out,
        grad_up,
        grad_down,
        grad_gain_attn,
        grad_shift_attn,
        grad_gain_ffn,
        grad_shift_ffn,
    )


def solution(mesh):
    return jax.shard_map(
        shards,
        mesh=mesh,
        in_specs=(
            P("items", "seq", None),
            P("items"),
            P("items", None),
            P(),
            P(),
            P(),
            P(),
            P(),
            P(),
            P(),
            P(),
            P("items", "seq", None),
        ),
        out_specs=(
            P("items", "seq", None),
            P("items", "seq", None),
            P(),
            P(),
            P(),
            P(),
            P(),
            P(),
            P(),
            P(),
        ),
        check_vma=False,
    )
```

profile of v0, /device:TPU:0, one launch (start us, length us, event | category | flops | bytes accessed | tf_op | source)
XLA Modules:
  0.0 352.7 jit_solution(5371661242328786696)
XLA Ops:
  17.4 3.2 collective-permute-start
  38.0 2.5 fusion.68
  43.5 3.5 multiply_convert_fusion
  47.0 2.4 fusion.109
  49.4 2.5 fusion.13
  51.9 7.3 %fusion.7 = bf16[2304,1024]{1,0:T(8,128)(2,1)S(1)} fusion(f32[2304,1024]{1,0:T(8,128)S(1)} %get-tuple-element.40, bf16[2304,256]{1,0:T(8,128)(2,1)S(1)} %fusion.37, bf16[1024,256]{1,0:T(8,128)(2,1)S(1)} %copy-done.37), kind=kOutput, calls=%fused_computation.9 | convolution fusion | flops 1255145472 | bytes 15859712 | tf_op jit(solution)/shard_map/nd,fd->nf/dot_general | solution.py:121
  59.2 2.2 multiply_reduce_fusion.1
  67.5 2.8 reshape.330
  70.2 5.6 %fusion.27 = f32[24,2,96,192]{3,2,1,0:T(8,128)} fusion(bf16[24,24,2,8,128]{4,3,2,1,0:T(8,128)(2,1)} %copy-done.20, bf16[24,96,2,128]{3,2,1,0:T(2,128)(2,1)S(1)} %reshape.330), kind=kOutput, calls=%fused_computation.41 | convolution fusion | flops 226492416 | bytes 7077888 | tf_op jit(solution)/shard_map/rqhd,rkhd->rhqk/dot_general | solution.py:145
  75.8 33.4 %fusion.71 = bf16[24,96,2,128]{3,1,2,0:T(8,128)(2,1)} fusion(bf16[24,24,2,8,128]{4,3,2,1,0:T(8,128)(2,1)} %copy-done.24, f32[24,2,96,192]{3,2,1,0:T(8,128)} %fusion.27, f32[24,2,96,192]{3,2,1,0:T(8,128)} %copy-done.12, f32[24,2,96]{2,1,0:T(2,128)S(1)} %bitcast.136, pred[24,96,192]{2,1,0:T(8,128)(4,1)} %copy-done.31), kind=kOutput, calls=%fused_computation.88 | convolution fusion | flops 233870016 | bytes 11077632 | tf_op jit(solution)/shard_map/rhqk,rkhd->rqhd/dot_general | solution.py:152
  109.2 35.8 %multiply_bitcast_fusion = bf16[24,192,2,128]{3,1,2,0:T(8,128)(2,1)} fusion(f32[24,2,96,192]{3,2,1,0:T(8,128)} %fusion.27, f32[24,2,96,192]{3,2,1,0:T(8,128)} %copy-done.12, f32[24,2,96]{2,1,0:T(2,128)S(1)} %bitcast.137, pred[24,96,192]{2,1,0:T(8,128)(4,1)} %copy-done.31, bf16[24,96,2,128]{3,2,1,0:T(2,128)(2,1)} %reshape.325), kind=kOutput, calls=%fused_computation.15 | convolution fusion | flops 235049664 | bytes 11077632 | tf_op jit(solution)/shard_map/rhqk,rqhd->rkhd/dot_general | solution.py:155
  145.0 4.5 %fusion.50 = bf16[24,192,2,128]{3,1,2,0:T(8,128)(2,1)S(1)} fusion(f32[24,2,96,192]{3,2,1,0:T(8,128)} %copy-done.12, f32[24,2,96]{2,1,0:T(2,128)S(1)} %bitcast.138, bf16[24,96,2,128]{3,2,1,0:T(2,128)(2,1)S(1)} %reshape.330), kind=kOutput, calls=%fused_computation.78 | convolution fusion | flops 228261888 | bytes 7096320 | tf_op jit(solution)/shard_map/rhqk,rqhd->rkhd/dot_general | solution.py:142
  149.5 3.9 %copy.46 = bf16[24,192,2,128]{3,2,1,0:T(2,128)(2,1)} copy(bf16[24,192,2,128]{3,1,2,0:T(8,128)(2,1)S(1)} %fusion.50) | data formatting | bytes 4718592 | tf_op jit(solution)/shard_map/rhqk,rqhd->rkhd/transpose | solution.py:142
  153.4 6.6 %concatenate.62 = bf16[6,4,192,256]{3,2,1,0:T(8,128)(2,1)} reshape(bf16[24,192,2,128]{3,2,1,0:T(2,128)(2,1)} %copy.46) | data formatting | bytes 4718592 | tf_op jit(solution)/shard_map/concatenate | solution.py:158
  160.1 5.6 %copy.43 = bf16[24,192,2,128]{3,2,1,0:T(2,128)(2,1)} copy(bf16[24,192,2,128]{3,1,2,0:T(8,128)(2,1)} %multiply_bitcast_fusion) | data formatting | bytes 4718592 | tf_op jit(solution)/shard_map/mul | solution.py:155
  165.6 6.4 %concatenate.61 = bf16[6,4,192,256]{3,2,1,0:T(8,128)(2,1)} reshape(bf16[24,192,2,128]{3,2,1,0:T(2,128)(2,1)} %copy.43) | data formatting | bytes 4718592 | tf_op jit(solution)/shard_map/concatenate | solution.py:158
  178.8 2.6 fusion.54
  184.3 3.1 fusion.100
  191.9 4.7 %fusion.102 = (f32[256]{0:T(256)S(1)}, f32[2304]{0:T(1024)S(1)}, f32[2304,256]{1,0:T(8,128)}) fusion(f32[256]{0:T(256)S(1)} %copy-done.33, f32[2304]{0:T(1024)S(1)} %div.47, bf16[6,384,256]{2,1,0:T(8,128)(2,1)S(1)} %copy-done.2, f32[2304,256]{1,0:T(8,128)} %fusion.54, bf16[2304,512]{1,0:T(8,128)(2,1)} %bitcast.124, bf16[256,768]{1,0:T(8,128)(2,1)S(1)} %copy-done.28), kind=kOutput, calls=%fused_computation.139 | convolution fusion | flops 608105984 | bytes 8543232 | tf_op jit(solution)/shard_map/ne,de->nd/dot_general | solution.py:178
  196.6 3.6 %multiply_reduce_fusion.2 = (f32[256]{0:T(256)S(1)}, f32[2304]{0:T(1024)S(1)}) fusion(f32[2304,256]{1,0:T(8,128)} %get-tuple-element.42, bf16[6,384,256]{2,1,0:T(8,128)(2,1)S(1)} %copy-done.2, f32[2304]{0:T(1024)S(1)} %rsqrt.23, f32[2304]{0:T(1024)S(1)} %div.47, f32[2304]{0:T(1024)S(1)} %multiply_multiply_fusion.2, f32[256]{0:T(256)S(1)} %copy-done.33), kind=kLoop, calls=%fused_computation.58 | loop fusion | flops 6485504 | bytes 3577856 | tf_op jit(solution)/shard_map/transpose(jvp())/reduce_sum | solution.py:26
  200.3 43.4 %all-reduce.1 = (f32[256]{0:T(256)}, f32[256]{0:T(256)}, f32[256]{0:T(256)}, f32[256]{0:T(256)}) all-reduce(f32[256]{0:T(256)S(1)} %get-tuple-element.12, f32[256]{0:T(256)S(1)} %get-tuple-element.15, f32[256]{0:T(256)S(1)} %get-tuple-element.10, f32[256]{0:T(256)S(1)} %get-tuple-element.14), channel_id=1, replica_groups=mesh['items'=4,'seq'=8] {'items','seq'}, use_global_device_ids=true, to_apply=%region_16.17 | all-reduce | flops 1024 | bytes 8192 | tf_op jit(solution)/shard_map/psum | solution.py:195
  243.6 5.5 %add_add_fusion.2 = f32[2304,256]{1,0:T(8,128)} fusion(f32[2304,256]{1,0:T(8,128)} %copy-done.9, bf16[6,384,256]{2,1,0:T(8,128)(2,1)S(1)} %copy-done.18, f32[2304]{0:T(1024)S(1)} %negate_multiply_fusion, f32[2304]{0:T(1024)S(1)} %negate_multiply_fusion.1, f32[2304]{0:T(1024)S(1)} %reshape.333, f32[2304]{0:T(1024)S(1)} %multiply_multiply_fusion.2, ...), kind=kLoop, calls=%fused_computation.60 | loop fusion | flops 7667712 | bytes 9493504 | tf_op jit(solution)/shard_map/add | solution.py:182
  249.1 90.5 %all-reduce.5.cloned.1.call-done = (f32[256,768]{1,0:T(8,128)}, f32[256,256]{1,0:T(8,128)}, f32[256,1024]{1,0:T(8,128)}, f32[1024,256]{1,0:T(8,128)}) async-done(((f32[256,768]{1,0:T(8,128)}, f32[256,256]{1,0:T(8,128)}, f32[256,1024]{1,0:T(8,128)}, f32[1024,256]{1,0:T(8,128)}), (f32[256,768]{1,0:T(8,128)}, f32[256,256]{1,0:T(8,128)}, f32[256,1024]{1,0:T(8,128)}, ...) | async-done | bytes 3145744 | tf_op jit(solution)/shard_map/psum | solution.py:195
  339.6 2.2 copy.107
  (155 shorter events, 53.8 us)
Async XLA Ops:
  7.2 36.3 %copy-start = (bf16[256,1024]{1,0:T(8,128)(2,1)S(1)}, bf16[256,1024]{1,0:T(8,128)(2,1)}, u32[]{:S(2)}) copy-start(bf16[256,1024]{1,0:T(8,128)(2,1)} %param.17) | copy-start | bytes 1572868
  7.2 3.9 %copy-start.2 = (bf16[6,384,256]{2,1,0:T(8,128)(2,1)S(1)}, bf16[6,384,256]{2,1,0:T(8,128)(2,1)}, u32[]{:S(2)}) copy-start(bf16[6,384,256]{2,1,0:T(8,128)(2,1)} %param.12) | copy-start | bytes 3538948
  7.2 3.9 %copy-start.33 = (f32[256]{0:T(256)S(1)}, f32[256]{0:T(256)}, u32[]{:S(2)}) copy-start(f32[256]{0:T(256)} %param.19) | copy-start | bytes 3076
  7.2 3.9 %copy-start.34 = (f32[256]{0:T(256)S(1)}, f32[256]{0:T(256)}, u32[]{:S(2)}) copy-start(f32[256]{0:T(256)} %param.20) | copy-start | bytes 3076
  7.2 6.3 %copy-start.28 = (bf16[256,768]{1,0:T(8,128)(2,1)S(1)}, bf16[256,768]{1,0:T(8,128)(2,1)}, u32[]{:S(2)}) copy-start(bf16[256,768]{1,0:T(8,128)(2,1)} %param.15) | copy-start | bytes 1179652
  7.2 332.4 %all-reduce.5.cloned.1.call-start = ((), (), s32[]{:S(2)}) async-start(), calls=%async_computation | async-start | bytes 6291456 | tf_op jit(solution)/shard_map/psum | solution.py:195
  14.7 6.0 %copy-start.35 = (s32[6]{0:T(128)S(1)}, s32[6]{0:T(128)}, u32[]{:S(2)}) copy-start(s32[6]{0:T(128)} %param.13) | copy-start | bytes 76
  14.9 2.5 copy-start.4
  17.4 13.5 %collective-permute-start = (bf16[6,96,512]{2,1,0:T(8,128)(2,1)}, bf16[6,96,512]{2,1,0:T(8,128)(2,1)}, u32[]{:S(2)}, u32[]{:S(2)}) collective-permute-start(bf16[6,96,512]{2,1,0:T(8,128)(2,1)} %slice_bitcast_fusion), channel_id=1, source_target_pairs={{0,1},{1,2},{2,3},{3,4},{4,5},{5,6},{6,7},{8,9},{9,10},{10,11},{11... | collective-permute-start | bytes 1769480 | tf_op jit(solution)/shard_map/ppermute | solution.py:19
  23.4 3.8 %slice-start = ((bf16[2304,768]{1,0:T(8,128)(2,1)}), bf16[2304,256]{1,0:T(8,128)(2,1)S(1)}, s32[]{:S(2)}) async-start(bf16[2304,768]{1,0:T(8,128)(2,1)} %copy-done.3), calls=%async_computation.1 | async-start | bytes 2359296 | tf_op jit(solution)/shard_map/slice | solution.py:91
  28.4 2.5 copy-start.23
  29.0 4.6 %copy-start.31 = (pred[24,96,192]{2,1,0:T(8,128)(4,1)}, pred[24,96,192]{2,1,0:T(8,128)(4,1)S(1)}, u32[]{:S(2)}) copy-start(pred[24,96,192]{2,1,0:T(8,128)(4,1)S(1)} %and_or_fusion) | copy-start | bytes 1327108
  33.6 4.0 %copy-start.20 = (bf16[24,24,2,8,128]{4,3,2,1,0:T(8,128)(2,1)}, bf16[24,24,2,8,128]{4,3,2,1,0:T(8,128)(2,1)S(1)}, u32[]{:S(2)}) copy-start(bf16[24,24,2,8,128]{4,3,2,1,0:T(8,128)(2,1)S(1)} %get-tuple-element.30) | copy-start | bytes 7077892
  42.8 18.7 %copy-start.7 = (f32[2304,256]{1,0:T(8,128)}, f32[2304,256]{1,0:T(8,128)S(1)}, u32[]{:S(2)}) copy-start(f32[2304,256]{1,0:T(8,128)S(1)} %get-tuple-element.38) | copy-start | bytes 7077892
  172.1 2.6 copy-start.11
  177.2 10.1 %collective-permute-start.1 = (bf16[6,96,512]{2,1,0:T(8,128)(2,1)S(1)}, bf16[6,96,512]{2,1,0:T(8,128)(2,1)S(1)}, u32[]{:S(2)}, u32[]{:S(2)}) collective-permute-start(bf16[6,96,512]{2,1,0:T(8,128)(2,1)S(1)} %fusion.85), channel_id=1, source_target_pairs={{1,0},{2,1},{3,2},{4,3},{5,4},{6,5},{7,6},{9,8},{10,9},{11,10},{12... | collective-permute-start | bytes 1769480 | tf_op jit(solution)/shard_map/ppermute | solution.py:19
  178.5 4.3 %slice-start.1 = ((s8[4718592]{0:T(1024)(128)(4,1)}), s8[4194304]{0:T(1024)(128)(4,1)S(1)}, s32[]{:S(2)}) async-start(s8[4718592]{0:T(1024)(128)(4,1)} %bitcast.143), calls=%async_computation.2 | async-start | bytes 8388608
  178.8 2.6 copy-start.14
  178.8 2.6 copy-start.16
  178.8 4.0 %slice-start.2 = ((s8[4718592]{0:T(1024)(128)(4,1)}), s8[524288]{0:T(1024)(128)(4,1)S(1)}, s32[]{:S(2)}) async-start(s8[4718592]{0:T(1024)(128)(4,1)} %bitcast.143), calls=%async_computation.3 | async-start | bytes 1048576
  196.6 47.0 %copy-start.18 = (bf16[6,384,256]{2,1,0:T(8,128)(2,1)S(1)}, bf16[6,384,256]{2,1,0:T(8,128)(2,1)}, u32[]{:S(2)}) copy-start(bf16[6,384,256]{2,1,0:T(8,128)(2,1)} %param.23) | copy-start | bytes 3538948
  339.6 3.9 %copy-start.30 = (f32[256,1024]{1,0:T(8,128)S(1)}, f32[256,1024]{1,0:T(8,128)}, u32[]{:S(2)}) copy-start(f32[256,1024]{1,0:T(8,128)} %get-tuple-element.47) | copy-start | bytes 3145732
  339.6 4.9 %copy-start.29 = (f32[1024,256]{1,0:T(8,128)S(1)}, f32[1024,256]{1,0:T(8,128)}, u32[]{:S(2)}) copy-start(f32[1024,256]{1,0:T(8,128)} %get-tuple-element.48) | copy-start | bytes 3145732
  339.6 5.8 %copy-start.1 = (bf16[256,1024]{1,0:T(8,128)(2,1)S(1)}, bf16[256,1024]{1,0:T(8,128)(2,1)}, u32[]{:S(2)}) copy-start(bf16[256,1024]{1,0:T(8,128)(2,1)} %param.17) | copy-start | bytes 1572868
  (22 other events, 34.9 us)
Sparse Core Ops, SparseCore 0:
  196.7 142.8 all-reduce.4
where the time goes:
time: 360 us; the launch traced here: 353 us
  matrix products  119 us (33%)
  waiting for transfers between devices  90.5 us (25%)
  local copies, waits for them, and re-layouts  50.2 us (14%)
  blocking collectives  43.4 us (12%)
  other arithmetic  29.8 us (8%)
  between operations  15.2 us (4%)
  starting transfers between devices  4.51 us (1%)
    psum x1, waiting for transfers between devices, shards(): lax.psum((grad_qkv, grad_out, grad_up, grad_down, grad_gain_attn, grad_sh...  90.5 us
    psum x1, blocking collectives, shards(): lax.psum((grad_qkv, grad_out, grad_up, grad_down, grad_gain_attn, grad_sh...  43.4 us
    dot_general x1, matrix products, shards(): jnp.einsum('rhqk,rqhd->rkhd', score_grad, queries, preferred_element_type...  35.8 us
    dot_general x1, matrix products, shards(): jnp.einsum('rhqk,rkhd->rqhd', score_grad, keys_all, preferred_element_typ...  33.4 us
    unnamed x89, local copies, waits for them, and re-layouts  18.2 us
    concatenate x2, local copies, waits for them, and re-layouts, shards(): jnp.concatenate([key_grad.reshape(batch_rows, 2 * ROW, feature_width), va...  13.1 us
    dot_general x1, matrix products, shards(): jnp.einsum('nd,fd->nf', ffn_grad_low, w_down, preferred_element_type=jnp....  7.27 us
  transfers between devices with their start and end apart: 3, of which 1 were waited for; matrix products, arithmetic and copies ran while one was open for 7% of the time, Pallas kernels for 0%

commit v1 on v0

v1 whole, which is shorter than its diff:
```python
import functools
import math

import jax
import jax.numpy as jnp
from jax import lax
from jax.experimental import pallas as pl
from jax.experimental.pallas import tpu as pltpu
from jax.sharding import PartitionSpec as P

HEADS = 2
HEAD_DIM = 128
ROW = 96
D = HEADS * HEAD_DIM

epsilon = 1e-05
branch_scale = 0.7071067811865476
masked_value = -1e30
score_scale = HEAD_DIM ** (-0.5)
log2e = math.log2(math.e)
gelu_in = math.sqrt(2 / math.pi)
gelu_cube = gelu_in * 0.044715
f32 = jnp.float32
bf16 = jnp.bfloat16


def dot(left, right, left_dim=1, right_dim=0):
    return lax.dot_general(
        left, right, (((left_dim,), (right_dim,)), ((), ())), preferred_element_type=f32
    )


def normalise(inputs):
    average = jnp.mean(inputs, -1, keepdims=True)
    centred = inputs - average
    spread = jnp.mean(centred * centred, -1, keepdims=True)
    factor = lax.rsqrt(spread + epsilon)
    return centred * factor, factor


def norm_back(grad, normed, factor, gain):
    e = grad * gain
    first = jnp.mean(e, -1, keepdims=True)
    second = jnp.mean(e * normed, -1, keepdims=True)
    return factor * (e - first - normed * second)


def fold_rows(values):
    count = values.shape[0] // 8
    return jnp.sum(values.reshape(count, 8, values.shape[1]), 0)


def layer_kernel(
    items,
    rows,
    tokens_ref,
    halo_ref,
    cot_ref,
    alive_ref,
    keys_ref,
    wqkv_ref,
    wout_ref,
    wup_ref,
    wdown_ref,
    vecs_ref,
    output_ref,
    gtok_ref,
    ghalo_ref,
    gqkv_ref,
    gout_ref,
    gup_ref,
    gdown_ref,
    gvec_ref,
    h1,
    n1,
    r1,
    proj,
    exps,
    inv,
    att,
    middle,
    n2,
    r2,
    h2,
    dbr,
    hid,
    dpre,
    dmid,
    datt,
    dproj,
):
    block = rows * ROW
    total = items * block
    steps = 3
    size = total // steps
    gain_attn = vecs_ref[0:1]
    shift_attn = vecs_ref[1:2]
    gain_ffn = vecs_ref[2:3]
    shift_ffn = vecs_ref[3:4]
    ff = wup_ref.shape[1]
    chunks = ff // 256

    def first_norm(x, i, at, count):
        normed, factor = normalise(x)
        low = (normed * gain_attn + shift_attn).astype(bf16)
        h1[i, at : at + count] = low
        n1[i, at : at + count] = normed.astype(bf16)
        r1[i, at : at + count] = jnp.broadcast_to(factor, (count, 128))
        return low

    def project(i, _):
        low = first_norm(tokens_ref[i].astype(f32), i, ROW, block)
        proj[i, ROW:] = dot(low, wqkv_ref[...]).astype(bf16)
        return _

    lax.fori_loop(0, items, project, 0)

    def project_halo(i, _):
        low = first_norm(halo_ref[i].astype(f32), i, 0, ROW)
        proj[i, :ROW, D:] = dot(low, wqkv_ref[:, D:]).astype(bf16)
        return _

    lax.fori_loop(0, items, project_halo, 0)

    query_pos = lax.broadcasted_iota(jnp.int32, (ROW, 2 * ROW), 0)
    key_pos = lax.broadcasted_iota(jnp.int32, (ROW, 2 * ROW), 1) - ROW
    causal = jnp.where(key_pos <= query_pos, 0.0, masked_value)
    itself = jnp.where(key_pos == query_pos, 0.0, masked_value)

    def attend(i, _):
        for r in range(rows):
            bias = jnp.maximum(jnp.minimum(causal, keys_ref[i, r : r + 1]), itself)
            for h in range(HEADS):
                at = h * HEAD_DIM
                q = proj[i, (r + 1) * ROW : (r + 2) * ROW, at : at + HEAD_DIM]
                k = proj[i, r * ROW : (r + 2) * ROW, D + at : D + at + HEAD_DIM]
                v = proj[i, r * ROW : (r + 2) * ROW, 2 * D + at : 2 * D + at + HEAD_DIM]
                scores = dot(q, k, 1, 1) * (score_scale * log2e) + bias
                top = jnp.max(scores, -1, keepdims=True)
                e = jnp.exp2(scores - top)
                share = 1.0 / jnp.sum(e, -1, keepdims=True)
                low = e.astype(bf16)
                exps[i, r * HEADS + h, :, : 2 * ROW] = low
                share = jnp.broadcast_to(share, (ROW, HEAD_DIM))
                inv[i, r * ROW : (r + 1) * ROW, at : at + HEAD_DIM] = share
                att[i, r * ROW : (r + 1) * ROW, at : at + HEAD_DIM] = (dot(low, v) * share).astype(bf16)
        mid = tokens_ref[i].astype(f32) + branch_scale * dot(att[i], wout_ref[...])
        middle[i] = mid
        normed, factor = normalise(mid)
        n2[i] = normed.astype(bf16)
        r2[i] = jnp.broadcast_to(factor, (block, 128))
        h2[pl.ds(i * block, block)] = (normed * gain_ffn + shift_ffn).astype(bf16)
        mask = jnp.concatenate([alive_ref[i]] * 2, 1)
        dbr[pl.ds(i * block, block)] = (branch_scale * (mask * cot_ref[i].astype(f32))).astype(bf16)
        return _

    lax.fori_loop(0, items, attend, 0)

    gup_ref[...] = jnp.zeros_like(gup_ref)
    gdown_ref[...] = jnp.zeros_like(gdown_ref)
    for c in range(chunks):
        cols = slice(c * 256, (c + 1) * 256)

        def feed(t, _):
            here = pl.ds(pl.multiple_of(t * size, 128), size)
            u = dot(h2[here], wup_ref[:, cols])
            back = dot(dbr[here], wdown_ref[cols], 1, 1)
            square = u * u
            s = 0.5 * jnp.tanh(u * (gelu_in + gelu_cube * square)) + 0.5
            hidden = (u * s).astype(bf16)
            slope = s + u * ((s - s * s) * (2 * gelu_in + 6 * gelu_cube * square))
            before = (back * slope).astype(bf16)
            hid[here, cols] = hidden
            dpre[here, cols] = before
            gdown_ref[:, cols] += dot(dbr[here], hidden, 0, 0)
            gup_ref[:, cols] += dot(h2[here], before, 0, 0)
            return _

        lax.fori_loop(0, steps, feed, 0)

    gvec_ref[...] = jnp.zeros_like(gvec_ref)
    gout_ref[...] = jnp.zeros_like(gout_ref)

    def middle_back(i, _):
        here = pl.ds(pl.multiple_of(i * block, 64), block)
        grad = dot(dpre[here], wup_ref[...], 1, 1)
        normed = n2[i].astype(f32)
        gvec_ref[16:24] += fold_rows(grad * normed)
        gvec_ref[24:32] += fold_rows(grad)
        factor = jnp.concatenate([r2[i]] * 2, 1)
        mask = jnp.concatenate([alive_ref[i]] * 2, 1)
        grad = mask * cot_ref[i].astype(f32) + norm_back(grad, normed, factor, gain_ffn)
        dmid[i] = grad
        low = (branch_scale * grad).astype(bf16)
        gout_ref[...] += dot(att[i], low, 0, 0)
        datt[i] = dot(low, wout_ref[...], 1, 1).astype(bf16)
        return _

    lax.fori_loop(0, items, middle_back, 0)

    def attend_back(i, _):
        for h in range(HEADS):
            at = h * HEAD_DIM
            held_k = None
            held_v = None
            for r in range(rows):
                q = proj[i, (r + 1) * ROW : (r + 2) * ROW, at : at + HEAD_DIM]
                k = proj[i, r * ROW : (r + 2) * ROW, D + at : D + at + HEAD_DIM]
                v = proj[i, r * ROW : (r + 2) * ROW, 2 * D + at : 2 * D + at + HEAD_DIM]
                own = slice(r * ROW, (r + 1) * ROW)
                grad = datt[i, own, at : at + HEAD_DIM].astype(f32) * inv[i, own, at : at + HEAD_DIM]
                low = grad.astype(bf16)
                row_dot = jnp.sum(grad * att[i, own, at : at + HEAD_DIM].astype(f32), -1, keepdims=True)
                e = exps[i, r * HEADS + h, :, : 2 * ROW]
                ds = (e.astype(f32) * ((dot(low, v, 1, 1) - row_dot) * score_scale)).astype(bf16)
                dv = dot(e, low, 0, 0)
                dk = dot(ds, q, 0, 0)
                dproj[i, (r + 1) * ROW : (r + 2) * ROW, at : at + HEAD_DIM] = dot(ds, k).astype(bf16)
                first_k, first_v = dk[:ROW], dv[:ROW]
                if held_k is not None:
                    first_k += held_k
                    first_v += held_v
                dproj[i, r * ROW : (r + 1) * ROW, D + at : D + at + HEAD_DIM] = first_k.astype(bf16)
                dproj[i, r * ROW : (r + 1) * ROW, 2 * D + at : 2 * D + at + HEAD_DIM] = first_v.astype(bf16)
                held_k, held_v = dk[ROW:], dv[ROW:]
            dproj[i, rows * ROW :, D + at : D + at + HEAD_DIM] = held_k.astype(bf16)
            dproj[i, rows * ROW :, 2 * D + at : 2 * D + at + HEAD_DIM] = held_v.astype(bf16)
        dproj[i, :ROW, :D] = jnp.zeros((ROW, D), bf16)
        return _

    lax.fori_loop(0, items, attend_back, 0)

    gqkv_ref[...] = jnp.zeros_like(gqkv_ref)

    def weight_back(i, _):
        gqkv_ref[...] += dot(h1[i], dproj[i], 0, 0)
        return _

    lax.fori_loop(0, items, weight_back, 0)

    def tokens_back(i, _):
        grad = dot(dproj[i], wqkv_ref[...], 1, 1)
        normed = n1[i].astype(f32)
        gvec_ref[0:8] += fold_rows(grad * normed)
        gvec_ref[8:16] += fold_rows(grad)
        factor = jnp.concatenate([r1[i]] * 2, 1)
        grad = norm_back(grad, normed, factor, gain_attn)
        ghalo_ref[i] = grad[:ROW].astype(bf16)
        gtok_ref[i] = dmid[i] + grad[ROW:]
        return _

    lax.fori_loop(0, items, tokens_back, 0)

    def finish(i, _):
        here = pl.ds(pl.multiple_of(i * block, 64), block)
        branch = dot(hid[here], wdown_ref[...])
        mask = jnp.concatenate([alive_ref[i]] * 2, 1)
        output_ref[i] = (mask * (middle[i] + branch_scale * branch)).astype(bf16)
        return _

    lax.fori_loop(0, items, finish, 0)


def from_behind(block, axis, distance):
    devices = range(lax.axis_size(axis))
    route = [(i - distance, i) for i in devices if i - distance in devices]
    return lax.ppermute(block, axis, route)


def shards(
    tokens,
    lengths,
    pad_mask,
    w_qkv,
    w_out,
    w_up,
    w_down,
    gain_attn,
    shift_attn,
    gain_ffn,
    shift_ffn,
    cotangent,
):
    items, block, width = tokens.shape
    rows = block // ROW
    total = items * block
    ff = w_up.shape[1]
    first_pos = lax.axis_index("seq") * block
    padded = jnp.pad(pad_mask, ((0, 0), (ROW, 0)))
    positions = first_pos - ROW + jnp.arange(block + ROW, dtype=jnp.int32)
    here = lax.dynamic_slice_in_dim(padded, first_pos, block + ROW, 1)
    alive = (positions[None, :] < lengths[:, None]) & (here == 1)
    alive_cols = jnp.broadcast_to(alive[:, ROW:, None].astype(f32), (items, block, 128))
    key_bias = jnp.where(alive, 0.0, masked_value)
    key_bias = jnp.stack([key_bias[:, r * ROW : (r + 2) * ROW] for r in range(rows)], 1)
    halo = from_behind(tokens[:, -ROW:], "seq", 1)
    vecs = jnp.stack([gain_attn, shift_attn, gain_ffn, shift_ffn])
    ext = block + ROW
    shapes = [
        jax.ShapeDtypeStruct((items, block, width), bf16),
        jax.ShapeDtypeStruct((items, block, width), f32),
        jax.ShapeDtypeStruct((items, ROW, width), bf16),
        jax.ShapeDtypeStruct((width, 3 * width), f32),
        jax.ShapeDtypeStruct((width, width), f32),
        jax.ShapeDtypeStruct((width, ff), f32),
        jax.ShapeDtypeStruct((width, ff), f32),
        jax.ShapeDtypeStruct((32, width), f32),
    ]
    outs = pl.pallas_call(
        functools.partial(layer_kernel, items, rows),
        out_shape=shapes,
        in_specs=[pl.BlockSpec(memory_space=pltpu.VMEM)] * 10,
        out_specs=[pl.BlockSpec(memory_space=pltpu.VMEM)] * 8,
        scratch_shapes=[
            pltpu.VMEM((items, ext, width), bf16),
            pltpu.VMEM((items, ext, width), bf16),
            pltpu.VMEM((items, ext, 128), f32),
            pltpu.VMEM((items, ext, 3 * width), bf16),
            pltpu.VMEM((items, rows * HEADS, ROW, 256), bf16),
            pltpu.VMEM((items, block, width), f32),
            pltpu.VMEM((items, block, width), bf16),
            pltpu.VMEM((items, block, width), f32),
            pltpu.VMEM((items, block, width), bf16),
            pltpu.VMEM((items, block, 128), f32),
            pltpu.VMEM((total, width), bf16),
            pltpu.VMEM((total, width), bf16),
            pltpu.VMEM((total, ff), bf16),
            pltpu.VMEM((total, ff), bf16),
            pltpu.VMEM((items, block, width), f32),
            pltpu.VMEM((items, block, width), bf16),
            pltpu.VMEM((items, ext, 3 * width), bf16),
        ],
        compiler_params=pltpu.CompilerParams(vmem_limit_bytes=60 * 2**20),
    )(tokens, halo, cotangent, alive_cols, key_bias, w_qkv, w_out, w_up, w_down, vecs)
    output, gtok, ghalo, gqkv, gout, gup, gdown, gvec = outs
    returned = from_behind(ghalo, "seq", -1)
    gtok = gtok.at[:, -ROW:].add(returned.astype(f32))
    gvec = jnp.sum(gvec.reshape(4, 8, width), 1)
    gqkv, gout, gup, gdown, gvec = lax.psum((gqkv, gout, gup, gdown.T, gvec), ("items", "seq"))
    return (output, gtok, gqkv, gout, gup, gdown, gvec[0], gvec[1], gvec[2], gvec[3])


def solution(mesh):
    split = P("items", "seq", None)
    return jax.shard_map(
        shards,
        mesh=mesh,
        in_specs=(split, P("items"), P("items", None)) + (P(),) * 8 + (split,),
        out_specs=(split, split) + (P(),) * 8,
        check_vma=False,
    )
```

time: 360 us -> 233 us (0.65); the launches traced: 353 us -> 232 us
  matrix products: 119 us -> 0 us
  Pallas kernels: 0 us -> 60.7 us
  local copies, waits for them, and re-layouts: 50.2 us -> 9.24 us
  other arithmetic: 29.8 us -> 4.84 us
  waiting for transfers between devices: 90.5 us -> 94.2 us
    dot_general x20 -> x0, matrix products: 119 us -> none  [the longest x1 35.8 us: shards(): jnp.einsum('rhqk,rqhd->rkhd', score_grad, queries, preferred_element_type...]
    pallas_call x0 -> x1, Pallas kernels: none -> 60.7 us  [shards(): pl.pallas_call(functools.partial(layer_kernel, items, rows), out_shape=sh...]
    concatenate x4 -> x0, local copies, waits for them, and re-layouts: 13.2 us -> none  [the longest x2 13.1 us: shards(): jnp.concatenate([key_grad.reshape(batch_rows, 2 * ROW, feature_width), va...]
    unnamed x89 -> x16, local copies, waits for them, and re-layouts: 18.2 us -> 6.17 us
    reduce_sum x6 -> x1, other arithmetic: 11.7 us -> 0.02 us  [shards(): gvec = jnp.sum(gvec.reshape(4, 8, width), 1)]
    convert_element_type x5 -> x1, other arithmetic: 6.91 us -> 0.07 us  [shards(): alive[:, ROW:, None].astype(f32)]
    mul x1 -> x0, local copies, waits for them, and re-layouts: 5.57 us -> none  [shards(): jnp.einsum('rhqk,rqhd->rkhd', score_grad, queries, preferred_element_type...]
    add x4 -> x1, other arithmetic: 5.5 us -> 0.01 us  [shards(): positions = first_pos - ROW + jnp.arange(block + ROW, dtype=jnp.int32)]
  transfers between devices with their start and end apart: 3 -> 3, of which waited for: 1 -> 1; matrix products, arithmetic and copies ran while one was open for 7% -> 2% of each run, Pallas kernels for 0% -> 0%
where the time goes in v1:
time: 233 us; the launch traced here: 232 us
  waiting for transfers between devices  94.2 us (40%)
  Pallas kernels  60.7 us (26%)
  blocking collectives  45.6 us (20%)
  between operations  14.1 us (6%)
  local copies, waits for them, and re-layouts  9.24 us (4%)
  other arithmetic  4.84 us (2%)
  starting transfers between devices  3.69 us (2%)
    psum x1, waiting for transfers between devices, shards(): lax.psum((gqkv, gout, gup, gdown.T, gvec), ('items', 'seq'))  94.2 us
    pallas_call x1, Pallas kernels, shards(): pl.pallas_call(functools.partial(layer_kernel, items, rows), out_shape=sh...  60.7 us
    psum x1, blocking collectives, shards(): lax.psum((gqkv, gout, gup, gdown.T, gvec), ('items', 'seq'))  45.6 us
    unnamed x16, local copies, waits for them, and re-layouts  6.17 us
  transfers between devices with their start and end apart: 3, of which 1 were waited for; matrix products, arithmetic and copies ran while one was open for 2% of the time, Pallas kernels for 0%

profile of v1, /device:TPU:0, one launch (start us, length us, event | category | flops | bytes accessed | tf_op | source)
XLA Modules:
  0.0 232.5 jit_solution(11777130349717461808)
XLA Ops:
  7.2 0.0 all-reduce.4.cloned.1.call-start
  7.2 1.0 slice.54
  8.2 2.4 %collective-permute-start = (bf16[6,96,256]{2,1,0:T(8,128)(2,1)S(1)}, bf16[6,96,256]{2,1,0:T(8,128)(2,1)S(1)}, u32[]{:S(2)}, u32[]{:S(2)}) collective-permute-start(bf16[6,96,256]{2,1,0:T(8,128)(2,1)S(1)} %slice.54), channel_id=1, source_target_pairs={{0,1},{1,2},{2,3},{3,4},{4,5},{5,6},{6,7},{8,9},{9,10},{10,11},{11... | collective-permute-start | bytes 884744 | tf_op jit(solution)/shard_map/ppermute | solution.py:267
  10.6 0.8 broadcast_select_fusion
  11.4 0.1 slice_bitcast_fusion.2
  11.6 0.6 pad_maximum_fusion.keys_ref
  12.2 1.3 pad_maximum_fusion.1.vecs_ref
  13.5 0.1 slice_convert_fusion
  13.6 0.0 collective-permute-done.halo_ref
  13.6 1.4 broadcast_in_dim.16.alive_ref
  15.0 60.7 %shard_map.195 = (bf16[6,384,256]{2,1,0:T(8,128)(2,1)}, f32[6,384,256]{2,1,0:T(8,128)}, bf16[6,96,256]{2,1,0:T(8,128)(2,1)}, f32[256,768]{1,0:T(8,128)}, f32[256...) custom-call(bf16[6,384,256]{2,1,0:T(8,128)(2,1)} %tokens_ref.1, ...), custom_call_target="tpu_custom_call" | custom-call | tf_op jit(solution)/shard_map/pallas_call | solution.py:309
  75.7 0.0 copy-start.5
  75.8 0.0 all-reduce.4.cloned.1.call-update
  75.8 0.9 copy-done.5
  76.7 1.3 collective-permute-start.1
  78.0 45.6 %psum.39 = f32[4,256]{1,0:T(4,128)S(1)} all-reduce(f32[4,256]{1,0:T(4,128)S(1)} %bitcast_reduce_fusion), channel_id=1, replica_groups=mesh['items'=4,'seq'=8] {'items','seq'}, use_global_device_ids=true, to_apply=%region_5.6 | all-reduce | flops 1024 | bytes 8192 | tf_op jit(solution)/shard_map/psum | solution.py:339
  123.7 0.6 fusion.1
  124.2 0.0 collective-permute-done.1
  124.3 2.0 add_dynamic-update-slice_fusion
  126.2 94.2 %all-reduce.4.cloned.1.call-done = (f32[256,768]{1,0:T(8,128)}, f32[256,256]{1,0:T(8,128)}, f32[256,1024]{1,0:T(8,128)}, f32[1024,256]{0,1:T(8,128)}) async-done(((f32[256,768]{1,0:T(8,128)}, f32[256,256]{1,0:T(8,128)}, f32[256,1024]{1,0:T(8,128)}, f32[1024,256]{0,1:T(8,128)}), (f32[256,768]{1,0:T(8,128)}, f32[256,256]{1,0:T(8,128)}, f32[256,1024]{1,0:T(8,128)}, ...) | async-done | bytes 3145744 | tf_op jit(solution)/shard_map/psum | solution.py:339
  220.4 2.7 %copy.25 = f32[1024,256]{1,0:T(8,128)} copy(f32[1024,256]{0,1:T(8,128)} %get-tuple-element.51) | data formatting | bytes 2097152
  223.1 0.9 copy.31
  224.0 0.7 copy.32
  224.7 1.0 copy.33
  (16 shorter events, 0.1 us)
Async XLA Ops:
  7.2 213.2 %all-reduce.4.cloned.1.call-start = ((), (), s32[]{:S(2)}) async-start(), calls=%async_computation | async-start | bytes 6291456 | tf_op jit(solution)/shard_map/psum | solution.py:339
  8.2 5.4 %collective-permute-start = (bf16[6,96,256]{2,1,0:T(8,128)(2,1)S(1)}, bf16[6,96,256]{2,1,0:T(8,128)(2,1)S(1)}, u32[]{:S(2)}, u32[]{:S(2)}) collective-permute-start(bf16[6,96,256]{2,1,0:T(8,128)(2,1)S(1)} %slice.54), channel_id=1, source_target_pairs={{0,1},{1,2},{2,3},{3,4},{4,5},{5,6},{6,7},{8,9},{9,10},{10,11},{11... | collective-permute-start | bytes 884744 | tf_op jit(solution)/shard_map/ppermute | solution.py:267
  13.6 1.4 copy-start.2
  75.7 1.0 copy-start.5
  75.8 2.2 copy-start.4
  76.7 47.5 %collective-permute-start.1 = (bf16[6,96,256]{2,1,0:T(8,128)(2,1)S(1)}, bf16[6,96,256]{2,1,0:T(8,128)(2,1)S(1)}, u32[]{:S(2)}, u32[]{:S(2)}) collective-permute-start(bf16[6,96,256]{2,1,0:T(8,128)(2,1)S(1)} %copy-done.5), channel_id=1, source_target_pairs={{1,0},{2,1},{3,2},{4,3},{5,4},{6,5},{7,6},{9,8},{10,9},{11,10},{12... | collective-permute-start | bytes 884744 | tf_op jit(solution)/shard_map/ppermute | solution.py:267
  220.4 2.7 %copy-start.1 = (f32[256,768]{1,0:T(8,128)S(1)}, f32[256,768]{1,0:T(8,128)}, u32[]{:S(2)}) copy-start(f32[256,768]{1,0:T(8,128)} %get-tuple-element.64) | copy-start | bytes 2359300
  220.4 3.6 %copy-start.3 = (f32[256,256]{1,0:T(8,128)S(1)}, f32[256,256]{1,0:T(8,128)}, u32[]{:S(2)}) copy-start(f32[256,256]{1,0:T(8,128)} %get-tuple-element.65) | copy-start | bytes 786436
  220.4 4.3 %copy-start = (f32[256,1024]{1,0:T(8,128)S(1)}, f32[256,1024]{1,0:T(8,128)}, u32[]{:S(2)}) copy-start(f32[256,1024]{1,0:T(8,128)} %get-tuple-element.66) | copy-start | bytes 3145732
Sparse Core Ops, SparseCore 0:
  75.9 144.4 all-reduce.3

commit v2 on v1

v2 whole, which is shorter than its diff:
```python
import functools
import math

import jax
import jax.numpy as jnp
from jax import lax
from jax.experimental import pallas as pl
from jax.experimental.pallas import tpu as pltpu
from jax.sharding import PartitionSpec as P

HEADS = 2
HEAD_DIM = 128
ROW = 96
D = HEADS * HEAD_DIM

epsilon = 1e-05
branch_scale = 0.7071067811865476
masked_value = -1e30
score_scale = HEAD_DIM ** (-0.5)
log2e = math.log2(math.e)
gelu_in = math.sqrt(2 / math.pi)
gelu_cube = gelu_in * 0.044715
f32 = jnp.float32
bf16 = jnp.bfloat16


def dot(left, right, left_dim=1, right_dim=0):
    return lax.dot_general(
        left, right, (((left_dim,), (right_dim,)), ((), ())), preferred_element_type=f32
    )


def normalise(inputs):
    average = jnp.mean(inputs, -1, keepdims=True)
    centred = inputs - average
    spread = jnp.mean(centred * centred, -1, keepdims=True)
    factor = lax.rsqrt(spread + epsilon)
    return centred * factor, factor


def norm_back(grad, normed, factor, gain):
    e = grad * gain
    first = jnp.mean(e, -1, keepdims=True)
    second = jnp.mean(e * normed, -1, keepdims=True)
    return factor * (e - first - normed * second)


def fold_rows(values):
    count = values.shape[0] // 8
    return jnp.sum(values.reshape(count, 8, values.shape[1]), 0)


class Sums:
    def __init__(self, mesh_sizes, refs):
        (self.partial, self.c_out, self.c_in, self.i_out, self.i_in, self.z_out, self.z_in,
         self.full, self.send, self.recv) = refs
        self.n_items, self.n_z = mesh_sizes
        self.item = lax.axis_index("items")
        seq = lax.axis_index("seq")
        self.core = lax.rem(seq, 2)
        self.z = seq // 2

    def partner(self, kind, step):
        if kind == "core":
            return {"items": self.item, "seq": self.z * 2 + 1 - self.core}
        if kind == "items":
            return {"items": lax.rem(self.item + step, self.n_items), "seq": self.z * 2 + self.core}
        return {"items": self.item, "seq": lax.rem(self.z + step, self.n_z) * 2 + self.core}

    def steps_of(self, kind):
        return range(1, {"core": 2, "items": self.n_items, "z": self.n_z}[kind])

    def copies(self, part, phase, kind, source, target):
        result = []
        base = {"core": 0, "items": 1, "z": self.n_items}[kind]
        for step in self.steps_of(kind):
            slot = (part * 2 + phase, base + step - 1)
            result.append(
                pltpu.make_async_remote_copy(
                    src_ref=source(step),
                    dst_ref=target(step),
                    send_sem=self.send.at[slot],
                    recv_sem=self.recv.at[slot],
                    device_id=self.partner(kind, step),
                    device_id_type=pl.DeviceIdType.MESH,
                )
            )
        return result

    def start(self, copies):
        for copy in copies:
            copy.start()

    def finish(self, copies):
        for copy in copies:
            copy.wait_recv()
        for copy in copies:
            copy.wait_send()

    def place(self, first, rows):
        half = rows // 2
        quarter = half // self.n_items
        split = quarter % (16 * self.n_z) == 0
        last = quarter // self.n_z if split else quarter
        return half, quarter, split, last

    def first_copies(self, part, first, rows):
        half, _, _, _ = self.place(first, rows)
        here = pl.ds(first // 2, half)
        return self.copies(part, 0, "core", lambda s: self.c_out.at[here], lambda s: self.c_in.at[here])

    def items_copies(self, part, first, rows):
        half, quarter, _, _ = self.place(first, rows)

        def source(step):
            to = lax.rem(self.item + step, self.n_items)
            return self.i_out.at[pl.ds(pl.multiple_of(first // 2 + to * quarter, 16), quarter)]

        at = pl.ds(first // 2 // self.n_items, quarter)
        return self.copies(part, 0, "items", source, lambda s: self.i_in.at[s - 1, at])

    def z_copies(self, part, first, rows):
        half, quarter, split, last = self.place(first, rows)
        base = first // 2 // self.n_items
        if split:
            def source(step):
                to = lax.rem(self.z + step, self.n_z)
                return self.z_out.at[pl.ds(pl.multiple_of(base + to * last, 16), last)]

            at = pl.ds(base // self.n_z, last)
            return self.copies(part, 0, "z", source, lambda s: self.z_in.at[s - 1, at])
        at = pl.ds(base, quarter)
        return self.copies(part, 0, "z", lambda s: self.z_out.at[at], lambda s: self.z_in.at[self.z, at])

    def held(self, first, rows, level):
        half, quarter, split, last = self.place(first, rows)
        at = first + self.core * half
        count = half
        if level > 0:
            at += self.item * quarter
            count = quarter
        if level > 1 and split:
            at += self.z * last
            count = last
        return self.full.at[pl.ds(pl.multiple_of(at, 16), count)]

    def back_copies(self, part, first, rows, kind):
        level = {"core": 0, "items": 1, "z": 2}[kind]
        ref = self.held(first, rows, level)
        return self.copies(part, 1, kind, lambda s: ref, lambda s: ref)

    def step(self, part, first, rows, number):
        half, quarter, split, last = self.place(first, rows)
        base_c = first // 2
        base_i = base_c // self.n_items
        if number == 0:
            away = pl.ds(pl.multiple_of(first + (1 - self.core) * half, 16), half)
            self.c_out[pl.ds(base_c, half)] = self.partial[away].astype(bf16)
            self.start(self.first_copies(part, first, rows))
        if number == 1:
            self.finish(self.first_copies(part, first, rows))
            here = pl.ds(base_c, half)
            own = pl.ds(pl.multiple_of(first + self.core * half, 16), half)
            self.i_out[here] = (self.partial[own] + self.c_in[here].astype(f32)).astype(bf16)
            self.start(self.items_copies(part, first, rows))
        if number == 2:
            self.finish(self.items_copies(part, first, rows))
            own = pl.ds(pl.multiple_of(base_c + self.item * quarter, 16), quarter)
            at = pl.ds(base_i, quarter)
            value = self.i_out[own].astype(f32)
            for step in self.steps_of("items"):
                value += self.i_in[step - 1, at].astype(f32)
            self.z_out[at] = value.astype(bf16)
            if not split:
                self.z_in[self.z, at] = value.astype(bf16)
            self.start(self.z_copies(part, first, rows))
        if number == 3:
            self.finish(self.z_copies(part, first, rows))
            if split:
                own = pl.ds(pl.multiple_of(base_i + self.z * last, 16), last)
                at = pl.ds(base_i // self.n_z, last)
                value = self.z_out[own].astype(f32)
                for step in self.steps_of("z"):
                    value += self.z_in[step - 1, at].astype(f32)
            else:
                at = pl.ds(base_i, quarter)
                value = self.z_in[0, at].astype(f32)
                for step in self.steps_of("z"):
                    value += self.z_in[step, at].astype(f32)
            self.held(first, rows, 2)[...] = value.astype(bf16)
            if split:
                self.start(self.back_copies(part, first, rows, "z"))
            else:
                self.start(self.back_copies(part, first, rows, "items"))
        if number == 4 and split:
            self.finish(self.back_copies(part, first, rows, "z"))
            self.start(self.back_copies(part, first, rows, "items"))
        if number == 5:
            self.finish(self.back_copies(part, first, rows, "items"))
            self.start(self.back_copies(part, first, rows, "core"))
        if number == 6:
            self.finish(self.back_copies(part, first, rows, "core"))


def layer_kernel(
    items,
    rows,
    mesh_sizes,
    seq_size,
    lengths_ref,
    pad_ref,
    tokens_ref,
    cot_hbm,
    wqkv_hbm,
    wout_hbm,
    wup_hbm,
    wdown_hbm,
    gain_attn_ref,
    shift_attn_ref,
    gain_ffn_ref,
    shift_ffn_ref,
    output_ref,
    gtok_ref,
    grads_ref,
    gvec_ref,
    x,
    cot,
    alive,
    keys,
    wqkv,
    wout,
    wup,
    wdown,
    h1,
    n1,
    r1,
    proj,
    exps,
    inv,
    att,
    middle,
    n2,
    r2,
    h2,
    dbr,
    hid,
    dpre,
    dmid,
    datt,
    dproj,
    ghalo,
    ghalo_in,
    out,
    gvec,
    vec_buf,
    partial,
    c_out,
    c_in,
    i_out,
    i_in,
    z_out,
    z_in,
    full,
    load_sems,
    store_sems,
    halo_sems,
    vec_sems,
    send_sems,
    recv_sems,
):
    block = rows * ROW
    total = items * block
    steps = 3
    size = total // steps
    gain_attn = gain_attn_ref[...]
    shift_attn = shift_attn_ref[...]
    gain_ffn = gain_ffn_ref[...]
    shift_ffn = shift_ffn_ref[...]
    ff = wup.shape[1]
    chunks = ff // D
    n_items, n_z = mesh_sizes
    item = lax.axis_index("items")
    seq = lax.axis_index("seq")
    MESH = pl.DeviceIdType.MESH
    sums = Sums(
        mesh_sizes, (partial, c_out, c_in, i_out, i_in, z_out, z_in, full, send_sems, recv_sems)
    )
    parts = [(c * 2 * D, 2 * D) for c in range(chunks)] + [(chunks * 2 * D, 4 * D)]

    def step(part, number):
        sums.step(part, *parts[part], number)

    after = {"items": item, "seq": lax.rem(seq + 1, seq_size)}
    ahead = {"items": item, "seq": lax.rem(seq + seq_size - 1, seq_size)}
    barrier = pltpu.get_barrier_semaphore()
    greeted = [after, ahead]
    for kind in ("core", "items", "z"):
        greeted += [sums.partner(kind, s) for s in sums.steps_of(kind)]
    for device in greeted:
        pl.semaphore_signal(barrier, inc=1, device_id=device, device_id_type=MESH)

    loads = [
        (wqkv_hbm, wqkv),
        (wout_hbm, wout),
        (wup_hbm, wup),
        (wdown_hbm, wdown),
        (cot_hbm, cot),
    ]
    token_loads = [
        pltpu.make_async_copy(tokens_ref.at[i], x.at[i, pl.ds(ROW, block)], load_sems.at[5 + i])
        for i in range(items)
    ]
    weight_loads = [
        pltpu.make_async_copy(source, target, load_sems.at[k])
        for k, (source, target) in enumerate(loads)
    ]
    weight_loads[0].start()
    for copy in token_loads:
        copy.start()
    for copy in weight_loads[1:]:
        copy.start()

    pl.semaphore_wait(barrier, len(greeted))
    halo_copy = pltpu.make_async_remote_copy(
        src_ref=tokens_ref.at[:, pl.ds(block - ROW, ROW)],
        dst_ref=x.at[:, pl.ds(0, ROW)],
        send_sem=halo_sems.at[0],
        recv_sem=halo_sems.at[1],
        device_id=after,
        device_id_type=MESH,
    )
    halo_copy.start()

    first_pos = seq * block

    def window(start, width):
        spots = sorted({(s * block + (start if s else 0)) % 128 for s in range(seq_size)})
        if start:
            spots = sorted({(s * block + start) % 128 for s in range(1, seq_size)})
        at = jnp.maximum(first_pos + start, 0)
        low = pl.multiple_of(at // 128 * 128, 128)
        wide = (spots[-1] + width + 127) // 128 * 128
        held = pad_ref[:, pl.ds(low, wide)]
        result = held[:, spots[0] : spots[0] + width]
        for spot in spots[1:]:
            result = jnp.where(at % 128 == spot, held[:, spot : spot + width], result)
        return result

    count = jnp.zeros((items, 1), jnp.int32)
    which = lax.broadcasted_iota(jnp.int32, (items, 1), 0)
    for i in range(items):
        count = jnp.where(which == i, lengths_ref[i], count)

    def there(start, width):
        position = first_pos + start + lax.broadcasted_iota(jnp.int32, (items, width), 1)
        good = (position >= 0) & (position < count) & (window(start, width) == 1)
        return jnp.where(good, 1.0, 0.0)

    row_there = [there((r - 1) * ROW, ROW) for r in range(rows + 1)]
    spread = lax.broadcasted_iota(jnp.int32, (items, items * 128), 1) // 128
    spread = jnp.where(spread == lax.broadcasted_iota(jnp.int32, (items, items * 128), 0), 1.0, 0.0)
    for r in range(rows):
        both = jnp.concatenate([row_there[r], row_there[r + 1]], 1)
        keys[r, :items, : 2 * ROW] = (1.0 - both) * masked_value
        column = dot(row_there[r + 1].astype(bf16), spread.astype(bf16), 0, 0)
        for i in range(items):
            alive[i, r * ROW : (r + 1) * ROW] = column[:, i * 128 : (i + 1) * 128]

    def alive_of(i):
        mask = alive[i]
        return jnp.concatenate([mask, mask], 1)

    def first_norm(values, i, at, count):
        normed, factor = normalise(values)
        low = (normed * gain_attn + shift_attn).astype(bf16)
        h1[i, at : at + count] = low
        n1[i, at : at + count] = normed.astype(bf16)
        r1[i, at : at + count] = jnp.broadcast_to(factor, (count, 128))
        return low

    weight_loads[0].wait()

    def project(i, _):
        pltpu.make_async_copy(
            tokens_ref.at[i], x.at[i, pl.ds(ROW, block)], load_sems.at[5 + i]
        ).wait()
        low = first_norm(x[i, ROW:].astype(f32), i, ROW, block)
        proj[i, ROW:] = dot(low, wqkv[...]).astype(bf16)
        return _

    lax.fori_loop(0, items, project, 0)
    halo_copy.wait()

    def project_halo(i, _):
        low = first_norm(x[i, :ROW].astype(f32), i, 0, ROW)
        proj[i, :ROW, D:] = dot(low, wqkv[:, D:]).astype(bf16)
        return _

    lax.fori_loop(0, items, project_halo, 0)

    query_pos = lax.broadcasted_iota(jnp.int32, (ROW, 2 * ROW), 0)
    key_pos = lax.broadcasted_iota(jnp.int32, (ROW, 2 * ROW), 1) - ROW
    causal = jnp.where(key_pos <= query_pos, 0.0, masked_value)
    itself = jnp.where(key_pos == query_pos, 0.0, masked_value)
    for copy in weight_loads[1:]:
        copy.wait()

    def attend(i, _):
        for r in range(rows):
            bias = jnp.maximum(jnp.minimum(causal, keys[r, pl.ds(i, 1), : 2 * ROW]), itself)
            for h in range(HEADS):
                at = h * HEAD_DIM
                q = proj[i, (r + 1) * ROW : (r + 2) * ROW, at : at + HEAD_DIM]
                k = proj[i, r * ROW : (r + 2) * ROW, D + at : D + at + HEAD_DIM]
                v = proj[i, r * ROW : (r + 2) * ROW, 2 * D + at : 2 * D + at + HEAD_DIM]
                scores = dot(q, k, 1, 1) * (score_scale * log2e) + bias
                top = jnp.max(scores, -1, keepdims=True)
                e = jnp.exp2(scores - top)
                share = 1.0 / jnp.sum(e, -1, keepdims=True)
                low = e.astype(bf16)
                exps[i, r * HEADS + h, :, : 2 * ROW] = low
                share = jnp.broadcast_to(share, (ROW, HEAD_DIM))
                inv[i, r * ROW : (r + 1) * ROW, at : at + HEAD_DIM] = share
                att[i, r * ROW : (r + 1) * ROW, at : at + HEAD_DIM] = (dot(low, v) * share).astype(bf16)
        mid = x[i, ROW:].astype(f32) + branch_scale * dot(att[i], wout[...])
        middle[i] = mid
        normed, factor = normalise(mid)
        n2[i] = normed.astype(bf16)
        r2[i] = jnp.broadcast_to(factor, (block, 128))
        here = pl.ds(pl.multiple_of(i * block, 64), block)
        h2[here] = (normed * gain_ffn + shift_ffn).astype(bf16)
        dbr[here] = (branch_scale * (alive_of(i) * cot[i].astype(f32))).astype(bf16)
        return _

    lax.fori_loop(0, items, attend, 0)

    partial[...] = jnp.zeros_like(partial)
    for c in range(chunks):
        cols = slice(c * D, (c + 1) * D)
        down = slice(c * 2 * D, c * 2 * D + D)
        up = slice(c * 2 * D + D, (c + 1) * 2 * D)

        def feed(t, _):
            here = pl.ds(pl.multiple_of(t * size, 128), size)
            u = dot(h2[here], wup[:, cols])
            back = dot(dbr[here], wdown[cols], 1, 1)
            square = u * u
            s = 0.5 * jnp.tanh(u * (gelu_in + gelu_cube * square)) + 0.5
            hidden = (u * s).astype(bf16)
            slope = s + u * ((s - s * s) * (2 * gelu_in + 6 * gelu_cube * square))
            before = (back * slope).astype(bf16)
            hid[here, cols] = hidden
            dpre[here, cols] = before
            partial[down] += dot(hidden, dbr[here], 0, 0)
            partial[up] += dot(h2[here], before, 0, 0)
            return _

        lax.fori_loop(0, steps, feed, 0)
        step(c, 0)
        if c >= 1:
            step(c - 1, 1)
        if c >= 2:
            step(c - 2, 2)
        if c >= 3:
            step(c - 3, 3)

    gvec[...] = jnp.zeros_like(gvec)
    last = parts[-1][0]

    def at_step(i, when, tasks):
        @pl.when(i == when)
        def _():
            for part, number in tasks:
                step(part, number)

    def middle_back(i, _):
        at_step(i, 2, [(3, 1), (2, 2), (1, 3), (0, 4)])
        at_step(i, 5, [(3, 2), (2, 3), (1, 4), (0, 5)])
        here = pl.ds(pl.multiple_of(i * block, 64), block)
        grad = dot(dpre[here], wup[...], 1, 1)
        normed = n2[i].astype(f32)
        gvec[16:24] += fold_rows(grad * normed)
        gvec[24:32] += fold_rows(grad)
        factor = jnp.concatenate([r2[i]] * 2, 1)
        grad = alive_of(i) * cot[i].astype(f32) + norm_back(grad, normed, factor, gain_ffn)
        dmid[i] = grad
        low = (branch_scale * grad).astype(bf16)
        partial[last + 3 * D :] += dot(att[i], low, 0, 0)
        datt[i] = dot(low, wout[...], 1, 1).astype(bf16)
        return _

    lax.fori_loop(0, items, middle_back, 0)

    def attend_back(i, _):
        at_step(i, 1, [(3, 3), (2, 4), (1, 5), (0, 6)])
        at_step(i, 3, [(3, 4), (2, 5), (1, 6)])
        at_step(i, 5, [(3, 5), (2, 6)])
        for h in range(HEADS):
            at = h * HEAD_DIM
            held_k = None
            held_v = None
            for r in range(rows):
                q = proj[i, (r + 1) * ROW : (r + 2) * ROW, at : at + HEAD_DIM]
                k = proj[i, r * ROW : (r + 2) * ROW, D + at : D + at + HEAD_DIM]
                v = proj[i, r * ROW : (r + 2) * ROW, 2 * D + at : 2 * D + at + HEAD_DIM]
                own = slice(r * ROW, (r + 1) * ROW)
                grad = datt[i, own, at : at + HEAD_DIM].astype(f32) * inv[i, own, at : at + HEAD_DIM]
                low = grad.astype(bf16)
                row_dot = jnp.sum(grad * att[i, own, at : at + HEAD_DIM].astype(f32), -1, keepdims=True)
                e = exps[i, r * HEADS + h, :, : 2 * ROW]
                ds = (e.astype(f32) * ((dot(low, v, 1, 1) - row_dot) * score_scale)).astype(bf16)
                dv = dot(e, low, 0, 0)
                dk = dot(ds, q, 0, 0)
                dproj[i, (r + 1) * ROW : (r + 2) * ROW, at : at + HEAD_DIM] = dot(ds, k).astype(bf16)
                first_k, first_v = dk[:ROW], dv[:ROW]
                if held_k is not None:
                    first_k += held_k
                    first_v += held_v
                dproj[i, r * ROW : (r + 1) * ROW, D + at : D + at + HEAD_DIM] = first_k.astype(bf16)
                dproj[i, r * ROW : (r + 1) * ROW, 2 * D + at : 2 * D + at + HEAD_DIM] = first_v.astype(bf16)
                held_k, held_v = dk[ROW:], dv[ROW:]
            dproj[i, rows * ROW :, D + at : D + at + HEAD_DIM] = held_k.astype(bf16)
            dproj[i, rows * ROW :, 2 * D + at : 2 * D + at + HEAD_DIM] = held_v.astype(bf16)
        dproj[i, :ROW, :D] = jnp.zeros((ROW, D), bf16)
        return _

    lax.fori_loop(0, items, attend_back, 0)

    def weight_back(i, _):
        for p in range(3):
            partial[last + p * D : last + (p + 1) * D] += dot(
                h1[i], dproj[i, :, p * D : (p + 1) * D], 0, 0
            )
        return _

    lax.fori_loop(0, items, weight_back, 0)
    step(4, 0)
    step(3, 6)

    def tokens_back(i, _):
        at_step(i, 2, [(4, 1)])
        grad = dot(dproj[i], wqkv[...], 1, 1)
        normed = n1[i].astype(f32)
        gvec[0:8] += fold_rows(grad * normed)
        gvec[8:16] += fold_rows(grad)
        factor = jnp.concatenate([r1[i]] * 2, 1)
        grad = norm_back(grad, normed, factor, gain_attn)
        ghalo[i] = grad[:ROW].astype(bf16)
        dmid[i] += grad[ROW:]
        return _

    lax.fori_loop(0, items, tokens_back, 0)
    ghalo_copy = pltpu.make_async_remote_copy(
        src_ref=ghalo,
        dst_ref=ghalo_in,
        send_sem=halo_sems.at[2],
        recv_sem=halo_sems.at[3],
        device_id=ahead,
        device_id_type=MESH,
    )
    ghalo_copy.start()

    def vec_copies(kind, number):
        result = []
        place = {"core": sums.core, "items": item, "z": sums.z}[kind]
        base = {"core": 0, "items": 1, "z": n_items}[kind]
        for s in sums.steps_of(kind):
            here = vec_buf.at[number, place]
            result.append(
                pltpu.make_async_remote_copy(
                    src_ref=here,
                    dst_ref=here,
                    send_sem=vec_sems.at[0, base + s - 1],
                    recv_sem=vec_sems.at[1, base + s - 1],
                    device_id=sums.partner(kind, s),
                    device_id_type=MESH,
                )
            )
        return result

    def vec_total(number, size):
        value = vec_buf[number, 0]
        for k in range(1, size):
            value += vec_buf[number, k]
        return value

    lines = [jnp.sum(gvec[8 * k : 8 * k + 8], 0, keepdims=True) for k in range(4)]
    vec_buf[0, sums.core] = jnp.concatenate(lines + [jnp.zeros((4, D), f32)], 0)
    sums.start(vec_copies("core", 0))

    def vec_step(number):
        if number == 1:
            sums.finish(vec_copies("core", 0))
            vec_buf[1, item] = vec_total(0, 2)
            sums.start(vec_copies("items", 1))
        if number == 2:
            sums.finish(vec_copies("items", 1))
            vec_buf[2, sums.z] = vec_total(1, n_items)
            sums.start(vec_copies("z", 2))
        if number == 3:
            sums.finish(vec_copies("z", 2))
            gvec[0:8] = vec_total(2, n_z)

    def finish(i, _):
        at_step(i, 1, [(4, 2)])
        here = pl.ds(pl.multiple_of(i * block, 64), block)
        branch = dot(hid[here], wdown[...])
        out[i] = (alive_of(i) * (middle[i] + branch_scale * branch)).astype(bf16)
        return _

    lax.fori_loop(0, items, finish, 0)
    out_copy = pltpu.make_async_copy(out, output_ref, store_sems.at[0])
    out_copy.start()
    vec_step(1)
    step(4, 3)
    ghalo_copy.wait()
    for i in range(items):
        dmid[i, block - ROW :] += ghalo_in[i].astype(f32)
    tok_copy = pltpu.make_async_copy(dmid, gtok_ref, store_sems.at[1])
    tok_copy.start()
    vec_step(2)
    step(4, 4)
    step(4, 5)
    vec_step(3)
    vec_copy = pltpu.make_async_copy(gvec.at[pl.ds(0, 8)], gvec_ref, store_sems.at[2])
    vec_copy.start()
    step(4, 6)
    grad_copy = pltpu.make_async_copy(full, grads_ref, store_sems.at[3])
    grad_copy.start()
    out_copy.wait()
    tok_copy.wait()
    vec_copy.wait()
    grad_copy.wait()


def split_kernel(
    raw_out,
    raw_tok,
    grads,
    gvec,
    output,
    gtok,
    gqkv,
    gout,
    gup,
    gdown,
    gain_attn,
    shift_attn,
    gain_ffn,
    shift_ffn,
    qkv,
    wout,
    up,
    down,
    sems,
):
    copies = [
        pltpu.make_async_copy(raw_tok, gtok, sems.at[0]),
        pltpu.make_async_copy(raw_out, output, sems.at[1]),
    ]
    for copy in copies:
        copy.start()
    chunks = up.shape[1] // D

    def send(source, target, number):
        copy = pltpu.make_async_copy(source, target, sems.at[number])
        copy.start()
        copies.append(copy)

    for c in range(chunks):
        down[c * D : (c + 1) * D] = grads[c * 2 * D : c * 2 * D + D].astype(f32)
    send(down, gdown, 2)
    for c in range(chunks):
        up[:, c * D : (c + 1) * D] = grads[c * 2 * D + D : (c + 1) * 2 * D].astype(f32)
    send(up, gup, 3)
    last = chunks * 2 * D
    for p in range(3):
        qkv[:, p * D : (p + 1) * D] = grads[last + p * D : last + (p + 1) * D].astype(f32)
    send(qkv, gqkv, 4)
    wout[...] = grads[last + 3 * D :].astype(f32)
    send(wout, gout, 5)
    gain_attn[...] = gvec[0:1]
    shift_attn[...] = gvec[1:2]
    gain_ffn[...] = gvec[2:3]
    shift_ffn[...] = gvec[3:4]
    for copy in copies:
        copy.wait()


def shards(
    seq_size,
    mesh_sizes,
    tokens,
    lengths,
    pad_mask,
    w_qkv,
    w_out,
    w_up,
    w_down,
    gain_attn,
    shift_attn,
    gain_ffn,
    shift_ffn,
    cotangent,
):
    items, block, width = tokens.shape
    rows = block // ROW
    total = items * block
    ff = w_up.shape[1]
    ext = block + ROW
    n_items, n_z = mesh_sizes
    grad_rows = 2 * ff + 4 * width
    half = grad_rows // 2
    links = n_items + n_z - 1
    vmem = pl.BlockSpec(memory_space=pltpu.VMEM)
    anywhere = pl.BlockSpec(memory_space=pl.ANY)
    raw = [
        jax.ShapeDtypeStruct((items, block, width), bf16),
        jax.ShapeDtypeStruct((items, block, width), f32),
        jax.ShapeDtypeStruct((grad_rows, width), bf16),
        jax.ShapeDtypeStruct((8, width), f32),
    ]
    vectors = [v.reshape(1, width) for v in (gain_attn, shift_attn, gain_ffn, shift_ffn)]
    parts = ff // width + 1
    vm = pltpu.VMEM
    raw = pl.pallas_call(
        functools.partial(layer_kernel, items, rows, mesh_sizes, seq_size),
        out_shape=raw,
        in_specs=[pl.BlockSpec(memory_space=pltpu.SMEM), vmem] + [anywhere] * 6 + [vmem] * 4,
        out_specs=[anywhere] * 4,
        scratch_shapes=[
            vm((items, ext, width), bf16),
            vm((items, block, width), bf16),
            vm((items, block, 128), f32),
            vm((rows, 8, 256), f32),
            vm((width, 3 * width), bf16),
            vm((width, width), bf16),
            vm((width, ff), bf16),
            vm((ff, width), bf16),
            vm((items, ext, width), bf16),
            vm((items, ext, width), bf16),
            vm((items, ext, 128), f32),
            vm((items, ext, 3 * width), bf16),
            vm((items, rows * HEADS, ROW, 256), bf16),
            vm((items, block, width), f32),
            vm((items, block, width), bf16),
            vm((items, block, width), f32),
            vm((items, block, width), bf16),
            vm((items, block, 128), f32),
            vm((total, width), bf16),
            vm((total, width), bf16),
            vm((total, ff), bf16),
            vm((total, ff), bf16),
            vm((items, block, width), f32),
            vm((items, block, width), bf16),
            vm((items, ext, 3 * width), bf16),
            vm((items, ROW, width), bf16),
            vm((items, ROW, width), bf16),
            vm((items, block, width), bf16),
            vm((32, width), f32),
            vm((3, max(n_items, n_z), 8, width), f32),
            vm((grad_rows, width), f32),
            vm((half, width), bf16),
            vm((half, width), bf16),
            vm((half, width), bf16),
            vm((n_items - 1, half // n_items, width), bf16),
            vm((half // n_items, width), bf16),
            vm((n_z, half // n_items, width), bf16),
            vm((grad_rows, width), bf16),
            pltpu.SemaphoreType.DMA((5 + items,)),
            pltpu.SemaphoreType.DMA((4,)),
            pltpu.SemaphoreType.DMA((4,)),
            pltpu.SemaphoreType.DMA((2, links)),
            pltpu.SemaphoreType.DMA((2 * parts, links)),
            pltpu.SemaphoreType.DMA((2 * parts, links)),
        ],
        compiler_params=pltpu.CompilerParams(
            vmem_limit_bytes=63 * 2**20, collective_id=0, has_side_effects=True
        ),
    )(lengths, pad_mask, tokens, cotangent, w_qkv, w_out, w_up, w_down, *vectors)
    shapes = [
        jax.ShapeDtypeStruct((items, block, width), bf16),
        jax.ShapeDtypeStruct((items, block, width), f32),
        jax.ShapeDtypeStruct((width, 3 * width), f32),
        jax.ShapeDtypeStruct((width, width), f32),
        jax.ShapeDtypeStruct((width, ff), f32),
        jax.ShapeDtypeStruct((ff, width), f32),
    ] + [jax.ShapeDtypeStruct((1, width), f32)] * 4
    outs = pl.pallas_call(
        split_kernel,
        out_shape=shapes,
        in_specs=[anywhere] * 2 + [vmem] * 2,
        out_specs=[anywhere] * 6 + [vmem] * 4,
        scratch_shapes=[
            vm((width, 3 * width), f32),
            vm((width, width), f32),
            vm((width, ff), f32),
            vm((ff, width), f32),
            pltpu.SemaphoreType.DMA((6,)),
        ],
        compiler_params=pltpu.CompilerParams(vmem_limit_bytes=16 * 2**20),
    )(*raw)
    return tuple(outs[:6]) + tuple(v.reshape(width) for v in outs[6:])


def solution(mesh):
    split = P("items", "seq", None)
    seq_size = mesh.shape["seq"]
    mesh_sizes = (mesh.shape["items"], seq_size // 2)
    return jax.shard_map(
        functools.partial(shards, seq_size, mesh_sizes),
        mesh=mesh,
        in_specs=(split, P("items"), P("items", None)) + (P(),) * 8 + (split,),
        out_specs=(split, split) + (P(),) * 8,
        check_vma=False,
    )
```

time: 233 us -> 97.4 us (0.42)
  waiting for transfers between devices: 94.2 us -> 0 us
  blocking collectives: 45.6 us -> 0 us
  Pallas kernels: 60.7 us -> 91.4 us
  between operations: 14.1 us -> 0.67 us
  other arithmetic: 4.84 us -> 0 us
  local copies, waits for them, and re-layouts: 9.24 us -> 5.03 us
  starting transfers between devices: 3.69 us -> 0 us
    psum x1 -> x0, waiting for transfers between devices: 94.2 us -> none  [shards(): lax.psum((gqkv, gout, gup, gdown.T, gvec), ('items', 'seq'))]
    psum x1 -> x0, blocking collectives: 45.6 us -> none  [shards(): lax.psum((gqkv, gout, gup, gdown.T, gvec), ('items', 'seq'))]
    pallas_call x1 -> x2, Pallas kernels: 60.7 us -> 91.4 us  [the longest x1 88 us: shards(): pl.pallas_call(functools.partial(layer_kernel, items, rows, mesh_sizes, s...]
    ppermute x2 -> x0, starting transfers between devices: 3.65 us -> none  [from_behind(): return lax.ppermute(block, axis, route)]
    unnamed x16 -> x8, local copies, waits for them, and re-layouts: 6.17 us -> 5.03 us
  transfers between devices with their start and end apart: 3 -> 0, of which waited for: 1 -> 0; matrix products, arithmetic and copies ran while one was open for 2% -> 0% of each run, Pallas kernels for 0% -> 0%
where the time goes in v2:
time: 97.4 us; the launch traced here: 97.1 us
  Pallas kernels  91.4 us (94%)
  local copies, waits for them, and re-layouts  5.03 us (5%)
    pallas_call x1, Pallas kernels, shards(): pl.pallas_call(functools.partial(layer_kernel, items, rows, mesh_sizes, s...  88 us
    unnamed x8, local copies, waits for them, and re-layouts  5.03 us
    pallas_call x1, Pallas kernels, shards(): pl.pallas_call(split_kernel, out_shape=shapes, in_specs=[anywhere] * 2 +...  3.39 us

profile of v2, /device:TPU:0, one launch (start us, length us, event | category | flops | bytes accessed | tf_op | source)
XLA Modules:
  0.0 97.1 jit_solution(15506622296570010200)
XLA Ops:
  0.6 88.0 %shard_map.195 = (bf16[6,384,256]{2,1,0:T(8,128)(2,1)}, f32[6,384,256]{2,1,0:T(8,128)}, bf16[3072,256]{1,0:T(8,128)(2,1)}, f32[8,256]{1,0:T(8,128)}) custom-call(s32[6]{0:T(128)} %lengths_ref.1, s32[6,3072]{1,0:T(8,128)} %pad_ref.1, bf16[6,384,256]{2,1,0:T(8,128)(2,1)} %tokens_ref.1, bf16[6,384,256]{2,1,0:T(8,128)(2,1)} %cot_hbm.1, ...), custom_call_target="tpu_custom_call" | custom-call | tf_op jit(solution)/shard_map/pallas_call | solution.py:726
  88.6 0.0 copy-start
  88.7 1.7 %copy-done = f32[6,384,256]{2,1,0:T(8,128)S(1)} copy-done((f32[6,384,256]{2,1,0:T(8,128)S(1)}, f32[6,384,256]{2,1,0:T(8,128)}, u32[]{:S(2)}) %copy-start) | copy-done | bytes 2359320
  90.3 0.0 copy-start.1
  90.3 1.4 %copy-done.1 = bf16[3072,256]{1,0:T(8,128)(2,1)S(1)} copy-done((bf16[3072,256]{1,0:T(8,128)(2,1)S(1)}, bf16[3072,256]{1,0:T(8,128)(2,1)}, u32[]{:S(2)}) %copy-start.1) | copy-done | bytes 1572888
  91.7 0.0 copy-start.2
  91.7 1.3 %copy-done.2 = bf16[6,384,256]{2,1,0:T(8,128)(2,1)S(1)} copy-done((bf16[6,384,256]{2,1,0:T(8,128)(2,1)S(1)}, bf16[6,384,256]{2,1,0:T(8,128)(2,1)}, u32[]{:S(2)}) %copy-start.2) | copy-done | bytes 1179672
  93.0 0.0 copy-start.3
  93.0 0.7 copy-done.3
  93.7 3.4 %shard_map.196 = (bf16[6,384,256]{2,1,0:T(8,128)(2,1)}, f32[6,384,256]{2,1,0:T(8,128)}, f32[256,768]{1,0:T(8,128)}, f32[256,256]{1,0:T(8,128)}, f32[256,1024]{1,...) custom-call(bf16[6,384,256]{2,1,0:T(8,128)(2,1)S(1)} %copy-done.2, ...), custom_call_target="tpu_custom_call" | custom-call | tf_op jit(solution)/shard_map/pallas_call | solution.py:789
Async XLA Ops:
  88.6 1.7 %copy-start = (f32[6,384,256]{2,1,0:T(8,128)S(1)}, f32[6,384,256]{2,1,0:T(8,128)}, u32[]{:S(2)}) copy-start(f32[6,384,256]{2,1,0:T(8,128)} %get-tuple-element.25.raw_tok) | copy-start | bytes 7077892
  90.3 1.4 %copy-start.1 = (bf16[3072,256]{1,0:T(8,128)(2,1)S(1)}, bf16[3072,256]{1,0:T(8,128)(2,1)}, u32[]{:S(2)}) copy-start(bf16[3072,256]{1,0:T(8,128)(2,1)} %get-tuple-element.26.grads) | copy-start | bytes 4718596
  91.7 1.3 %copy-start.2 = (bf16[6,384,256]{2,1,0:T(8,128)(2,1)S(1)}, bf16[6,384,256]{2,1,0:T(8,128)(2,1)}, u32[]{:S(2)}) copy-start(bf16[6,384,256]{2,1,0:T(8,128)(2,1)} %get-tuple-element.24.raw_out) | copy-start | bytes 3538948
  93.0 0.7 copy-start.3

commit v3 on v2

--- a/solution.py
+++ b/solution.py
@@ -53,7 +53,7 @@
 class Sums:
     def __init__(self, mesh_sizes, refs):
         (self.partial, self.c_out, self.c_in, self.i_out, self.i_in, self.z_out, self.z_in,
-         self.full, self.send, self.recv) = refs
+         self.d_in, self.full, self.send, self.recv) = refs
         self.n_items, self.n_z = mesh_sizes
         self.item = lax.axis_index("items")
         seq = lax.axis_index("seq")
@@ -63,16 +63,27 @@
     def partner(self, kind, step):
         if kind == "core":
             return {"items": self.item, "seq": self.z * 2 + 1 - self.core}
-        if kind == "items":
-            return {"items": lax.rem(self.item + step, self.n_items), "seq": self.z * 2 + self.core}
-        return {"items": self.item, "seq": lax.rem(self.z + step, self.n_z) * 2 + self.core}
+        item, z = self.spot(kind, step)
+        return {"items": item, "seq": z * 2 + self.core}
+
+    def spot(self, kind, step):
+        items_step, z_step = {
+            "items": (step, 0),
+            "z": (0, step),
+            "plane": (step // self.n_z, step % self.n_z),
+        }[kind]
+        return (
+            lax.rem(self.item + items_step, self.n_items),
+            lax.rem(self.z + z_step, self.n_z),
+        )
 
     def steps_of(self, kind):
-        return range(1, {"core": 2, "items": self.n_items, "z": self.n_z}[kind])
+        counts = {"core": 2, "items": self.n_items, "z": self.n_z, "plane": self.n_items * self.n_z}
+        return range(1, counts[kind])
 
     def copies(self, part, phase, kind, source, target):
         result = []
-        base = {"core": 0, "items": 1, "z": self.n_items}[kind]
+        base = {"core": 0, "items": 1, "z": self.n_items, "plane": 1}[kind]
         for step in self.steps_of(kind):
             slot = (part * 2 + phase, base + step - 1)
             result.append(
@@ -132,6 +143,17 @@
         at = pl.ds(base, quarter)
         return self.copies(part, 0, "z", lambda s: self.z_out.at[at], lambda s: self.z_in.at[self.z, at])
 
+    def plane_copies(self, part, first, rows):
+        count = rows // 2 // (self.n_items * self.n_z)
+
+        def source(step):
+            item, z = self.spot("plane", step)
+            at = first // 2 + (item * self.n_z + z) * count
+            return self.i_out.at[pl.ds(pl.multiple_of(at, 16), count)]
+
+        at = pl.ds(first // 2 // (self.n_items * self.n_z), count)
+        return self.copies(part, 0, "plane", source, lambda s: self.d_in.at[s - 1, at])
+
     def held(self, first, rows, level):
         half, quarter, split, last = self.place(first, rows)
         at = first + self.core * half
@@ -145,11 +167,32 @@
         return self.full.at[pl.ds(pl.multiple_of(at, 16), count)]
 
     def back_copies(self, part, first, rows, kind):
-        level = {"core": 0, "items": 1, "z": 2}[kind]
+        level = {"core": 0, "items": 1, "z": 2, "plane": 2}[kind]
         ref = self.held(first, rows, level)
         return self.copies(part, 1, kind, lambda s: ref, lambda s: ref)
 
-    def step(self, part, first, rows, number):
+    def plane_step(self, part, first, rows, number):
+        count = rows // 2 // (self.n_items * self.n_z)
+        base = first // 2
+        if number == 2:
+            self.finish(self.plane_copies(part, first, rows))
+            own = base + (self.item * self.n_z + self.z) * count
+            value = self.i_out[pl.ds(pl.multiple_of(own, 16), count)].astype(f32)
+            at = pl.ds(base // (self.n_items * self.n_z), count)
+            for step in self.steps_of("plane"):
+                value += self.d_in[step - 1, at].astype(f32)
+            self.held(first, rows, 2)[...] = value.astype(bf16)
+            self.start(self.back_copies(part, first, rows, "plane"))
+        if number == 3:
+            self.finish(self.back_copies(part, first, rows, "plane"))
+            self.start(self.back_copies(part, first, rows, "core"))
+        if number == 4:
+            self.finish(self.back_copies(part, first, rows, "core"))
+
+    def step(self, part, first, rows, number, plane=False):
+        if plane and number > 1:
+            self.plane_step(part, first, rows, number)
+            return
         half, quarter, split, last = self.place(first, rows)
         base_c = first // 2
         base_i = base_c // self.n_items
@@ -162,7 +205,10 @@
             here = pl.ds(base_c, half)
             own = pl.ds(pl.multiple_of(first + self.core * half, 16), half)
             self.i_out[here] = (self.partial[own] + self.c_in[here].astype(f32)).astype(bf16)
-            self.start(self.items_copies(part, first, rows))
+            if plane:
+                self.start(self.plane_copies(part, first, rows))
+            else:
+                self.start(self.items_copies(part, first, rows))
         if number == 2:
             self.finish(self.items_copies(part, first, rows))
             own = pl.ds(pl.multiple_of(base_c + self.item * quarter, 16), quarter)
@@ -260,6 +306,7 @@
     i_in,
     z_out,
     z_in,
+    d_in,
     full,
     load_sems,
     store_sems,
@@ -270,8 +317,6 @@
 ):
     block = rows * ROW
     total = items * block
-    steps = 3
-    size = total // steps
     gain_attn = gain_attn_ref[...]
     shift_attn = shift_attn_ref[...]
     gain_ffn = gain_ffn_ref[...]
@@ -283,41 +328,51 @@
     seq = lax.axis_index("seq")
     MESH = pl.DeviceIdType.MESH
     sums = Sums(
-        mesh_sizes, (partial, c_out, c_in, i_out, i_in, z_out, z_in, full, send_sems, recv_sems)
+        mesh_sizes, (partial, c_out, c_in, i_out, i_in, z_out, z_in, d_in, full, send_sems, recv_sems)
     )
-    parts = [(c * 2 * D, 2 * D) for c in range(chunks)] + [(chunks * 2 * D, 4 * D)]
+    parts = [(c * 2 * D, 2 * D) for c in range(chunks + HEADS)]
+    direct = D % (16 * n_items * n_z) == 0
 
     def step(part, number):
-        sums.step(part, *parts[part], number)
+        sums.step(part, *parts[part], number, plane=direct and part >= chunks)
 
     after = {"items": item, "seq": lax.rem(seq + 1, seq_size)}
     ahead = {"items": item, "seq": lax.rem(seq + seq_size - 1, seq_size)}
     barrier = pltpu.get_barrier_semaphore()
     greeted = [after, ahead]
-    for kind in ("core", "items", "z"):
+    for kind in ("core", "plane") if direct else ("core", "items", "z"):
         greeted += [sums.partner(kind, s) for s in sums.steps_of(kind)]
     for device in greeted:
         pl.semaphore_signal(barrier, inc=1, device_id=device, device_id_type=MESH)
 
     loads = [
-        (wqkv_hbm, wqkv),
         (wout_hbm, wout),
         (wup_hbm, wup),
         (wdown_hbm, wdown),
         (cot_hbm, cot),
     ]
     token_loads = [
-        pltpu.make_async_copy(tokens_ref.at[i], x.at[i, pl.ds(ROW, block)], load_sems.at[5 + i])
+        pltpu.make_async_copy(tokens_ref.at[i], x.at[i, pl.ds(ROW, block)], load_sems.at[4 + i])
         for i in range(items)
     ]
     weight_loads = [
         pltpu.make_async_copy(source, target, load_sems.at[k])
         for k, (source, target) in enumerate(loads)
     ]
-    weight_loads[0].start()
+    qkv_loads = [
+        pltpu.make_async_copy(
+            wqkv_hbm.at[:, pl.ds(p * D + h * HEAD_DIM, HEAD_DIM)],
+            wqkv.at[:, pl.ds((h * 3 + p) * HEAD_DIM, HEAD_DIM)],
+            load_sems.at[4 + items + h * 3 + p],
+        )
+        for h in range(HEADS)
+        for p in range(3)
+    ]
+    for copy in qkv_loads:
+        copy.start()
     for copy in token_loads:
         copy.start()
-    for copy in weight_loads[1:]:
+    for copy in weight_loads:
         copy.start()
 
     pl.semaphore_wait(barrier, len(greeted))
@@ -370,102 +425,166 @@
         mask = alive[i]
         return jnp.concatenate([mask, mask], 1)
 
-    def first_norm(values, i, at, count):
+    def first_norm(values):
         normed, factor = normalise(values)
-        low = (normed * gain_attn + shift_attn).astype(bf16)
-        h1[i, at : at + count] = low
-        n1[i, at : at + count] = normed.astype(bf16)
-        r1[i, at : at + count] = jnp.broadcast_to(factor, (count, 128))
-        return low
-
-    weight_loads[0].wait()
-
-    def project(i, _):
-        pltpu.make_async_copy(
-            tokens_ref.at[i], x.at[i, pl.ds(ROW, block)], load_sems.at[5 + i]
-        ).wait()
-        low = first_norm(x[i, ROW:].astype(f32), i, ROW, block)
-        proj[i, ROW:] = dot(low, wqkv[...]).astype(bf16)
+        return (normed * gain_attn + shift_attn).astype(bf16), normed.astype(bf16), factor
+
+    for copy in qkv_loads:
+        copy.wait()
+    pair = 2 if items % 2 == 0 else 1
+
+    def project(p, _):
+        for j in range(pair):
+            pltpu.make_async_copy(
+                tokens_ref.at[p * pair + j],
+                x.at[p * pair + j, pl.ds(ROW, block)],
+                load_sems.at[4 + p * pair + j],
+            ).wait()
+        found = [first_norm(x[p * pair + j, ROW:].astype(f32)) for j in range(pair)]
+        results = [dot(low, wqkv[...]).astype(bf16) for low, _, _ in found]
+        for j in range(pair):
+            low, normed, factor = found[j]
+            h1[p * pair + j, ROW:] = low
+            n1[p * pair + j, ROW:] = normed
+            r1[p * pair + j, ROW:] = jnp.broadcast_to(factor, (block, 128))
+            proj[p * pair + j, ROW:] = results[j]
         return _
 
-    lax.fori_loop(0, items, project, 0)
-    halo_copy.wait()
-
-    def project_halo(i, _):
-        low = first_norm(x[i, :ROW].astype(f32), i, 0, ROW)
-        proj[i, :ROW, D:] = dot(low, wqkv[:, D:]).astype(bf16)
-        return _
-
-    lax.fori_loop(0, items, project_halo, 0)
-
+    lax.fori_loop(0, items // pair, project, 0)
     query_pos = lax.broadcasted_iota(jnp.int32, (ROW, 2 * ROW), 0)
     key_pos = lax.broadcasted_iota(jnp.int32, (ROW, 2 * ROW), 1) - ROW
     causal = jnp.where(key_pos <= query_pos, 0.0, masked_value)
     itself = jnp.where(key_pos == query_pos, 0.0, masked_value)
-    for copy in weight_loads[1:]:
+    for copy in weight_loads:
         copy.wait()
 
-    def attend(i, _):
-        for r in range(rows):
-            bias = jnp.maximum(jnp.minimum(causal, keys[r, pl.ds(i, 1), : 2 * ROW]), itself)
+    def part_of(whole, r, count, number, h):
+        at = (h * 3 + number) * HEAD_DIM
+        return whole[r * ROW : (r + count) * ROW, at : at + HEAD_DIM]
+
+    def weigh(mine, keys_of, units):
+        biases = {r: jnp.maximum(jnp.minimum(causal, keys_of(r)), itself) for r, _ in units}
+        scores = [
+            dot(part_of(mine, r + 1, 1, 0, h), part_of(mine, r, 2, 1, h), 1, 1)
+            * (score_scale * log2e)
+            + biases[r]
+            for r, h in units
+        ]
+        es = [jnp.exp2(one - jnp.max(one, -1, keepdims=True)) for one in scores]
+        shares = [
+            jnp.broadcast_to(1.0 / jnp.sum(e, -1, keepdims=True), (ROW, HEAD_DIM)) for e in es
+        ]
+        lows = [e.astype(bf16) for e in es]
+        results = [
+            (dot(e, part_of(mine, r, 2, 2, h)) * share).astype(bf16)
+            for e, share, (r, h) in zip(lows, shares, units)
+        ]
+        return lows, shares, results
+
+    def heads(values):
+        return jnp.concatenate(values, 1)
+
+    def attend(p, _):
+        units = [(r, h) for r in range(1, rows) for h in range(HEADS)]
+        found = []
+        for j in range(pair):
+            i = p * pair + j
+            found.append(weigh(proj[i], lambda r: keys[r, pl.ds(i, 1), : 2 * ROW], units))
+        for j in range(pair):
+            i = p * pair + j
+            lows, shares, results = found[j]
+            for (r, h), e in zip(units, lows):
+                exps[i, r * HEADS + h, :, : 2 * ROW] = e
+            for r in range(1, rows):
+                at = (r - 1) * HEADS
+                inv[i, r * ROW : (r + 1) * ROW] = heads(shares[at : at + HEADS])
+                att[i, r * ROW : (r + 1) * ROW] = heads(results[at : at + HEADS])
+        return _
+
+    if rows > 1:
+        lax.fori_loop(0, items // pair, attend, 0)
+    halo_copy.wait()
+
+    def project_halo(p, _):
+        low, normed, factor = first_norm(x[:, :ROW].astype(f32).reshape(items * ROW, D))
+        results = [
+            dot(low, wqkv[:, (h * 3 + 1) * HEAD_DIM : (h * 3 + 3) * HEAD_DIM]).astype(bf16)
+            for h in range(HEADS)
+        ]
+        h1[:, :ROW] = low.reshape(items, ROW, D)
+        n1[:, :ROW] = normed.reshape(items, ROW, D)
+        r1[:, :ROW] = jnp.broadcast_to(factor, (items * ROW, 128)).reshape(items, ROW, 128)
+        for h in range(HEADS):
+            at = (h * 3 + 1) * HEAD_DIM
+            proj[:, :ROW, at : at + 2 * HEAD_DIM] = results[h].reshape(items, ROW, 2 * HEAD_DIM)
+        return _
+
+    lax.fori_loop(0, 1, project_halo, 0)
+
+    def attend_first(p, _):
+        units = [(0, h) for h in range(HEADS)]
+        found = []
+        for j in range(pair):
+            i = p * pair + j
+            others = att[i, ROW:]
+            inputs = x[i, ROW:].astype(f32)
+            grad = (branch_scale * (alive_of(i) * cot[i].astype(f32))).astype(bf16)
+            lows, shares, results = weigh(
+                proj[i, : 2 * ROW], lambda r: keys[r, pl.ds(i, 1), : 2 * ROW], units
+            )
+            result = heads(results)
+            whole = jnp.concatenate([result, others], 0) if rows > 1 else result
+            mid = inputs + branch_scale * dot(whole, wout[...])
+            normed, factor = normalise(mid)
+            low = (normed * gain_ffn + shift_ffn).astype(bf16)
+            found.append((lows, shares, result, mid, normed.astype(bf16), factor, low, grad))
+        for j in range(pair):
+            i = p * pair + j
+            lows, shares, result, mid, normed, factor, low, grad = found[j]
+            here = pl.ds(pl.multiple_of(i * block, 64), block)
             for h in range(HEADS):
-                at = h * HEAD_DIM
-                q = proj[i, (r + 1) * ROW : (r + 2) * ROW, at : at + HEAD_DIM]
-                k = proj[i, r * ROW : (r + 2) * ROW, D + at : D + at + HEAD_DIM]
-                v = proj[i, r * ROW : (r + 2) * ROW, 2 * D + at : 2 * D + at + HEAD_DIM]
-                scores = dot(q, k, 1, 1) * (score_scale * log2e) + bias
-                top = jnp.max(scores, -1, keepdims=True)
-                e = jnp.exp2(scores - top)
-                share = 1.0 / jnp.sum(e, -1, keepdims=True)
-                low = e.astype(bf16)
-                exps[i, r * HEADS + h, :, : 2 * ROW] = low
-                share = jnp.broadcast_to(share, (ROW, HEAD_DIM))
-                inv[i, r * ROW : (r + 1) * ROW, at : at + HEAD_DIM] = share
-                att[i, r * ROW : (r + 1) * ROW, at : at + HEAD_DIM] = (dot(low, v) * share).astype(bf16)
-        mid = x[i, ROW:].astype(f32) + branch_scale * dot(att[i], wout[...])
-        middle[i] = mid
-        normed, factor = normalise(mid)
-        n2[i] = normed.astype(bf16)
-        r2[i] = jnp.broadcast_to(factor, (block, 128))
-        here = pl.ds(pl.multiple_of(i * block, 64), block)
-        h2[here] = (normed * gain_ffn + shift_ffn).astype(bf16)
-        dbr[here] = (branch_scale * (alive_of(i) * cot[i].astype(f32))).astype(bf16)
+                exps[i, h, :, : 2 * ROW] = lows[h]
+            inv[i, :ROW] = heads(shares)
+            att[i, :ROW] = result
+            middle[i] = mid
+            n2[i] = normed
+            r2[i] = jnp.broadcast_to(factor, (block, 128))
+            h2[here] = low
+            dbr[here] = grad
         return _
 
-    lax.fori_loop(0, items, attend, 0)
-
-    partial[...] = jnp.zeros_like(partial)
+    lax.fori_loop(0, items // pair, attend_first, 0)
+
     for c in range(chunks):
         cols = slice(c * D, (c + 1) * D)
         down = slice(c * 2 * D, c * 2 * D + D)
         up = slice(c * 2 * D + D, (c + 1) * 2 * D)
 
         def feed(t, _):
-            here = pl.ds(pl.multiple_of(t * size, 128), size)
-            u = dot(h2[here], wup[:, cols])
-            back = dot(dbr[here], wdown[cols], 1, 1)
+            normed = h2[...]
+            grad = dbr[...]
+            u = dot(normed, wup[:, cols])
+            back = dot(grad, wdown[cols], 1, 1)
             square = u * u
             s = 0.5 * jnp.tanh(u * (gelu_in + gelu_cube * square)) + 0.5
             hidden = (u * s).astype(bf16)
             slope = s + u * ((s - s * s) * (2 * gelu_in + 6 * gelu_cube * square))
             before = (back * slope).astype(bf16)
-            hid[here, cols] = hidden
-            dpre[here, cols] = before
-            partial[down] += dot(hidden, dbr[here], 0, 0)
-            partial[up] += dot(h2[here], before, 0, 0)
+            down_grad = dot(hidden, grad, 0, 0)
+            up_grad = dot(normed, before, 0, 0)
+            hid[:, cols] = hidden
+            dpre[:, cols] = before
+            partial[down] = down_grad
+            partial[up] = up_grad
             return _
 
-        lax.fori_loop(0, steps, feed, 0)
+        lax.fori_loop(0, 1, feed, 0)
         step(c, 0)
         if c >= 1:
             step(c - 1, 1)
-        if c >= 2:
-            step(c - 2, 2)
-        if c >= 3:
-            step(c - 3, 3)
 
     gvec[...] = jnp.zeros_like(gvec)
-    last = parts[-1][0]
+    last = chunks * 2 * D
 
     def at_step(i, when, tasks):
         @pl.when(i == when)
@@ -473,83 +592,135 @@
             for part, number in tasks:
                 step(part, number)
 
-    def middle_back(i, _):
-        at_step(i, 2, [(3, 1), (2, 2), (1, 3), (0, 4)])
-        at_step(i, 5, [(3, 2), (2, 3), (1, 4), (0, 5)])
-        here = pl.ds(pl.multiple_of(i * block, 64), block)
-        grad = dot(dpre[here], wup[...], 1, 1)
-        normed = n2[i].astype(f32)
-        gvec[16:24] += fold_rows(grad * normed)
-        gvec[24:32] += fold_rows(grad)
-        factor = jnp.concatenate([r2[i]] * 2, 1)
-        grad = alive_of(i) * cot[i].astype(f32) + norm_back(grad, normed, factor, gain_ffn)
-        dmid[i] = grad
-        low = (branch_scale * grad).astype(bf16)
-        partial[last + 3 * D :] += dot(att[i], low, 0, 0)
-        datt[i] = dot(low, wout[...], 1, 1).astype(bf16)
+    for h in range(HEADS):
+        at = last + h * 2 * D + D
+        partial[at : at + D, HEAD_DIM:] = jnp.zeros((D, HEAD_DIM), f32)
+
+    def middle_back(p, _):
+        at_step(p, 1, [(3, 1), (0, 2)])
+        at_step(p, 2, [(1, 2)])
+        here = pl.ds(pl.multiple_of(p * pair * block, 64), pair * block)
+        grads = dpre[here]
+        found = []
+        for j in range(pair):
+            i = p * pair + j
+            normed = n2[i].astype(f32)
+            factor = jnp.concatenate([r2[i]] * 2, 1)
+            outer = alive_of(i) * cot[i].astype(f32)
+            attended = att[i]
+            grad = dot(grads[j * block : (j + 1) * block], wup[...], 1, 1)
+            sums_here = fold_rows(grad * normed), fold_rows(grad)
+            grad = outer + norm_back(grad, normed, factor, gain_ffn)
+            low = (branch_scale * grad).astype(bf16)
+            found.append((grad, low, attended, sums_here))
+        lows = jnp.concatenate([f[1] for f in found], 0)
+        out_grad = dot(jnp.concatenate([f[2] for f in found], 0), lows, 0, 0)
+        back = dot(lows, wout[...], 1, 1).astype(bf16)
+        for j in range(pair):
+            dmid[p * pair + j] = found[j][0]
+            datt[p * pair + j] = back[j * block : (j + 1) * block]
+        for h in range(HEADS):
+            at = last + h * 2 * D + D
+            partial[at : at + D, HEAD_DIM:] += out_grad[:, h * HEAD_DIM : (h + 1) * HEAD_DIM]
+        gvec[16:24] += sum(f[3][0] for f in found)
+        gvec[24:32] += sum(f[3][1] for f in found)
         return _
 
-    lax.fori_loop(0, items, middle_back, 0)
-
-    def attend_back(i, _):
-        at_step(i, 1, [(3, 3), (2, 4), (1, 5), (0, 6)])
-        at_step(i, 3, [(3, 4), (2, 5), (1, 6)])
-        at_step(i, 5, [(3, 5), (2, 6)])
-        for h in range(HEADS):
-            at = h * HEAD_DIM
-            held_k = None
-            held_v = None
+    lax.fori_loop(0, items // pair, middle_back, 0)
+
+    def attend_back(h, p, _):
+        at = h * 3 * HEAD_DIM
+        lanes = slice(h * HEAD_DIM, (h + 1) * HEAD_DIM)
+        found = []
+        for j in range(pair):
+            i = p * pair + j
+            mine = proj[i, :, at : at + 3 * HEAD_DIM]
+            es = [exps[i, r * HEADS + h, :, : 2 * ROW] for r in range(rows)]
+            scaled = datt[i, :, lanes].astype(f32) * inv[i, :, lanes]
+            product = scaled * att[i, :, lanes].astype(f32)
+            low = scaled.astype(bf16)
+            dqs, dks, dvs = [], [], []
+            dps = [
+                dot(low[r * ROW : (r + 1) * ROW], part_of(mine, r, 2, 2, 0), 1, 1)
+                for r in range(rows)
+            ]
+            dss = []
             for r in range(rows):
-                q = proj[i, (r + 1) * ROW : (r + 2) * ROW, at : at + HEAD_DIM]
-                k = proj[i, r * ROW : (r + 2) * ROW, D + at : D + at + HEAD_DIM]
-                v = proj[i, r * ROW : (r + 2) * ROW, 2 * D + at : 2 * D + at + HEAD_DIM]
-                own = slice(r * ROW, (r + 1) * ROW)
-                grad = datt[i, own, at : at + HEAD_DIM].astype(f32) * inv[i, own, at : at + HEAD_DIM]
-                low = grad.astype(bf16)
-                row_dot = jnp.sum(grad * att[i, own, at : at + HEAD_DIM].astype(f32), -1, keepdims=True)
-                e = exps[i, r * HEADS + h, :, : 2 * ROW]
-                ds = (e.astype(f32) * ((dot(low, v, 1, 1) - row_dot) * score_scale)).astype(bf16)
-                dv = dot(e, low, 0, 0)
-                dk = dot(ds, q, 0, 0)
-                dproj[i, (r + 1) * ROW : (r + 2) * ROW, at : at + HEAD_DIM] = dot(ds, k).astype(bf16)
-                first_k, first_v = dk[:ROW], dv[:ROW]
-                if held_k is not None:
-                    first_k += held_k
-                    first_v += held_v
-                dproj[i, r * ROW : (r + 1) * ROW, D + at : D + at + HEAD_DIM] = first_k.astype(bf16)
-                dproj[i, r * ROW : (r + 1) * ROW, 2 * D + at : 2 * D + at + HEAD_DIM] = first_v.astype(bf16)
-                held_k, held_v = dk[ROW:], dv[ROW:]
-            dproj[i, rows * ROW :, D + at : D + at + HEAD_DIM] = held_k.astype(bf16)
-            dproj[i, rows * ROW :, 2 * D + at : 2 * D + at + HEAD_DIM] = held_v.astype(bf16)
-        dproj[i, :ROW, :D] = jnp.zeros((ROW, D), bf16)
+                row_dot = jnp.sum(product[r * ROW : (r + 1) * ROW], -1, keepdims=True)
+                dss.append((es[r].astype(f32) * ((dps[r] - row_dot) * score_scale)).astype(bf16))
+            dvs = [dot(es[r], low[r * ROW : (r + 1) * ROW], 0, 0) for r in range(rows)]
+            dks = [dot(dss[r], part_of(mine, r + 1, 1, 0, 0), 0, 0) for r in range(rows)]
+            dqs = [dot(dss[r], part_of(mine, r, 2, 1, 0)).astype(bf16) for r in range(rows)]
+
+            def gather(grads):
+                lines = []
+                for r in range(rows + 1):
+                    value = 0.0
+                    if r < rows:
+                        value = grads[r][:ROW]
+                    if r > 0:
+                        value += grads[r - 1][ROW:]
+                    lines.append(value.astype(bf16))
+                return jnp.concatenate(lines, 0)
+
+            found.append((jnp.concatenate(dqs, 0), gather(dks), gather(dvs)))
+        for j in range(pair):
+            i = p * pair + j
+            dproj[i, :ROW, at : at + HEAD_DIM] = jnp.zeros((ROW, HEAD_DIM), bf16)
+            dproj[i, ROW:, at : at + HEAD_DIM] = found[j][0]
+            dproj[i, :, at + HEAD_DIM : at + 2 * HEAD_DIM] = found[j][1]
+            dproj[i, :, at + 2 * HEAD_DIM : at + 3 * HEAD_DIM] = found[j][2]
         return _
 
-    lax.fori_loop(0, items, attend_back, 0)
-
-    def weight_back(i, _):
-        for p in range(3):
-            partial[last + p * D : last + (p + 1) * D] += dot(
-                h1[i], dproj[i, :, p * D : (p + 1) * D], 0, 0
-            )
+    def weight_back(h, p, _):
+        left = h1[...].reshape(items * (block + ROW), D)
+        at = h * 3 * HEAD_DIM
+        right = dproj[:, :, at : at + 3 * HEAD_DIM].reshape(items * (block + ROW), 3 * HEAD_DIM)
+        grad = dot(left, right, 0, 0)
+        start = last + h * 2 * D
+        partial[start : start + D] = grad[:, :D]
+        partial[start + D : start + 2 * D, :HEAD_DIM] = grad[:, D:]
         return _
 
-    lax.fori_loop(0, items, weight_back, 0)
-    step(4, 0)
-    step(3, 6)
-
-    def tokens_back(i, _):
-        at_step(i, 2, [(4, 1)])
-        grad = dot(dproj[i], wqkv[...], 1, 1)
-        normed = n1[i].astype(f32)
-        gvec[0:8] += fold_rows(grad * normed)
-        gvec[8:16] += fold_rows(grad)
-        factor = jnp.concatenate([r1[i]] * 2, 1)
-        grad = norm_back(grad, normed, factor, gain_attn)
-        ghalo[i] = grad[:ROW].astype(bf16)
-        dmid[i] += grad[ROW:]
+    for h in range(HEADS):
+
+        def back(p, _):
+            if h == 0:
+                at_step(p, 0, [(2, 2)])
+                at_step(p, 1, [(0, 3)])
+                at_step(p, 2, [(3, 2)])
+            else:
+                at_step(p, 0, [(1, 3)])
+                at_step(p, 1, [(chunks, 1), (2, 3)])
+                at_step(p, 2, [(0, 4)])
+            return attend_back(h, p, _)
+
+        lax.fori_loop(0, items // pair, back, 0)
+        lax.fori_loop(0, 1, functools.partial(weight_back, h), 0)
+        step(chunks + h, 0)
+    step(3, 3)
+    step(1, 4)
+
+    def tokens_back(p, _):
+        at_step(p, 1, [(chunks + 1, 1), (2, 4)])
+        at_step(p, 2, [(chunks, 2), (0, 5)])
+        found = []
+        for j in range(pair):
+            i = p * pair + j
+            grad = dot(dproj[i], wqkv[...], 1, 1)
+            normed = n1[i].astype(f32)
+            factor = jnp.concatenate([r1[i]] * 2, 1)
+            sums_here = fold_rows(grad * normed), fold_rows(grad)
+            grad = norm_back(grad, normed, factor, gain_attn)
+            found.append((grad[:ROW].astype(bf16), dmid[i] + grad[ROW:], sums_here))
+        for j in range(pair):
+            ghalo[p * pair + j] = found[j][0]
+            dmid[p * pair + j] = found[j][1]
+        gvec[0:8] += sum(f[2][0] for f in found)
+        gvec[8:16] += sum(f[2][1] for f in found)
         return _
 
-    lax.fori_loop(0, items, tokens_back, 0)
+    lax.fori_loop(0, items // pair, tokens_back, 0)
     ghalo_copy = pltpu.make_async_remote_copy(
         src_ref=ghalo,
         dst_ref=ghalo_in,
@@ -559,6 +730,12 @@
         device_id_type=MESH,
     )
     ghalo_copy.start()
+
+    own_copy = None
+    if rows > 1:
+        own = pl.ds(0, block - ROW)
+        own_copy = pltpu.make_async_copy(dmid.at[:, own], gtok_ref.at[:, own], store_sems.at[5])
+        own_copy.start()
 
     def vec_copies(kind, number):
         result = []
@@ -601,43 +778,63 @@
             sums.finish(vec_copies("z", 2))
             gvec[0:8] = vec_total(2, n_z)
 
-    def finish(i, _):
-        at_step(i, 1, [(4, 2)])
-        here = pl.ds(pl.multiple_of(i * block, 64), block)
+    def finish(p, _):
+        at_step(p, 0, [(3, 4), (1, 5)])
+        at_step(p, 2, [(chunks + 1, 2)])
+        here = pl.ds(pl.multiple_of(p * pair * block, 64), pair * block)
         branch = dot(hid[here], wdown[...])
-        out[i] = (alive_of(i) * (middle[i] + branch_scale * branch)).astype(bf16)
+        results = [
+            (alive_of(p * pair + j) * (middle[p * pair + j] + branch_scale * branch[j * block : (j + 1) * block])).astype(bf16)
+            for j in range(pair)
+        ]
+        for j in range(pair):
+            out[p * pair + j] = results[j]
         return _
 
-    lax.fori_loop(0, items, finish, 0)
+    lax.fori_loop(0, items // pair, finish, 0)
     out_copy = pltpu.make_async_copy(out, output_ref, store_sems.at[0])
     out_copy.start()
+    step(2, 5)
     vec_step(1)
-    step(4, 3)
     ghalo_copy.wait()
+    tail = block - ROW
     for i in range(items):
-        dmid[i, block - ROW :] += ghalo_in[i].astype(f32)
-    tok_copy = pltpu.make_async_copy(dmid, gtok_ref, store_sems.at[1])
+        dmid[i, tail:] += ghalo_in[i].astype(f32)
+    tok_copy = pltpu.make_async_copy(dmid.at[:, pl.ds(tail, ROW)], gtok_ref.at[:, pl.ds(tail, ROW)], store_sems.at[1])
     tok_copy.start()
+    step(0, 6)
+    step(1, 6)
+    step(3, 5)
     vec_step(2)
-    step(4, 4)
-    step(4, 5)
+    stores = []
+    if direct:
+        order = [(chunks, 3), (2, 6), (3, 6), (chunks + 1, 3)]
+    else:
+        order = [(2, 6), (3, 6)]
+        order += [(chunks + h, n) for n in (3, 4, 5) for h in range(HEADS)]
+    for part, number in order:
+        step(part, number)
     vec_step(3)
     vec_copy = pltpu.make_async_copy(gvec.at[pl.ds(0, 8)], gvec_ref, store_sems.at[2])
     vec_copy.start()
-    step(4, 6)
-    grad_copy = pltpu.make_async_copy(full, grads_ref, store_sems.at[3])
-    grad_copy.start()
-    out_copy.wait()
-    tok_copy.wait()
-    vec_copy.wait()
-    grad_copy.wait()
+    early = pl.ds(0, last)
+    early_copy = pltpu.make_async_copy(full.at[early], grads_ref.at[early], store_sems.at[3])
+    early_copy.start()
+    for h in range(HEADS):
+        step(chunks + h, 4 if direct else 6)
+    late = pl.ds(last, HEADS * 2 * D)
+    late_copy = pltpu.make_async_copy(full.at[late], grads_ref.at[late], store_sems.at[4])
+    late_copy.start()
+    for copy in (out_copy, own_copy, tok_copy, vec_copy, early_copy, late_copy):
+        if copy is not None:
+            copy.wait()
 
 
 def split_kernel(
     raw_out,
     raw_tok,
-    grads,
-    gvec,
+    raw_grads,
+    raw_vec,
     output,
     gtok,
     gqkv,
@@ -648,42 +845,69 @@
     shift_attn,
     gain_ffn,
     shift_ffn,
+    held_out,
+    held_tok,
+    grads,
+    gvec,
     qkv,
     wout,
     up,
     down,
-    sems,
+    load_sems,
+    store_sems,
 ):
-    copies = [
-        pltpu.make_async_copy(raw_tok, gtok, sems.at[0]),
-        pltpu.make_async_copy(raw_out, output, sems.at[1]),
-    ]
-    for copy in copies:
+    chunks = up.shape[1] // D
+    items = raw_tok.shape[0]
+    last = chunks * 2 * D
+    stores = []
+
+    def load(source, target, number):
+        copy = pltpu.make_async_copy(source, target, load_sems.at[number])
         copy.start()
-    chunks = up.shape[1] // D
-
-    def send(source, target, number):
-        copy = pltpu.make_async_copy(source, target, sems.at[number])
+        return copy
+
+    def store(source, target):
+        copy = pltpu.make_async_copy(source, target, store_sems.at[len(stores)])
         copy.start()
-        copies.append(copy)
-
+        stores.append(copy)
+
+    early = load(raw_grads.at[pl.ds(0, last)], grads.at[pl.ds(0, last)], 0)
+    late_rows = pl.ds(last, HEADS * 2 * D)
+    late = load(raw_grads.at[late_rows], grads.at[late_rows], 1)
+    vec_load = load(raw_vec, gvec, 2)
+    half = items // 2
+    tok_loads = [load(raw_tok.at[pl.ds(k * half, half)], held_tok.at[pl.ds(k * half, half)], 3 + k) for k in range(2)]
+    out_load = load(raw_out, held_out, 5)
+    early.wait()
     for c in range(chunks):
         down[c * D : (c + 1) * D] = grads[c * 2 * D : c * 2 * D + D].astype(f32)
-    send(down, gdown, 2)
+    store(down, gdown)
     for c in range(chunks):
         up[:, c * D : (c + 1) * D] = grads[c * 2 * D + D : (c + 1) * 2 * D].astype(f32)
-    send(up, gup, 3)
-    last = chunks * 2 * D
-    for p in range(3):
-        qkv[:, p * D : (p + 1) * D] = grads[last + p * D : last + (p + 1) * D].astype(f32)
-    send(qkv, gqkv, 4)
-    wout[...] = grads[last + 3 * D :].astype(f32)
-    send(wout, gout, 5)
+    store(up, gup)
+    late.wait()
+    for h in range(HEADS):
+        at = last + h * 2 * D
+        lanes = slice(h * HEAD_DIM, (h + 1) * HEAD_DIM)
+        first = grads[at : at + D].astype(f32)
+        second = grads[at + D : at + 2 * D].astype(f32)
+        qkv[:, h * HEAD_DIM : (h + 1) * HEAD_DIM] = first[:, :HEAD_DIM]
+        qkv[:, D + h * HEAD_DIM : D + (h + 1) * HEAD_DIM] = first[:, HEAD_DIM:]
+        qkv[:, 2 * D + h * HEAD_DIM : 2 * D + (h + 1) * HEAD_DIM] = second[:, :HEAD_DIM]
+        wout[:, lanes] = second[:, HEAD_DIM:]
+    store(qkv, gqkv)
+    store(wout, gout)
+    for k in range(2):
+        tok_loads[k].wait()
+        store(held_tok.at[pl.ds(k * half, half)], gtok.at[pl.ds(k * half, half)])
+    out_load.wait()
+    store(held_out, output)
+    vec_load.wait()
     gain_attn[...] = gvec[0:1]
     shift_attn[...] = gvec[1:2]
     gain_ffn[...] = gvec[2:3]
     shift_ffn[...] = gvec[3:4]
-    for copy in copies:
+    for copy in stores:
         copy.wait()
 
 
@@ -712,6 +936,9 @@
     grad_rows = 2 * ff + 4 * width
     half = grad_rows // 2
     links = n_items + n_z - 1
+    plane = n_items * n_z
+    if width % (16 * plane) == 0:
+        links = plane
     vmem = pl.BlockSpec(memory_space=pltpu.VMEM)
     anywhere = pl.BlockSpec(memory_space=pl.ANY)
     raw = [
@@ -721,7 +948,7 @@
         jax.ShapeDtypeStruct((8, width), f32),
     ]
     vectors = [v.reshape(1, width) for v in (gain_attn, shift_attn, gain_ffn, shift_ffn)]
-    parts = ff // width + 1
+    parts = ff // width + HEADS
     vm = pltpu.VMEM
     raw = pl.pallas_call(
         functools.partial(layer_kernel, items, rows, mesh_sizes, seq_size),
@@ -766,9 +993,10 @@
             vm((n_items - 1, half // n_items, width), bf16),
             vm((half // n_items, width), bf16),
             vm((n_z, half // n_items, width), bf16),
+            vm((plane - 1, half // plane // 16 * 16 + 16, width), bf16),
             vm((grad_rows, width), bf16),
-            pltpu.SemaphoreType.DMA((5 + items,)),
-            pltpu.SemaphoreType.DMA((4,)),
+            pltpu.SemaphoreType.DMA((4 + items + 3 * HEADS,)),
+            pltpu.SemaphoreType.DMA((6,)),
             pltpu.SemaphoreType.DMA((4,)),
             pltpu.SemaphoreType.DMA((2, links)),
             pltpu.SemaphoreType.DMA((2 * parts, links)),
@@ -789,16 +1017,21 @@
     outs = pl.pallas_call(
         split_kernel,
         out_shape=shapes,
-        in_specs=[anywhere] * 2 + [vmem] * 2,
+        in_specs=[anywhere] * 4,
         out_specs=[anywhere] * 6 + [vmem] * 4,
         scratch_shapes=[
+            vm((items, block, width), bf16),
+            vm((items, block, width), f32),
+            vm((grad_rows, width), bf16),
+            vm((8, width), f32),
             vm((width, 3 * width), f32),
             vm((width, width), f32),
             vm((width, ff), f32),
             vm((ff, width), f32),
             pltpu.SemaphoreType.DMA((6,)),
+            pltpu.SemaphoreType.DMA((7,)),
         ],
-        compiler_params=pltpu.CompilerParams(vmem_limit_bytes=16 * 2**20),
+        compiler_params=pltpu.CompilerParams(vmem_limit_bytes=63 * 2**20),
     )(*raw)
     return tuple(outs[:6]) + tuple(v.reshape(width) for v in outs[6:])
 

time: 97.4 us -> 66.2 us (0.68)
  Pallas kernels: 91.4 us -> 65.2 us
  local copies, waits for them, and re-layouts: 5.03 us -> 0 us
    pallas_call x1, Pallas kernels: 88 us -> 60.5 us  [shards(): pl.pallas_call(functools.partial(layer_kernel, items, rows, mesh_sizes, s...]
    unnamed x8 -> x0, local copies, waits for them, and re-layouts: 5.03 us -> none
    pallas_call x1, Pallas kernels: 3.39 us -> 4.77 us  [shards(): pl.pallas_call(split_kernel, out_shape=shapes, in_specs=[anywhere] * 4, o...]
where the time goes in v3:
time: 66.2 us; the launch traced here: 66.1 us
  Pallas kernels  65.2 us (98%)
  between operations  0.82 us (1%)
    pallas_call x1, Pallas kernels, shards(): pl.pallas_call(functools.partial(layer_kernel, items, rows, mesh_sizes, s...  60.5 us
    pallas_call x1, Pallas kernels, shards(): pl.pallas_call(split_kernel, out_shape=shapes, in_specs=[anywhere] * 4, o...  4.77 us

profile of v3, /device:TPU:0, one launch (start us, length us, event | category | flops | bytes accessed | tf_op | source)
XLA Modules:
  0.0 66.1 jit_solution(3972468496839581394)
XLA Ops:
  0.6 60.5 %shard_map.195 = (bf16[6,384,256]{2,1,0:T(8,128)(2,1)}, f32[6,384,256]{2,1,0:T(8,128)}, bf16[3072,256]{1,0:T(8,128)(2,1)}, f32[8,256]{1,0:T(8,128)}) custom-call(s32[6]{0:T(128)} %lengths_ref.1, s32[6,3072]{1,0:T(8,128)} %pad_ref.1, bf16[6,384,256]{2,1,0:T(8,128)(2,1)} %tokens_ref.1, bf16[6,384,256]{2,1,0:T(8,128)(2,1)} %cot_hbm.1, ...), custom_call_target="tpu_custom_call" | custom-call | tf_op jit(solution)/shard_map/pallas_call | solution.py:953
  61.1 4.8 %shard_map.196 = (bf16[6,384,256]{2,1,0:T(8,128)(2,1)}, f32[6,384,256]{2,1,0:T(8,128)}, f32[256,768]{1,0:T(8,128)}, f32[256,256]{1,0:T(8,128)}, f32[256,1024]{1,...) custom-call(bf16[6,384,256]{2,1,0:T(8,128)(2,1)} %get-tuple-element., ...), custom_call_target="tpu_custom_call" | custom-call | tf_op jit(solution)/shard_map/pallas_call | solution.py:1017

commit v4 on v3

--- a/solution.py
+++ b/solution.py
@@ -48,6 +48,32 @@
 def fold_rows(values):
     count = values.shape[0] // 8
     return jnp.sum(values.reshape(count, 8, values.shape[1]), 0)
+
+
+def plan(direct):
+    plan = {
+        "feed0": [],
+        "feed1": [(0, 0)],
+        "feed2": [(0, 1)],
+        "feed3": [(1, 0)],
+        "middle": [(1, 1)],
+        "back0": [(0, 2)],
+        "weight0": [(2, 0)],
+        "back1": [(2, 1), (1, 2)],
+        "weight1": [(3, 0)],
+        "tokens0": [(0, 3)],
+        "tokens1": [(3, 1)],
+        "finish0": [("v", 1)],
+        "finish1": [(1, 3)],
+        "tail": [(0, 4), (2, 2), ("v", 2), (1, 4), (3, 2), (0, 5), (1, 5)],
+        "last": [(2, 4), (3, 4)],
+    }
+    if direct:
+        plan["tail"] += [(2, 3), ("v", 3), (3, 3), (0, 6), (1, 6)]
+    else:
+        plan["tail"] += [(0, 6), (1, 6)] + [(p, n) for n in (3, 4, 5) for p in (2, 3)] + [("v", 3)]
+        plan["last"] = [(2, 6), (3, 6)]
+    return plan
 
 
 class Sums:
@@ -82,31 +108,28 @@
         return range(1, counts[kind])
 
     def copies(self, part, phase, kind, source, target):
-        result = []
-        base = {"core": 0, "items": 1, "z": self.n_items, "plane": 1}[kind]
-        for step in self.steps_of(kind):
-            slot = (part * 2 + phase, base + step - 1)
-            result.append(
-                pltpu.make_async_remote_copy(
-                    src_ref=source(step),
-                    dst_ref=target(step),
-                    send_sem=self.send.at[slot],
-                    recv_sem=self.recv.at[slot],
-                    device_id=self.partner(kind, step),
-                    device_id_type=pl.DeviceIdType.MESH,
-                )
+        number = part * 6 + phase * 3 + {"core": 0, "items": 1, "z": 2, "plane": 1}[kind]
+        return number, [
+            pltpu.make_async_remote_copy(
+                src_ref=source(step),
+                dst_ref=target(step),
+                send_sem=self.send.at[number],
+                recv_sem=self.recv.at[number],
+                device_id=self.partner(kind, step),
+                device_id_type=pl.DeviceIdType.MESH,
             )
-        return result
+            for step in self.steps_of(kind)
+        ]
 
     def start(self, copies):
-        for copy in copies:
+        for copy in copies[1]:
             copy.start()
 
-    def finish(self, copies):
-        for copy in copies:
-            copy.wait_recv()
-        for copy in copies:
-            copy.wait_send()
+    def finish(self, copies, count):
+        number, each = copies
+        size = self.full.at[pl.ds(0, len(each) * count)]
+        pltpu.make_async_copy(size, size, self.recv.at[number]).wait()
+        pltpu.make_async_copy(size, size, self.send.at[number]).wait()
 
     def place(self, first, rows):
         half = rows // 2
@@ -175,7 +198,7 @@
         count = rows // 2 // (self.n_items * self.n_z)
         base = first // 2
         if number == 2:
-            self.finish(self.plane_copies(part, first, rows))
+            self.finish(self.plane_copies(part, first, rows), count)
             own = base + (self.item * self.n_z + self.z) * count
             value = self.i_out[pl.ds(pl.multiple_of(own, 16), count)].astype(f32)
             at = pl.ds(base // (self.n_items * self.n_z), count)
@@ -184,10 +207,10 @@
             self.held(first, rows, 2)[...] = value.astype(bf16)
             self.start(self.back_copies(part, first, rows, "plane"))
         if number == 3:
-            self.finish(self.back_copies(part, first, rows, "plane"))
+            self.finish(self.back_copies(part, first, rows, "plane"), count)
             self.start(self.back_copies(part, first, rows, "core"))
         if number == 4:
-            self.finish(self.back_copies(part, first, rows, "core"))
+            self.finish(self.back_copies(part, first, rows, "core"), rows // 2)
 
     def step(self, part, first, rows, number, plane=False):
         if plane and number > 1:
@@ -201,7 +224,7 @@
             self.c_out[pl.ds(base_c, half)] = self.partial[away].astype(bf16)
             self.start(self.first_copies(part, first, rows))
         if number == 1:
-            self.finish(self.first_copies(part, first, rows))
+            self.finish(self.first_copies(part, first, rows), half)
             here = pl.ds(base_c, half)
             own = pl.ds(pl.multiple_of(first + self.core * half, 16), half)
             self.i_out[here] = (self.partial[own] + self.c_in[here].astype(f32)).astype(bf16)
@@ -210,7 +233,7 @@
             else:
                 self.start(self.items_copies(part, first, rows))
         if number == 2:
-            self.finish(self.items_copies(part, first, rows))
+            self.finish(self.items_copies(part, first, rows), quarter)
             own = pl.ds(pl.multiple_of(base_c + self.item * quarter, 16), quarter)
             at = pl.ds(base_i, quarter)
             value = self.i_out[own].astype(f32)
@@ -221,7 +244,7 @@
                 self.z_in[self.z, at] = value.astype(bf16)
             self.start(self.z_copies(part, first, rows))
         if number == 3:
-            self.finish(self.z_copies(part, first, rows))
+            self.finish(self.z_copies(part, first, rows), last)
             if split:
                 own = pl.ds(pl.multiple_of(base_i + self.z * last, 16), last)
                 at = pl.ds(base_i // self.n_z, last)
@@ -239,13 +262,13 @@
             else:
                 self.start(self.back_copies(part, first, rows, "items"))
         if number == 4 and split:
-            self.finish(self.back_copies(part, first, rows, "z"))
+            self.finish(self.back_copies(part, first, rows, "z"), last)
             self.start(self.back_copies(part, first, rows, "items"))
         if number == 5:
-            self.finish(self.back_copies(part, first, rows, "items"))
+            self.finish(self.back_copies(part, first, rows, "items"), quarter)
             self.start(self.back_copies(part, first, rows, "core"))
         if number == 6:
-            self.finish(self.back_copies(part, first, rows, "core"))
+            self.finish(self.back_copies(part, first, rows, "core"), rows // 2)
 
 
 def layer_kernel(
@@ -330,11 +353,18 @@
     sums = Sums(
         mesh_sizes, (partial, c_out, c_in, i_out, i_in, z_out, z_in, d_in, full, send_sems, recv_sems)
     )
-    parts = [(c * 2 * D, 2 * D) for c in range(chunks + HEADS)]
+    wide = chunks // 2
+    parts = [(k * wide * 2 * D, wide * 2 * D) for k in range(2)]
+    parts += [((chunks + h) * 2 * D, 2 * D) for h in range(HEADS)]
     direct = D % (16 * n_items * n_z) == 0
-
-    def step(part, number):
-        sums.step(part, *parts[part], number, plane=direct and part >= chunks)
+    schedule = plan(direct)
+
+    def hook(name):
+        for part, number in schedule[name]:
+            if part == "v":
+                vec_step(number)
+            else:
+                sums.step(part, *parts[part], number, plane=direct and part >= 2)
 
     after = {"items": item, "seq": lax.rem(seq + 1, seq_size)}
     ahead = {"items": item, "seq": lax.rem(seq + seq_size - 1, seq_size)}
@@ -342,9 +372,6 @@
     greeted = [after, ahead]
     for kind in ("core", "plane") if direct else ("core", "items", "z"):
         greeted += [sums.partner(kind, s) for s in sums.steps_of(kind)]
-    for device in greeted:
-        pl.semaphore_signal(barrier, inc=1, device_id=device, device_id_type=MESH)
-
     loads = [
         (wout_hbm, wout),
         (wup_hbm, wup),
@@ -375,16 +402,8 @@
     for copy in weight_loads:
         copy.start()
 
-    pl.semaphore_wait(barrier, len(greeted))
-    halo_copy = pltpu.make_async_remote_copy(
-        src_ref=tokens_ref.at[:, pl.ds(block - ROW, ROW)],
-        dst_ref=x.at[:, pl.ds(0, ROW)],
-        send_sem=halo_sems.at[0],
-        recv_sem=halo_sems.at[1],
-        device_id=after,
-        device_id_type=MESH,
-    )
-    halo_copy.start()
+    for device in greeted:
+        pl.semaphore_signal(barrier, inc=1, device_id=device, device_id_type=MESH)
 
     first_pos = seq * block
 
@@ -431,26 +450,28 @@
 
     for copy in qkv_loads:
         copy.wait()
-    pair = 2 if items % 2 == 0 else 1
-
-    def project(p, _):
-        for j in range(pair):
-            pltpu.make_async_copy(
-                tokens_ref.at[p * pair + j],
-                x.at[p * pair + j, pl.ds(ROW, block)],
-                load_sems.at[4 + p * pair + j],
-            ).wait()
-        found = [first_norm(x[p * pair + j, ROW:].astype(f32)) for j in range(pair)]
-        results = [dot(low, wqkv[...]).astype(bf16) for low, _, _ in found]
-        for j in range(pair):
-            low, normed, factor = found[j]
-            h1[p * pair + j, ROW:] = low
-            n1[p * pair + j, ROW:] = normed
-            r1[p * pair + j, ROW:] = jnp.broadcast_to(factor, (block, 128))
-            proj[p * pair + j, ROW:] = results[j]
-        return _
-
-    lax.fori_loop(0, items // pair, project, 0)
+    for copy in token_loads:
+        copy.wait()
+    found = [first_norm(x[i, ROW:].astype(f32)) for i in range(items)]
+    results = [dot(low, wqkv[...]).astype(bf16) for low, _, _ in found]
+    for i in range(items):
+        low, normed, factor = found[i]
+        h1[i, ROW:] = low
+        n1[i, ROW:] = normed
+        r1[i, ROW:] = jnp.broadcast_to(factor, (block, 128))
+        proj[i, ROW:] = results[i]
+
+    pl.semaphore_wait(barrier, len(greeted))
+    halo_copy = pltpu.make_async_remote_copy(
+        src_ref=tokens_ref.at[:, pl.ds(block - ROW, ROW)],
+        dst_ref=x.at[:, pl.ds(0, ROW)],
+        send_sem=halo_sems.at[0],
+        recv_sem=halo_sems.at[1],
+        device_id=after,
+        device_id_type=MESH,
+    )
+    halo_copy.start()
+
     query_pos = lax.broadcasted_iota(jnp.int32, (ROW, 2 * ROW), 0)
     key_pos = lax.broadcasted_iota(jnp.int32, (ROW, 2 * ROW), 1) - ROW
     causal = jnp.where(key_pos <= query_pos, 0.0, masked_value)
@@ -484,156 +505,104 @@
     def heads(values):
         return jnp.concatenate(values, 1)
 
-    def attend(p, _):
-        units = [(r, h) for r in range(1, rows) for h in range(HEADS)]
-        found = []
-        for j in range(pair):
-            i = p * pair + j
-            found.append(weigh(proj[i], lambda r: keys[r, pl.ds(i, 1), : 2 * ROW], units))
-        for j in range(pair):
-            i = p * pair + j
-            lows, shares, results = found[j]
-            for (r, h), e in zip(units, lows):
+    def attend(first, end):
+        units = [(r, h) for r in range(first, end) for h in range(HEADS)]
+        here = slice(first * ROW, end * ROW)
+        count = (end - first) * ROW
+        mask = alive[:, here]
+        grads = jnp.concatenate([mask, mask], 2) * cot[:, here].astype(f32)
+        grads = (branch_scale * grads).astype(bf16)
+        all_shares, all_results, all_lows = [], [], []
+        for i in range(items):
+            lows, shares, results = weigh(proj[i], lambda r: keys[r, i : i + 1, : 2 * ROW], units)
+            all_lows.append(lows)
+            for values, joined in ((shares, all_shares), (results, all_results)):
+                lines = [heads(values[k : k + HEADS]) for k in range(0, len(units), HEADS)]
+                joined.append(jnp.concatenate(lines, 0))
+        attended = jnp.concatenate(all_results, 0)
+        inputs = x[:, ROW + first * ROW : ROW + end * ROW].astype(f32).reshape(items * count, D)
+        mid = inputs + branch_scale * dot(attended, wout[...])
+        normed, factor = normalise(mid)
+        low = (normed * gain_ffn + shift_ffn).astype(bf16)
+        for i in range(items):
+            mine = slice(i * count, (i + 1) * count)
+            flat = slice(i * block + first * ROW, i * block + end * ROW)
+            for (r, h), e in zip(units, all_lows[i]):
                 exps[i, r * HEADS + h, :, : 2 * ROW] = e
-            for r in range(1, rows):
-                at = (r - 1) * HEADS
-                inv[i, r * ROW : (r + 1) * ROW] = heads(shares[at : at + HEADS])
-                att[i, r * ROW : (r + 1) * ROW] = heads(results[at : at + HEADS])
-        return _
-
-    if rows > 1:
-        lax.fori_loop(0, items // pair, attend, 0)
+            inv[i, here] = all_shares[i]
+            att[i, here] = all_results[i]
+            middle[i, here] = mid[mine]
+            n2[i, here] = normed[mine].astype(bf16)
+            r2[i, here] = jnp.broadcast_to(factor[mine], (count, 128))
+            h2[flat] = low[mine]
+            dbr[flat] = grads[i]
+
+    attend(1, rows)
     halo_copy.wait()
-
-    def project_halo(p, _):
-        low, normed, factor = first_norm(x[:, :ROW].astype(f32).reshape(items * ROW, D))
-        results = [
-            dot(low, wqkv[:, (h * 3 + 1) * HEAD_DIM : (h * 3 + 3) * HEAD_DIM]).astype(bf16)
-            for h in range(HEADS)
-        ]
-        h1[:, :ROW] = low.reshape(items, ROW, D)
-        n1[:, :ROW] = normed.reshape(items, ROW, D)
-        r1[:, :ROW] = jnp.broadcast_to(factor, (items * ROW, 128)).reshape(items, ROW, 128)
-        for h in range(HEADS):
-            at = (h * 3 + 1) * HEAD_DIM
-            proj[:, :ROW, at : at + 2 * HEAD_DIM] = results[h].reshape(items, ROW, 2 * HEAD_DIM)
-        return _
-
-    lax.fori_loop(0, 1, project_halo, 0)
-
-    def attend_first(p, _):
-        units = [(0, h) for h in range(HEADS)]
-        found = []
-        for j in range(pair):
-            i = p * pair + j
-            others = att[i, ROW:]
-            inputs = x[i, ROW:].astype(f32)
-            grad = (branch_scale * (alive_of(i) * cot[i].astype(f32))).astype(bf16)
-            lows, shares, results = weigh(
-                proj[i, : 2 * ROW], lambda r: keys[r, pl.ds(i, 1), : 2 * ROW], units
-            )
-            result = heads(results)
-            whole = jnp.concatenate([result, others], 0) if rows > 1 else result
-            mid = inputs + branch_scale * dot(whole, wout[...])
-            normed, factor = normalise(mid)
-            low = (normed * gain_ffn + shift_ffn).astype(bf16)
-            found.append((lows, shares, result, mid, normed.astype(bf16), factor, low, grad))
-        for j in range(pair):
-            i = p * pair + j
-            lows, shares, result, mid, normed, factor, low, grad = found[j]
-            here = pl.ds(pl.multiple_of(i * block, 64), block)
-            for h in range(HEADS):
-                exps[i, h, :, : 2 * ROW] = lows[h]
-            inv[i, :ROW] = heads(shares)
-            att[i, :ROW] = result
-            middle[i] = mid
-            n2[i] = normed
-            r2[i] = jnp.broadcast_to(factor, (block, 128))
-            h2[here] = low
-            dbr[here] = grad
-        return _
-
-    lax.fori_loop(0, items // pair, attend_first, 0)
+    low, normed, factor = first_norm(x[:, :ROW].astype(f32).reshape(items * ROW, D))
+    results = [
+        dot(low, wqkv[:, (h * 3 + 1) * HEAD_DIM : (h * 3 + 3) * HEAD_DIM]).astype(bf16)
+        for h in range(HEADS)
+    ]
+    h1[:, :ROW] = low.reshape(items, ROW, D)
+    n1[:, :ROW] = normed.reshape(items, ROW, D)
+    r1[:, :ROW] = jnp.broadcast_to(factor, (items * ROW, 128)).reshape(items, ROW, 128)
+    for h in range(HEADS):
+        at = (h * 3 + 1) * HEAD_DIM
+        proj[:, :ROW, at : at + 2 * HEAD_DIM] = results[h].reshape(items, ROW, 2 * HEAD_DIM)
+    attend(0, 1)
 
     for c in range(chunks):
         cols = slice(c * D, (c + 1) * D)
         down = slice(c * 2 * D, c * 2 * D + D)
         up = slice(c * 2 * D + D, (c + 1) * 2 * D)
 
-        def feed(t, _):
-            normed = h2[...]
-            grad = dbr[...]
-            u = dot(normed, wup[:, cols])
-            back = dot(grad, wdown[cols], 1, 1)
-            square = u * u
-            s = 0.5 * jnp.tanh(u * (gelu_in + gelu_cube * square)) + 0.5
-            hidden = (u * s).astype(bf16)
-            slope = s + u * ((s - s * s) * (2 * gelu_in + 6 * gelu_cube * square))
-            before = (back * slope).astype(bf16)
-            down_grad = dot(hidden, grad, 0, 0)
-            up_grad = dot(normed, before, 0, 0)
-            hid[:, cols] = hidden
-            dpre[:, cols] = before
-            partial[down] = down_grad
-            partial[up] = up_grad
-            return _
-
-        lax.fori_loop(0, 1, feed, 0)
-        step(c, 0)
-        if c >= 1:
-            step(c - 1, 1)
-
-    gvec[...] = jnp.zeros_like(gvec)
+        normed = h2[...]
+        grad = dbr[...]
+        u = dot(normed, wup[:, cols])
+        back = dot(grad, wdown[cols], 1, 1)
+        square = u * u
+        s = 0.5 * jnp.tanh(u * (gelu_in + gelu_cube * square)) + 0.5
+        hidden = (u * s).astype(bf16)
+        slope = s + u * ((s - s * s) * (2 * gelu_in + 6 * gelu_cube * square))
+        before = (back * slope).astype(bf16)
+        down_grad = dot(hidden, grad, 0, 0)
+        up_grad = dot(normed, before, 0, 0)
+        hid[:, cols] = hidden
+        dpre[:, cols] = before
+        partial[down] = down_grad
+        partial[up] = up_grad
+        hook("feed%d" % c)
+
     last = chunks * 2 * D
 
-    def at_step(i, when, tasks):
-        @pl.when(i == when)
-        def _():
-            for part, number in tasks:
-                step(part, number)
-
+    found = []
+    for i in range(items):
+        normed = n2[i].astype(f32)
+        factor = jnp.concatenate([r2[i]] * 2, 1)
+        outer = alive_of(i) * cot[i].astype(f32)
+        grad = dot(dpre[i * block : (i + 1) * block], wup[...], 1, 1)
+        sums_here = fold_rows(grad * normed), fold_rows(grad)
+        grad = outer + norm_back(grad, normed, factor, gain_ffn)
+        found.append((grad, (branch_scale * grad).astype(bf16), sums_here))
+    lows = jnp.concatenate([f[1] for f in found], 0)
+    out_grad = dot(att[...].reshape(total, D), lows, 0, 0)
+    back = dot(lows, wout[...], 1, 1).astype(bf16)
+    for i in range(items):
+        dmid[i] = found[i][0]
+        datt[i] = back[i * block : (i + 1) * block]
     for h in range(HEADS):
         at = last + h * 2 * D + D
-        partial[at : at + D, HEAD_DIM:] = jnp.zeros((D, HEAD_DIM), f32)
-
-    def middle_back(p, _):
-        at_step(p, 1, [(3, 1), (0, 2)])
-        at_step(p, 2, [(1, 2)])
-        here = pl.ds(pl.multiple_of(p * pair * block, 64), pair * block)
-        grads = dpre[here]
-        found = []
-        for j in range(pair):
-            i = p * pair + j
-            normed = n2[i].astype(f32)
-            factor = jnp.concatenate([r2[i]] * 2, 1)
-            outer = alive_of(i) * cot[i].astype(f32)
-            attended = att[i]
-            grad = dot(grads[j * block : (j + 1) * block], wup[...], 1, 1)
-            sums_here = fold_rows(grad * normed), fold_rows(grad)
-            grad = outer + norm_back(grad, normed, factor, gain_ffn)
-            low = (branch_scale * grad).astype(bf16)
-            found.append((grad, low, attended, sums_here))
-        lows = jnp.concatenate([f[1] for f in found], 0)
-        out_grad = dot(jnp.concatenate([f[2] for f in found], 0), lows, 0, 0)
-        back = dot(lows, wout[...], 1, 1).astype(bf16)
-        for j in range(pair):
-            dmid[p * pair + j] = found[j][0]
-            datt[p * pair + j] = back[j * block : (j + 1) * block]
-        for h in range(HEADS):
-            at = last + h * 2 * D + D
-            partial[at : at + D, HEAD_DIM:] += out_grad[:, h * HEAD_DIM : (h + 1) * HEAD_DIM]
-        gvec[16:24] += sum(f[3][0] for f in found)
-        gvec[24:32] += sum(f[3][1] for f in found)
-        return _
-
-    lax.fori_loop(0, items // pair, middle_back, 0)
-
-    def attend_back(h, p, _):
+        partial[at : at + D, HEAD_DIM:] = out_grad[:, h * HEAD_DIM : (h + 1) * HEAD_DIM]
+    gvec[16:24] = sum(f[2][0] for f in found)
+    gvec[24:32] = sum(f[2][1] for f in found)
+    hook("middle")
+
+    def attend_back(h):
         at = h * 3 * HEAD_DIM
         lanes = slice(h * HEAD_DIM, (h + 1) * HEAD_DIM)
         found = []
-        for j in range(pair):
-            i = p * pair + j
+        for i in range(items):
             mine = proj[i, :, at : at + 3 * HEAD_DIM]
             es = [exps[i, r * HEADS + h, :, : 2 * ROW] for r in range(rows)]
             scaled = datt[i, :, lanes].astype(f32) * inv[i, :, lanes]
@@ -664,15 +633,13 @@
                 return jnp.concatenate(lines, 0)
 
             found.append((jnp.concatenate(dqs, 0), gather(dks), gather(dvs)))
-        for j in range(pair):
-            i = p * pair + j
+        for i in range(items):
             dproj[i, :ROW, at : at + HEAD_DIM] = jnp.zeros((ROW, HEAD_DIM), bf16)
-            dproj[i, ROW:, at : at + HEAD_DIM] = found[j][0]
-            dproj[i, :, at + HEAD_DIM : at + 2 * HEAD_DIM] = found[j][1]
-            dproj[i, :, at + 2 * HEAD_DIM : at + 3 * HEAD_DIM] = found[j][2]
-        return _
-
-    def weight_back(h, p, _):
+            dproj[i, ROW:, at : at + HEAD_DIM] = found[i][0]
+            dproj[i, :, at + HEAD_DIM : at + 2 * HEAD_DIM] = found[i][1]
+            dproj[i, :, at + 2 * HEAD_DIM : at + 3 * HEAD_DIM] = found[i][2]
+
+    def weight_back(h):
         left = h1[...].reshape(items * (block + ROW), D)
         at = h * 3 * HEAD_DIM
         right = dproj[:, :, at : at + 3 * HEAD_DIM].reshape(items * (block + ROW), 3 * HEAD_DIM)
@@ -680,47 +647,36 @@
         start = last + h * 2 * D
         partial[start : start + D] = grad[:, :D]
         partial[start + D : start + 2 * D, :HEAD_DIM] = grad[:, D:]
-        return _
-
-    for h in range(HEADS):
-
-        def back(p, _):
-            if h == 0:
-                at_step(p, 0, [(2, 2)])
-                at_step(p, 1, [(0, 3)])
-                at_step(p, 2, [(3, 2)])
-            else:
-                at_step(p, 0, [(1, 3)])
-                at_step(p, 1, [(chunks, 1), (2, 3)])
-                at_step(p, 2, [(0, 4)])
-            return attend_back(h, p, _)
-
-        lax.fori_loop(0, items // pair, back, 0)
-        lax.fori_loop(0, 1, functools.partial(weight_back, h), 0)
-        step(chunks + h, 0)
-    step(3, 3)
-    step(1, 4)
-
-    def tokens_back(p, _):
-        at_step(p, 1, [(chunks + 1, 1), (2, 4)])
-        at_step(p, 2, [(chunks, 2), (0, 5)])
+
+    attend_back(0)
+    hook("back0")
+    weight_back(0)
+    hook("weight0")
+    attend_back(1)
+    hook("back1")
+    weight_back(1)
+    hook("weight1")
+
+    def tokens_back(first, end):
         found = []
-        for j in range(pair):
-            i = p * pair + j
+        for i in range(first, end):
             grad = dot(dproj[i], wqkv[...], 1, 1)
             normed = n1[i].astype(f32)
             factor = jnp.concatenate([r1[i]] * 2, 1)
             sums_here = fold_rows(grad * normed), fold_rows(grad)
             grad = norm_back(grad, normed, factor, gain_attn)
             found.append((grad[:ROW].astype(bf16), dmid[i] + grad[ROW:], sums_here))
-        for j in range(pair):
-            ghalo[p * pair + j] = found[j][0]
-            dmid[p * pair + j] = found[j][1]
-        gvec[0:8] += sum(f[2][0] for f in found)
-        gvec[8:16] += sum(f[2][1] for f in found)
-        return _
-
-    lax.fori_loop(0, items // pair, tokens_back, 0)
+        for i in range(first, end):
+            ghalo[i] = found[i - first][0]
+            dmid[i] = found[i - first][1]
+        return sum(f[2][0] for f in found), sum(f[2][1] for f in found)
+
+    half = items // 2
+    one = tokens_back(0, half)
+    hook("tokens0")
+    two = tokens_back(half, items)
+    gvec[0:8] = one[0] + two[0]
+    gvec[8:16] = one[1] + two[1]
     ghalo_copy = pltpu.make_async_remote_copy(
         src_ref=ghalo,
         dst_ref=ghalo_in,
@@ -755,6 +711,14 @@
             )
         return result
 
+    def start_all(copies):
+        for copy in copies:
+            copy.start()
+
+    def finish_all(copies):
+        for copy in copies:
+            copy.wait()
+
     def vec_total(number, size):
         value = vec_buf[number, 0]
         for k in range(1, size):
@@ -763,65 +727,51 @@
 
     lines = [jnp.sum(gvec[8 * k : 8 * k + 8], 0, keepdims=True) for k in range(4)]
     vec_buf[0, sums.core] = jnp.concatenate(lines + [jnp.zeros((4, D), f32)], 0)
-    sums.start(vec_copies("core", 0))
+    start_all(vec_copies("core", 0))
 
     def vec_step(number):
         if number == 1:
-            sums.finish(vec_copies("core", 0))
+            finish_all(vec_copies("core", 0))
             vec_buf[1, item] = vec_total(0, 2)
-            sums.start(vec_copies("items", 1))
+            start_all(vec_copies("items", 1))
         if number == 2:
-            sums.finish(vec_copies("items", 1))
+            finish_all(vec_copies("items", 1))
             vec_buf[2, sums.z] = vec_total(1, n_items)
-            sums.start(vec_copies("z", 2))
+            start_all(vec_copies("z", 2))
         if number == 3:
-            sums.finish(vec_copies("z", 2))
+            finish_all(vec_copies("z", 2))
             gvec[0:8] = vec_total(2, n_z)
 
-    def finish(p, _):
-        at_step(p, 0, [(3, 4), (1, 5)])
-        at_step(p, 2, [(chunks + 1, 2)])
-        here = pl.ds(pl.multiple_of(p * pair * block, 64), pair * block)
-        branch = dot(hid[here], wdown[...])
+    def finish(first, end):
+        branch = dot(hid[first * block : end * block], wdown[...])
         results = [
-            (alive_of(p * pair + j) * (middle[p * pair + j] + branch_scale * branch[j * block : (j + 1) * block])).astype(bf16)
-            for j in range(pair)
+            alive_of(i)
+            * (middle[i] + branch_scale * branch[(i - first) * block : (i - first + 1) * block])
+            for i in range(first, end)
         ]
-        for j in range(pair):
-            out[p * pair + j] = results[j]
-        return _
-
-    lax.fori_loop(0, items // pair, finish, 0)
+        for i in range(first, end):
+            out[i] = results[i - first].astype(bf16)
+
+    hook("tokens1")
+    finish(0, half)
+    hook("finish0")
+    finish(half, items)
     out_copy = pltpu.make_async_copy(out, output_ref, store_sems.at[0])
     out_copy.start()
-    step(2, 5)
-    vec_step(1)
+    hook("finish1")
     ghalo_copy.wait()
     tail = block - ROW
     for i in range(items):
         dmid[i, tail:] += ghalo_in[i].astype(f32)
     tok_copy = pltpu.make_async_copy(dmid.at[:, pl.ds(tail, ROW)], gtok_ref.at[:, pl.ds(tail, ROW)], store_sems.at[1])
     tok_copy.start()
-    step(0, 6)
-    step(1, 6)
-    step(3, 5)
-    vec_step(2)
-    stores = []
-    if direct:
-        order = [(chunks, 3), (2, 6), (3, 6), (chunks + 1, 3)]
-    else:
-        order = [(2, 6), (3, 6)]
-        order += [(chunks + h, n) for n in (3, 4, 5) for h in range(HEADS)]
-    for part, number in order:
-        step(part, number)
-    vec_step(3)
+    hook("tail")
     vec_copy = pltpu.make_async_copy(gvec.at[pl.ds(0, 8)], gvec_ref, store_sems.at[2])
     vec_copy.start()
     early = pl.ds(0, last)
     early_copy = pltpu.make_async_copy(full.at[early], grads_ref.at[early], store_sems.at[3])
     early_copy.start()
-    for h in range(HEADS):
-        step(chunks + h, 4 if direct else 6)
+    hook("last")
     late = pl.ds(last, HEADS * 2 * D)
     late_copy = pltpu.make_async_copy(full.at[late], grads_ref.at[late], store_sems.at[4])
     late_copy.start()
@@ -948,7 +898,7 @@
         jax.ShapeDtypeStruct((8, width), f32),
     ]
     vectors = [v.reshape(1, width) for v in (gain_attn, shift_attn, gain_ffn, shift_ffn)]
-    parts = ff // width + HEADS
+    parts = 2 + HEADS
     vm = pltpu.VMEM
     raw = pl.pallas_call(
         functools.partial(layer_kernel, items, rows, mesh_sizes, seq_size),
@@ -999,8 +949,8 @@
             pltpu.SemaphoreType.DMA((6,)),
             pltpu.SemaphoreType.DMA((4,)),
             pltpu.SemaphoreType.DMA((2, links)),
-            pltpu.SemaphoreType.DMA((2 * parts, links)),
-            pltpu.SemaphoreType.DMA((2 * parts, links)),
+            pltpu.SemaphoreType.DMA((6 * parts,)),
+            pltpu.SemaphoreType.DMA((6 * parts,)),
         ],
         compiler_params=pltpu.CompilerParams(
             vmem_limit_bytes=63 * 2**20, collective_id=0, has_side_effects=True

time: 66.2 us -> 63 us (0.952)
  Pallas kernels: 65.2 us -> 62 us
    pallas_call x1, Pallas kernels: 60.5 us -> 57.2 us  [shards(): pl.pallas_call(functools.partial(layer_kernel, items, rows, mesh_sizes, s...]
where the time goes in v4:
time: 63 us; the launch traced here: 62.8 us
  Pallas kernels  62 us (98%)
  between operations  0.84 us (1%)
    pallas_call x1, Pallas kernels, shards(): pl.pallas_call(functools.partial(layer_kernel, items, rows, mesh_sizes, s...  57.2 us
    pallas_call x1, Pallas kernels, shards(): pl.pallas_call(split_kernel, out_shape=shapes, in_specs=[anywhere] * 4, o...  4.77 us

profile of v4, /device:TPU:0, one launch (start us, length us, event | category | flops | bytes accessed | tf_op | source)
XLA Modules:
  0.0 62.8 jit_solution(16489906486558189106)
XLA Ops:
  0.6 57.2 %shard_map.195 = (bf16[6,384,256]{2,1,0:T(8,128)(2,1)}, f32[6,384,256]{2,1,0:T(8,128)}, bf16[3072,256]{1,0:T(8,128)(2,1)}, f32[8,256]{1,0:T(8,128)}) custom-call(s32[6]{0:T(128)} %lengths_ref.1, s32[6,3072]{1,0:T(8,128)} %pad_ref.1, bf16[6,384,256]{2,1,0:T(8,128)(2,1)} %tokens_ref.1, bf16[6,384,256]{2,1,0:T(8,128)(2,1)} %cot_hbm.1, ...), custom_call_target="tpu_custom_call" | custom-call | tf_op jit(solution)/shard_map/pallas_call | solution.py:903
  57.9 4.8 %shard_map.196 = (bf16[6,384,256]{2,1,0:T(8,128)(2,1)}, f32[6,384,256]{2,1,0:T(8,128)}, f32[256,768]{1,0:T(8,128)}, f32[256,256]{1,0:T(8,128)}, f32[256,1024]{1,...) custom-call(bf16[6,384,256]{2,1,0:T(8,128)(2,1)} %get-tuple-element., ...), custom_call_target="tpu_custom_call" | custom-call | tf_op jit(solution)/shard_map/pallas_call | solution.py:967

commit v5 on v4

--- a/solution.py
+++ b/solution.py
@@ -50,7 +50,7 @@
     return jnp.sum(values.reshape(count, 8, values.shape[1]), 0)
 
 
-def plan(direct):
+def plan():
     plan = {
         "feed0": [],
         "feed1": [(0, 0)],
@@ -63,23 +63,18 @@
         "weight1": [(3, 0)],
         "tokens0": [(0, 3)],
         "tokens1": [(3, 1)],
-        "finish0": [("v", 1)],
+        "finish0": [("v", 1), (2, 2)],
         "finish1": [(1, 3)],
-        "tail": [(0, 4), (2, 2), ("v", 2), (1, 4), (3, 2), (0, 5), (1, 5)],
-        "last": [(2, 4), (3, 4)],
+        "tail": [(0, 4), (3, 2), ("v", 2), (1, 4), (2, 3), (0, 5), (3, 3), (1, 5), (2, 5), (0, 6), (3, 5), (1, 6), ("v", 3)],
+        "last": [(2, 6), (3, 6)],
     }
-    if direct:
-        plan["tail"] += [(2, 3), ("v", 3), (3, 3), (0, 6), (1, 6)]
-    else:
-        plan["tail"] += [(0, 6), (1, 6)] + [(p, n) for n in (3, 4, 5) for p in (2, 3)] + [("v", 3)]
-        plan["last"] = [(2, 6), (3, 6)]
     return plan
 
 
 class Sums:
     def __init__(self, mesh_sizes, refs):
         (self.partial, self.c_out, self.c_in, self.i_out, self.i_in, self.z_out, self.z_in,
-         self.d_in, self.full, self.send, self.recv) = refs
+         self.full, self.send, self.recv) = refs
         self.n_items, self.n_z = mesh_sizes
         self.item = lax.axis_index("items")
         seq = lax.axis_index("seq")
@@ -89,26 +84,15 @@
     def partner(self, kind, step):
         if kind == "core":
             return {"items": self.item, "seq": self.z * 2 + 1 - self.core}
-        item, z = self.spot(kind, step)
-        return {"items": item, "seq": z * 2 + self.core}
-
-    def spot(self, kind, step):
-        items_step, z_step = {
-            "items": (step, 0),
-            "z": (0, step),
-            "plane": (step // self.n_z, step % self.n_z),
-        }[kind]
-        return (
-            lax.rem(self.item + items_step, self.n_items),
-            lax.rem(self.z + z_step, self.n_z),
-        )
+        if kind == "items":
+            return {"items": lax.rem(self.item + step, self.n_items), "seq": self.z * 2 + self.core}
+        return {"items": self.item, "seq": lax.rem(self.z + step, self.n_z) * 2 + self.core}
 
     def steps_of(self, kind):
-        counts = {"core": 2, "items": self.n_items, "z": self.n_z, "plane": self.n_items * self.n_z}
-        return range(1, counts[kind])
+        return range(1, {"core": 2, "items": self.n_items, "z": self.n_z}[kind])
 
     def copies(self, part, phase, kind, source, target):
-        number = part * 6 + phase * 3 + {"core": 0, "items": 1, "z": 2, "plane": 1}[kind]
+        number = part * 6 + phase * 3 + {"core": 0, "items": 1, "z": 2}[kind]
         return number, [
             pltpu.make_async_remote_copy(
                 src_ref=source(step),
@@ -134,7 +118,7 @@
     def place(self, first, rows):
         half = rows // 2
         quarter = half // self.n_items
-        split = quarter % (16 * self.n_z) == 0
+        split = quarter % (16 * self.n_z) == 0 and rows > 2 * D
         last = quarter // self.n_z if split else quarter
         return half, quarter, split, last
 
@@ -165,17 +149,6 @@
             return self.copies(part, 0, "z", source, lambda s: self.z_in.at[s - 1, at])
         at = pl.ds(base, quarter)
         return self.copies(part, 0, "z", lambda s: self.z_out.at[at], lambda s: self.z_in.at[self.z, at])
-
-    def plane_copies(self, part, first, rows):
-        count = rows // 2 // (self.n_items * self.n_z)
-
-        def source(step):
-            item, z = self.spot("plane", step)
-            at = first // 2 + (item * self.n_z + z) * count
-            return self.i_out.at[pl.ds(pl.multiple_of(at, 16), count)]
-
-        at = pl.ds(first // 2 // (self.n_items * self.n_z), count)
-        return self.copies(part, 0, "plane", source, lambda s: self.d_in.at[s - 1, at])
 
     def held(self, first, rows, level):
         half, quarter, split, last = self.place(first, rows)
@@ -190,32 +163,11 @@
         return self.full.at[pl.ds(pl.multiple_of(at, 16), count)]
 
     def back_copies(self, part, first, rows, kind):
-        level = {"core": 0, "items": 1, "z": 2, "plane": 2}[kind]
+        level = {"core": 0, "items": 1, "z": 2}[kind]
         ref = self.held(first, rows, level)
         return self.copies(part, 1, kind, lambda s: ref, lambda s: ref)
 
-    def plane_step(self, part, first, rows, number):
-        count = rows // 2 // (self.n_items * self.n_z)
-        base = first // 2
-        if number == 2:
-            self.finish(self.plane_copies(part, first, rows), count)
-            own = base + (self.item * self.n_z + self.z) * count
-            value = self.i_out[pl.ds(pl.multiple_of(own, 16), count)].astype(f32)
-            at = pl.ds(base // (self.n_items * self.n_z), count)
-            for step in self.steps_of("plane"):
-                value += self.d_in[step - 1, at].astype(f32)
-            self.held(first, rows, 2)[...] = value.astype(bf16)
-            self.start(self.back_copies(part, first, rows, "plane"))
-        if number == 3:
-            self.finish(self.back_copies(part, first, rows, "plane"), count)
-            self.start(self.back_copies(part, first, rows, "core"))
-        if number == 4:
-            self.finish(self.back_copies(part, first, rows, "core"), rows // 2)
-
-    def step(self, part, first, rows, number, plane=False):
-        if plane and number > 1:
-            self.plane_step(part, first, rows, number)
-            return
+    def step(self, part, first, rows, number):
         half, quarter, split, last = self.place(first, rows)
         base_c = first // 2
         base_i = base_c // self.n_items
@@ -228,10 +180,7 @@
             here = pl.ds(base_c, half)
             own = pl.ds(pl.multiple_of(first + self.core * half, 16), half)
             self.i_out[here] = (self.partial[own] + self.c_in[here].astype(f32)).astype(bf16)
-            if plane:
-                self.start(self.plane_copies(part, first, rows))
-            else:
-                self.start(self.items_copies(part, first, rows))
+            self.start(self.items_copies(part, first, rows))
         if number == 2:
             self.finish(self.items_copies(part, first, rows), quarter)
             own = pl.ds(pl.multiple_of(base_c + self.item * quarter, 16), quarter)
@@ -314,12 +263,8 @@
     dbr,
     hid,
     dpre,
-    dmid,
-    datt,
-    dproj,
     ghalo,
     ghalo_in,
-    out,
     gvec,
     vec_buf,
     partial,
@@ -329,10 +274,7 @@
     i_in,
     z_out,
     z_in,
-    d_in,
-    full,
     load_sems,
-    store_sems,
     halo_sems,
     vec_sems,
     send_sems,
@@ -351,27 +293,29 @@
     seq = lax.axis_index("seq")
     MESH = pl.DeviceIdType.MESH
     sums = Sums(
-        mesh_sizes, (partial, c_out, c_in, i_out, i_in, z_out, z_in, d_in, full, send_sems, recv_sems)
+        mesh_sizes, (partial, c_out, c_in, i_out, i_in, z_out, z_in, grads_ref, send_sems, recv_sems)
     )
     wide = chunks // 2
     parts = [(k * wide * 2 * D, wide * 2 * D) for k in range(2)]
     parts += [((chunks + h) * 2 * D, 2 * D) for h in range(HEADS)]
-    direct = D % (16 * n_items * n_z) == 0
-    schedule = plan(direct)
+    schedule = plan()
 
     def hook(name):
         for part, number in schedule[name]:
             if part == "v":
                 vec_step(number)
             else:
-                sums.step(part, *parts[part], number, plane=direct and part >= 2)
+                sums.step(part, *parts[part], number)
 
     after = {"items": item, "seq": lax.rem(seq + 1, seq_size)}
     ahead = {"items": item, "seq": lax.rem(seq + seq_size - 1, seq_size)}
     barrier = pltpu.get_barrier_semaphore()
     greeted = [after, ahead]
-    for kind in ("core", "plane") if direct else ("core", "items", "z"):
+    for kind in ("core", "items", "z"):
         greeted += [sums.partner(kind, s) for s in sums.steps_of(kind)]
+    for device in greeted:
+        pl.semaphore_signal(barrier, inc=1, device_id=device, device_id_type=MESH)
+
     loads = [
         (wout_hbm, wout),
         (wup_hbm, wup),
@@ -402,8 +346,6 @@
     for copy in weight_loads:
         copy.start()
 
-    for device in greeted:
-        pl.semaphore_signal(barrier, inc=1, device_id=device, device_id_type=MESH)
 
     first_pos = seq * block
 
@@ -450,17 +392,20 @@
 
     for copy in qkv_loads:
         copy.wait()
-    for copy in token_loads:
-        copy.wait()
-    found = [first_norm(x[i, ROW:].astype(f32)) for i in range(items)]
-    results = [dot(low, wqkv[...]).astype(bf16) for low, _, _ in found]
-    for i in range(items):
-        low, normed, factor = found[i]
-        h1[i, ROW:] = low
-        n1[i, ROW:] = normed
-        r1[i, ROW:] = jnp.broadcast_to(factor, (block, 128))
-        proj[i, ROW:] = results[i]
-
+    def project(first, end):
+        for i in range(first, end):
+            token_loads[i].wait()
+        found = [first_norm(x[i, ROW:].astype(f32)) for i in range(first, end)]
+        results = [dot(low, wqkv[...]).astype(bf16) for low, _, _ in found]
+        for i in range(first, end):
+            low, normed, factor = found[i - first]
+            h1[i, ROW:] = low
+            n1[i, ROW:] = normed
+            r1[i, ROW:] = jnp.broadcast_to(factor, (block, 128))
+            proj[i, ROW:] = results[i - first]
+
+    early = items // 3
+    project(0, early)
     pl.semaphore_wait(barrier, len(greeted))
     halo_copy = pltpu.make_async_remote_copy(
         src_ref=tokens_ref.at[:, pl.ds(block - ROW, ROW)],
@@ -471,6 +416,7 @@
         device_id_type=MESH,
     )
     halo_copy.start()
+    project(early, items)
 
     query_pos = lax.broadcasted_iota(jnp.int32, (ROW, 2 * ROW), 0)
     key_pos = lax.broadcasted_iota(jnp.int32, (ROW, 2 * ROW), 1) - ROW
@@ -589,8 +535,8 @@
     out_grad = dot(att[...].reshape(total, D), lows, 0, 0)
     back = dot(lows, wout[...], 1, 1).astype(bf16)
     for i in range(items):
-        dmid[i] = found[i][0]
-        datt[i] = back[i * block : (i + 1) * block]
+        gtok_ref[i] = found[i][0]
+    h2[...] = back
     for h in range(HEADS):
         at = last + h * 2 * D + D
         partial[at : at + D, HEAD_DIM:] = out_grad[:, h * HEAD_DIM : (h + 1) * HEAD_DIM]
@@ -605,7 +551,7 @@
         for i in range(items):
             mine = proj[i, :, at : at + 3 * HEAD_DIM]
             es = [exps[i, r * HEADS + h, :, : 2 * ROW] for r in range(rows)]
-            scaled = datt[i, :, lanes].astype(f32) * inv[i, :, lanes]
+            scaled = h2[i * block : (i + 1) * block, lanes].astype(f32) * inv[i, :, lanes]
             product = scaled * att[i, :, lanes].astype(f32)
             low = scaled.astype(bf16)
             dqs, dks, dvs = [], [], []
@@ -634,15 +580,15 @@
 
             found.append((jnp.concatenate(dqs, 0), gather(dks), gather(dvs)))
         for i in range(items):
-            dproj[i, :ROW, at : at + HEAD_DIM] = jnp.zeros((ROW, HEAD_DIM), bf16)
-            dproj[i, ROW:, at : at + HEAD_DIM] = found[i][0]
-            dproj[i, :, at + HEAD_DIM : at + 2 * HEAD_DIM] = found[i][1]
-            dproj[i, :, at + 2 * HEAD_DIM : at + 3 * HEAD_DIM] = found[i][2]
+            proj[i, :ROW, at : at + HEAD_DIM] = jnp.zeros((ROW, HEAD_DIM), bf16)
+            proj[i, ROW:, at : at + HEAD_DIM] = found[i][0]
+            proj[i, :, at + HEAD_DIM : at + 2 * HEAD_DIM] = found[i][1]
+            proj[i, :, at + 2 * HEAD_DIM : at + 3 * HEAD_DIM] = found[i][2]
 
     def weight_back(h):
         left = h1[...].reshape(items * (block + ROW), D)
         at = h * 3 * HEAD_DIM
-        right = dproj[:, :, at : at + 3 * HEAD_DIM].reshape(items * (block + ROW), 3 * HEAD_DIM)
+        right = proj[:, :, at : at + 3 * HEAD_DIM].reshape(items * (block + ROW), 3 * HEAD_DIM)
         grad = dot(left, right, 0, 0)
         start = last + h * 2 * D
         partial[start : start + D] = grad[:, :D]
@@ -660,15 +606,15 @@
     def tokens_back(first, end):
         found = []
         for i in range(first, end):
-            grad = dot(dproj[i], wqkv[...], 1, 1)
+            grad = dot(proj[i], wqkv[...], 1, 1)
             normed = n1[i].astype(f32)
             factor = jnp.concatenate([r1[i]] * 2, 1)
             sums_here = fold_rows(grad * normed), fold_rows(grad)
             grad = norm_back(grad, normed, factor, gain_attn)
-            found.append((grad[:ROW].astype(bf16), dmid[i] + grad[ROW:], sums_here))
+            found.append((grad[:ROW].astype(bf16), gtok_ref[i] + grad[ROW:], sums_here))
         for i in range(first, end):
             ghalo[i] = found[i - first][0]
-            dmid[i] = found[i - first][1]
+            gtok_ref[i] = found[i - first][1]
         return sum(f[2][0] for f in found), sum(f[2][1] for f in found)
 
     half = items // 2
@@ -686,12 +632,6 @@
         device_id_type=MESH,
     )
     ghalo_copy.start()
-
-    own_copy = None
-    if rows > 1:
-        own = pl.ds(0, block - ROW)
-        own_copy = pltpu.make_async_copy(dmid.at[:, own], gtok_ref.at[:, own], store_sems.at[5])
-        own_copy.start()
 
     def vec_copies(kind, number):
         result = []
@@ -740,7 +680,7 @@
             start_all(vec_copies("z", 2))
         if number == 3:
             finish_all(vec_copies("z", 2))
-            gvec[0:8] = vec_total(2, n_z)
+            gvec_ref[...] = vec_total(2, n_z)
 
     def finish(first, end):
         branch = dot(hid[first * block : end * block], wdown[...])
@@ -750,41 +690,26 @@
             for i in range(first, end)
         ]
         for i in range(first, end):
-            out[i] = results[i - first].astype(bf16)
+            output_ref[i] = results[i - first].astype(bf16)
 
     hook("tokens1")
     finish(0, half)
     hook("finish0")
     finish(half, items)
-    out_copy = pltpu.make_async_copy(out, output_ref, store_sems.at[0])
-    out_copy.start()
     hook("finish1")
     ghalo_copy.wait()
     tail = block - ROW
     for i in range(items):
-        dmid[i, tail:] += ghalo_in[i].astype(f32)
-    tok_copy = pltpu.make_async_copy(dmid.at[:, pl.ds(tail, ROW)], gtok_ref.at[:, pl.ds(tail, ROW)], store_sems.at[1])
-    tok_copy.start()
+        gtok_ref[i, tail:] += ghalo_in[i].astype(f32)
     hook("tail")
-    vec_copy = pltpu.make_async_copy(gvec.at[pl.ds(0, 8)], gvec_ref, store_sems.at[2])
-    vec_copy.start()
-    early = pl.ds(0, last)
-    early_copy = pltpu.make_async_copy(full.at[early], grads_ref.at[early], store_sems.at[3])
-    early_copy.start()
     hook("last")
-    late = pl.ds(last, HEADS * 2 * D)
-    late_copy = pltpu.make_async_copy(full.at[late], grads_ref.at[late], store_sems.at[4])
-    late_copy.start()
-    for copy in (out_copy, own_copy, tok_copy, vec_copy, early_copy, late_copy):
-        if copy is not None:
-            copy.wait()
 
 
 def split_kernel(
     raw_out,
     raw_tok,
-    raw_grads,
-    raw_vec,
+    grads,
+    gvec,
     output,
     gtok,
     gqkv,
@@ -795,47 +720,29 @@
     shift_attn,
     gain_ffn,
     shift_ffn,
-    held_out,
-    held_tok,
-    grads,
-    gvec,
     qkv,
     wout,
     up,
     down,
-    load_sems,
     store_sems,
 ):
     chunks = up.shape[1] // D
-    items = raw_tok.shape[0]
     last = chunks * 2 * D
     stores = []
-
-    def load(source, target, number):
-        copy = pltpu.make_async_copy(source, target, load_sems.at[number])
-        copy.start()
-        return copy
 
     def store(source, target):
         copy = pltpu.make_async_copy(source, target, store_sems.at[len(stores)])
         copy.start()
         stores.append(copy)
 
-    early = load(raw_grads.at[pl.ds(0, last)], grads.at[pl.ds(0, last)], 0)
-    late_rows = pl.ds(last, HEADS * 2 * D)
-    late = load(raw_grads.at[late_rows], grads.at[late_rows], 1)
-    vec_load = load(raw_vec, gvec, 2)
-    half = items // 2
-    tok_loads = [load(raw_tok.at[pl.ds(k * half, half)], held_tok.at[pl.ds(k * half, half)], 3 + k) for k in range(2)]
-    out_load = load(raw_out, held_out, 5)
-    early.wait()
+    store(raw_tok, gtok)
+    store(raw_out, output)
     for c in range(chunks):
         down[c * D : (c + 1) * D] = grads[c * 2 * D : c * 2 * D + D].astype(f32)
     store(down, gdown)
     for c in range(chunks):
         up[:, c * D : (c + 1) * D] = grads[c * 2 * D + D : (c + 1) * 2 * D].astype(f32)
     store(up, gup)
-    late.wait()
     for h in range(HEADS):
         at = last + h * 2 * D
         lanes = slice(h * HEAD_DIM, (h + 1) * HEAD_DIM)
@@ -847,12 +754,6 @@
         wout[:, lanes] = second[:, HEAD_DIM:]
     store(qkv, gqkv)
     store(wout, gout)
-    for k in range(2):
-        tok_loads[k].wait()
-        store(held_tok.at[pl.ds(k * half, half)], gtok.at[pl.ds(k * half, half)])
-    out_load.wait()
-    store(held_out, output)
-    vec_load.wait()
     gain_attn[...] = gvec[0:1]
     shift_attn[...] = gvec[1:2]
     gain_ffn[...] = gvec[2:3]
@@ -886,16 +787,13 @@
     grad_rows = 2 * ff + 4 * width
     half = grad_rows // 2
     links = n_items + n_z - 1
-    plane = n_items * n_z
-    if width % (16 * plane) == 0:
-        links = plane
     vmem = pl.BlockSpec(memory_space=pltpu.VMEM)
     anywhere = pl.BlockSpec(memory_space=pl.ANY)
     raw = [
-        jax.ShapeDtypeStruct((items, block, width), bf16),
-        jax.ShapeDtypeStruct((items, block, width), f32),
-        jax.ShapeDtypeStruct((grad_rows, width), bf16),
-        jax.ShapeDtypeStruct((8, width), f32),
+        pltpu.VMEM((items, block, width), bf16),
+        pltpu.VMEM((items, block, width), f32),
+        pltpu.VMEM((grad_rows, width), bf16),
+        pltpu.VMEM((8, width), f32),
     ]
     vectors = [v.reshape(1, width) for v in (gain_attn, shift_attn, gain_ffn, shift_ffn)]
     parts = 2 + HEADS
@@ -904,7 +802,7 @@
         functools.partial(layer_kernel, items, rows, mesh_sizes, seq_size),
         out_shape=raw,
         in_specs=[pl.BlockSpec(memory_space=pltpu.SMEM), vmem] + [anywhere] * 6 + [vmem] * 4,
-        out_specs=[anywhere] * 4,
+        out_specs=[vmem] * 4,
         scratch_shapes=[
             vm((items, ext, width), bf16),
             vm((items, block, width), bf16),
@@ -928,12 +826,8 @@
             vm((total, width), bf16),
             vm((total, ff), bf16),
             vm((total, ff), bf16),
-            vm((items, block, width), f32),
-            vm((items, block, width), bf16),
-            vm((items, ext, 3 * width), bf16),
             vm((items, ROW, width), bf16),
             vm((items, ROW, width), bf16),
-            vm((items, block, width), bf16),
             vm((32, width), f32),
             vm((3, max(n_items, n_z), 8, width), f32),
             vm((grad_rows, width), f32),
@@ -943,17 +837,14 @@
             vm((n_items - 1, half // n_items, width), bf16),
             vm((half // n_items, width), bf16),
             vm((n_z, half // n_items, width), bf16),
-            vm((plane - 1, half // plane // 16 * 16 + 16, width), bf16),
-            vm((grad_rows, width), bf16),
             pltpu.SemaphoreType.DMA((4 + items + 3 * HEADS,)),
-            pltpu.SemaphoreType.DMA((6,)),
             pltpu.SemaphoreType.DMA((4,)),
             pltpu.SemaphoreType.DMA((2, links)),
             pltpu.SemaphoreType.DMA((6 * parts,)),
             pltpu.SemaphoreType.DMA((6 * parts,)),
         ],
         compiler_params=pltpu.CompilerParams(
-            vmem_limit_bytes=63 * 2**20, collective_id=0, has_side_effects=True
+            vmem_limit_bytes=52 * 2**20, collective_id=0, has_side_effects=True
         ),
     )(lengths, pad_mask, tokens, cotangent, w_qkv, w_out, w_up, w_down, *vectors)
     shapes = [
@@ -967,21 +858,16 @@
     outs = pl.pallas_call(
         split_kernel,
         out_shape=shapes,
-        in_specs=[anywhere] * 4,
+        in_specs=[vmem] * 4,
         out_specs=[anywhere] * 6 + [vmem] * 4,
         scratch_shapes=[
-            vm((items, block, width), bf16),
-            vm((items, block, width), f32),
-            vm((grad_rows, width), bf16),
-            vm((8, width), f32),
             vm((width, 3 * width), f32),
             vm((width, width), f32),
             vm((width, ff), f32),
             vm((ff, width), f32),
             pltpu.SemaphoreType.DMA((6,)),
-            pltpu.SemaphoreType.DMA((7,)),
         ],
-        compiler_params=pltpu.CompilerParams(vmem_limit_bytes=63 * 2**20),
+        compiler_params=pltpu.CompilerParams(vmem_limit_bytes=8 * 2**20),
     )(*raw)
     return tuple(outs[:6]) + tuple(v.reshape(width) for v in outs[6:])
 

time: 63 us -> 58.7 us (0.932)
  Pallas kernels: 62 us -> 57.7 us
    pallas_call x1, Pallas kernels: 57.2 us -> 54.3 us  [shards(): pl.pallas_call(functools.partial(layer_kernel, items, rows, mesh_sizes, s...]
    pallas_call x1, Pallas kernels: 4.77 us -> 3.39 us  [shards(): pl.pallas_call(split_kernel, out_shape=shapes, in_specs=[vmem] * 4, out_s...]
where the time goes in v5:
time: 58.7 us; the launch traced here: 58.5 us
  Pallas kernels  57.7 us (98%)
  between operations  0.84 us (1%)
    pallas_call x1, Pallas kernels, shards(): pl.pallas_call(functools.partial(layer_kernel, items, rows, mesh_sizes, s...  54.3 us
    pallas_call x1, Pallas kernels, shards(): pl.pallas_call(split_kernel, out_shape=shapes, in_specs=[vmem] * 4, out_s...  3.39 us

profile of v5, /device:TPU:0, one launch (start us, length us, event | category | flops | bytes accessed | tf_op | source)
XLA Modules:
  0.0 58.5 jit_solution(17420090525052874525)
XLA Ops:
  0.6 54.3 %shard_map.195 = (bf16[6,384,256]{2,1,0:T(8,128)(2,1)S(1)}, f32[6,384,256]{2,1,0:T(8,128)S(1)}, bf16[3072,256]{1,0:T(8,128)(2,1)S(1)}, f32[8,256]{1,0:T(8,128)S(1)}) custom-call(s32[6]{0:T(128)} %lengths_ref.1, s32[6,3072]{1,0:T(8,128)} %pad_ref.1, bf16[6,384,256]{2,1,0:T(8,128)(2,1)} %tokens_ref.1, bf16[6,384,256]{2,1,0:T(8,128)(2,1)} %cot_hbm.1, ...), custom_call_target="tpu_custom_call" | custom-call | tf_op jit(solution)/shard_map/pallas_call | solution.py:801
  54.9 3.4 %shard_map.196 = (bf16[6,384,256]{2,1,0:T(8,128)(2,1)}, f32[6,384,256]{2,1,0:T(8,128)}, f32[256,768]{1,0:T(8,128)}, f32[256,256]{1,0:T(8,128)}, f32[256,1024]{1,...) custom-call(bf16[6,384,256]{2,1,0:T(8,128)(2,1)S(1)} %get-tuple-elem, ...), custom_call_target="tpu_custom_call" | custom-call | tf_op jit(solution)/shard_map/pallas_call | solution.py:858

commit v6 on v5

--- a/solution.py
+++ b/solution.py
@@ -57,15 +57,18 @@
         "feed2": [(0, 1)],
         "feed3": [(1, 0)],
         "middle": [(1, 1)],
-        "back0": [(0, 2)],
-        "weight0": [(2, 0)],
-        "back1": [(2, 1), (1, 2)],
+        "back0": [],
+        "weight0": [(2, 0), (0, 2)],
+        "back1": [(2, 1), (1, 2), (0, 3)],
         "weight1": [(3, 0)],
-        "tokens0": [(0, 3)],
+        "tokens0": [],
         "tokens1": [(3, 1)],
-        "finish0": [("v", 1), (2, 2)],
-        "finish1": [(1, 3)],
-        "tail": [(0, 4), (3, 2), ("v", 2), (1, 4), (2, 3), (0, 5), (3, 3), (1, 5), (2, 5), (0, 6), (3, 5), (1, 6), ("v", 3)],
+        "finish0": [],
+        "finish1": [("v", 1), (0, 4), (2, 2), (1, 3)],
+        "tail": [
+            (3, 2), ("v", 2), (1, 4), (2, 3), (0, 5), (3, 3),
+            (1, 5), (2, 5), (0, 6), (3, 5), (1, 6), ("v", 3),
+        ],
         "last": [(2, 6), (3, 6)],
     }
     return plan
@@ -80,6 +83,7 @@
         seq = lax.axis_index("seq")
         self.core = lax.rem(seq, 2)
         self.z = seq // 2
+        self.sent = []
 
     def partner(self, kind, step):
         if kind == "core":
@@ -113,7 +117,12 @@
         number, each = copies
         size = self.full.at[pl.ds(0, len(each) * count)]
         pltpu.make_async_copy(size, size, self.recv.at[number]).wait()
-        pltpu.make_async_copy(size, size, self.send.at[number]).wait()
+        self.sent.append((number, len(each) * count))
+
+    def drain(self):
+        for number, count in self.sent:
+            size = self.full.at[pl.ds(0, count)]
+            pltpu.make_async_copy(size, size, self.send.at[number]).wait()
 
     def place(self, first, rows):
         half = rows // 2
@@ -415,7 +424,14 @@
         device_id=after,
         device_id_type=MESH,
     )
-    halo_copy.start()
+
+    @pl.when(seq < seq_size - 1)
+    def _():
+        halo_copy.start()
+
+    @pl.when(seq == 0)
+    def _():
+        x[:, :ROW] = jnp.zeros((items, ROW, D), bf16)
     project(early, items)
 
     query_pos = lax.broadcasted_iota(jnp.int32, (ROW, 2 * ROW), 0)
@@ -484,7 +500,15 @@
             dbr[flat] = grads[i]
 
     attend(1, rows)
-    halo_copy.wait()
+
+    @pl.when(seq < seq_size - 1)
+    def _():
+        halo_copy.wait_send()
+
+    @pl.when(seq > 0)
+    def _():
+        halo_copy.wait_recv()
+
     low, normed, factor = first_norm(x[:, :ROW].astype(f32).reshape(items * ROW, D))
     results = [
         dot(low, wqkv[:, (h * 3 + 1) * HEAD_DIM : (h * 3 + 3) * HEAD_DIM]).astype(bf16)
@@ -537,9 +561,7 @@
     for i in range(items):
         gtok_ref[i] = found[i][0]
     h2[...] = back
-    for h in range(HEADS):
-        at = last + h * 2 * D + D
-        partial[at : at + D, HEAD_DIM:] = out_grad[:, h * HEAD_DIM : (h + 1) * HEAD_DIM]
+    partial[last + D : last + 2 * D] = out_grad
     gvec[16:24] = sum(f[2][0] for f in found)
     gvec[24:32] = sum(f[2][1] for f in found)
     hook("middle")
@@ -585,44 +607,32 @@
             proj[i, :, at + HEAD_DIM : at + 2 * HEAD_DIM] = found[i][1]
             proj[i, :, at + 2 * HEAD_DIM : at + 3 * HEAD_DIM] = found[i][2]
 
-    def weight_back(h):
+    def weight_back(first, end, rows_at):
         left = h1[...].reshape(items * (block + ROW), D)
-        at = h * 3 * HEAD_DIM
-        right = proj[:, :, at : at + 3 * HEAD_DIM].reshape(items * (block + ROW), 3 * HEAD_DIM)
+        right = proj[:, :, first * D : end * D].reshape(items * (block + ROW), (end - first) * D)
         grad = dot(left, right, 0, 0)
-        start = last + h * 2 * D
-        partial[start : start + D] = grad[:, :D]
-        partial[start + D : start + 2 * D, :HEAD_DIM] = grad[:, D:]
+        for k in range(end - first):
+            at = last + (rows_at + k) * D
+            partial[at : at + D] = grad[:, k * D : (k + 1) * D]
 
     attend_back(0)
     hook("back0")
-    weight_back(0)
+    weight_back(0, 1, 0)
     hook("weight0")
     attend_back(1)
     hook("back1")
-    weight_back(1)
+    weight_back(1, 3, 2)
     hook("weight1")
 
-    def tokens_back(first, end):
-        found = []
-        for i in range(first, end):
-            grad = dot(proj[i], wqkv[...], 1, 1)
-            normed = n1[i].astype(f32)
-            factor = jnp.concatenate([r1[i]] * 2, 1)
-            sums_here = fold_rows(grad * normed), fold_rows(grad)
-            grad = norm_back(grad, normed, factor, gain_attn)
-            found.append((grad[:ROW].astype(bf16), gtok_ref[i] + grad[ROW:], sums_here))
-        for i in range(first, end):
-            ghalo[i] = found[i - first][0]
-            gtok_ref[i] = found[i - first][1]
-        return sum(f[2][0] for f in found), sum(f[2][1] for f in found)
-
-    half = items // 2
-    one = tokens_back(0, half)
-    hook("tokens0")
-    two = tokens_back(half, items)
-    gvec[0:8] = one[0] + two[0]
-    gvec[8:16] = one[1] + two[1]
+    grad = 0.0
+    for h in range(HEADS):
+        cols = slice((h * 3 + 1) * HEAD_DIM, (h * 3 + 3) * HEAD_DIM)
+        grad += dot(proj[:, :ROW, cols].reshape(items * ROW, 2 * HEAD_DIM), wqkv[:, cols], 1, 1)
+    normed = n1[:, :ROW].reshape(items * ROW, D).astype(f32)
+    factor = r1[:, :ROW].reshape(items * ROW, 128)
+    halo_sums = fold_rows(grad * normed), fold_rows(grad)
+    grad = norm_back(grad, normed, jnp.concatenate([factor, factor], 1), gain_attn)
+    ghalo[...] = grad.astype(bf16).reshape(items, ROW, D)
     ghalo_copy = pltpu.make_async_remote_copy(
         src_ref=ghalo,
         dst_ref=ghalo_in,
@@ -631,7 +641,29 @@
         device_id=ahead,
         device_id_type=MESH,
     )
-    ghalo_copy.start()
+
+    @pl.when(seq > 0)
+    def _():
+        ghalo_copy.start()
+
+    def tokens_back(first, end):
+        found = []
+        for i in range(first, end):
+            grad = dot(proj[i, ROW:], wqkv[...], 1, 1)
+            normed = n1[i, ROW:].astype(f32)
+            factor = jnp.concatenate([r1[i, ROW:]] * 2, 1)
+            sums_here = fold_rows(grad * normed), fold_rows(grad)
+            found.append((gtok_ref[i] + norm_back(grad, normed, factor, gain_attn), sums_here))
+        for i in range(first, end):
+            gtok_ref[i] = found[i - first][0]
+        return sum(f[1][0] for f in found), sum(f[1][1] for f in found)
+
+    half = items // 2
+    one = tokens_back(0, half)
+    hook("tokens0")
+    two = tokens_back(half, items)
+    gvec[0:8] = one[0] + two[0] + halo_sums[0]
+    gvec[8:16] = one[1] + two[1] + halo_sums[1]
 
     def vec_copies(kind, number):
         result = []
@@ -697,12 +729,20 @@
     hook("finish0")
     finish(half, items)
     hook("finish1")
-    ghalo_copy.wait()
-    tail = block - ROW
-    for i in range(items):
-        gtok_ref[i, tail:] += ghalo_in[i].astype(f32)
+
+    @pl.when(seq > 0)
+    def _():
+        ghalo_copy.wait_send()
+
+    @pl.when(seq < seq_size - 1)
+    def _():
+        ghalo_copy.wait_recv()
+        for i in range(items):
+            gtok_ref[i, block - ROW :] += ghalo_in[i].astype(f32)
+
     hook("tail")
     hook("last")
+    sums.drain()
 
 
 def split_kernel(
@@ -743,15 +783,13 @@
     for c in range(chunks):
         up[:, c * D : (c + 1) * D] = grads[c * 2 * D + D : (c + 1) * 2 * D].astype(f32)
     store(up, gup)
-    for h in range(HEADS):
-        at = last + h * 2 * D
-        lanes = slice(h * HEAD_DIM, (h + 1) * HEAD_DIM)
-        first = grads[at : at + D].astype(f32)
-        second = grads[at + D : at + 2 * D].astype(f32)
-        qkv[:, h * HEAD_DIM : (h + 1) * HEAD_DIM] = first[:, :HEAD_DIM]
-        qkv[:, D + h * HEAD_DIM : D + (h + 1) * HEAD_DIM] = first[:, HEAD_DIM:]
-        qkv[:, 2 * D + h * HEAD_DIM : 2 * D + (h + 1) * HEAD_DIM] = second[:, :HEAD_DIM]
-        wout[:, lanes] = second[:, HEAD_DIM:]
+    wout[...] = grads[last + D : last + 2 * D].astype(f32)
+    for k, rows_at in enumerate((0, 2, 3)):
+        value = grads[last + rows_at * D : last + (rows_at + 1) * D].astype(f32)
+        for half in range(2):
+            h, p = divmod(2 * k + half, 3)
+            at = p * D + h * HEAD_DIM
+            qkv[:, at : at + HEAD_DIM] = value[:, half * HEAD_DIM : (half + 1) * HEAD_DIM]
     store(qkv, gqkv)
     store(wout, gout)
     gain_attn[...] = gvec[0:1]

time: 58.7 us -> 56.9 us (0.969)
  Pallas kernels: 57.7 us -> 56 us
    pallas_call x1, Pallas kernels: 54.3 us -> 52.6 us  [shards(): pl.pallas_call(functools.partial(layer_kernel, items, rows, mesh_sizes, s...]
where the time goes in v6:
time: 56.9 us; the launch traced here: 56.8 us
  Pallas kernels  56 us (98%)
  between operations  0.82 us (1%)
    pallas_call x1, Pallas kernels, shards(): pl.pallas_call(functools.partial(layer_kernel, items, rows, mesh_sizes, s...  52.6 us
    pallas_call x1, Pallas kernels, shards(): pl.pallas_call(split_kernel, out_shape=shapes, in_specs=[vmem] * 4, out_s...  3.39 us

profile of v6, /device:TPU:0, one launch (start us, length us, event | category | flops | bytes accessed | tf_op | source)
XLA Modules:
  0.0 56.8 jit_solution(17842805118798074403)
XLA Ops:
  0.6 52.6 %shard_map.195 = (bf16[6,384,256]{2,1,0:T(8,128)(2,1)S(1)}, f32[6,384,256]{2,1,0:T(8,128)S(1)}, bf16[3072,256]{1,0:T(8,128)(2,1)S(1)}, f32[8,256]{1,0:T(8,128)S(1)}) custom-call(s32[6]{0:T(128)} %lengths_ref.1, s32[6,3072]{1,0:T(8,128)} %pad_ref.1, bf16[6,384,256]{2,1,0:T(8,128)(2,1)} %tokens_ref.1, bf16[6,384,256]{2,1,0:T(8,128)(2,1)} %cot_hbm.1, ...), custom_call_target="tpu_custom_call" | custom-call | tf_op jit(solution)/shard_map/pallas_call | solution.py:839
  53.2 3.4 %shard_map.196 = (bf16[6,384,256]{2,1,0:T(8,128)(2,1)}, f32[6,384,256]{2,1,0:T(8,128)}, f32[256,768]{1,0:T(8,128)}, f32[256,256]{1,0:T(8,128)}, f32[256,1024]{1,...) custom-call(bf16[6,384,256]{2,1,0:T(8,128)(2,1)S(1)} %get-tuple-elem, ...), custom_call_target="tpu_custom_call" | custom-call | tf_op jit(solution)/shard_map/pallas_call | solution.py:896
